TPU v7x, 128 devices: a whole 4x4x4 slice. The times are simulated.
128 devices in a mesh: grp: 4 (over y), dev: 32 (over z, x, core).
Axes of the slice: x: 4, y: 4, z: 4, core: 2. Of those that a mesh axis runs over, the one named last changes fastest.
Arguments:
- embeddings: bfloat16 [32768, 768], P(('grp', 'dev'))
- cluster_id: int32 [32768], P(('grp', 'dev')), may hold values from 0 to 31, as said below
Outputs:
- max_similarity: float32 [32768], P(('grp', 'dev'))
Inputs may be any that keep to these rules, and one draw needn't show every extreme that they name: `cluster_id`: cluster c is owned by group c mod the number of groups. In each aligned block of 256 rows (the rows of one device), at most 128 rows have clusters owned by one group, and exactly 128 rows for some group in every block.
All inputs are finite; a program needn't handle non-finite values.
Results may differ from a plain program's by a relative error of at most 0.0065.
Values may be sent and summed in bfloat16 or wider, within the bound.
No kernel may reach another device: no remote copies, remote signals or barrier semaphores. Data moves between devices by JAX's collectives and lax.ppermute only.
A program may use at most 64 MiB of HBM per device.

v0:
```python
import jax
import jax.numpy as jnp
from jax import lax
from jax.sharding import PartitionSpec as P


def pair_scores(queries, query_ids, key_rows, key_ids):
    scores = jnp.einsum("qd,kd->qk", queries, key_rows, preferred_element_type=jnp.float32)
    match = (query_ids[:, None] == key_ids[None, :]) & (key_ids[None, :] >= 0)
    return (scores, match)


def per_device(embeddings, cluster_id):
    row_count = embeddings.shape[0]
    groups = lax.axis_size("grp")
    slot = row_count // 2
    query_count = groups * slot
    values = embeddings.astype(jnp.float32)
    normed = (values / jnp.sqrt(jnp.sum(values * values, axis=1, keepdims=True) + 1e-06)).astype(
        jnp.bfloat16
    )
    owner_group = jnp.remainder(cluster_id, groups)
    group_hits = (owner_group[:, None] == jnp.arange(groups, dtype=jnp.int32)[None, :]).astype(
        jnp.int32
    )
    slot_rank = jnp.sum((jnp.cumsum(group_hits, axis=0) - 1) * group_hits, axis=1)
    dest_slot = owner_group * slot + slot_rank
    placed = jnp.arange(query_count, dtype=jnp.int32)[:, None] == dest_slot[None, :]
    send_rows = jnp.dot(
        placed.astype(jnp.bfloat16), normed, preferred_element_type=jnp.float32
    ).astype(jnp.bfloat16)
    send_ids = jnp.where(
        jnp.any(placed, axis=1), jnp.sum(jnp.where(placed, cluster_id[None, :], 0), axis=1), -1
    )
    received, received_ids = (
        lax.all_to_all(
            send_rows.reshape(groups, slot, -1), "grp", split_axis=0, concat_axis=0, tiled=True
        ),
        lax.all_to_all(
            send_ids.reshape(groups, slot), "grp", split_axis=0, concat_axis=0, tiled=True
        ),
    )
    queries = received.reshape(query_count, -1)
    query_ids = received_ids.reshape(query_count)
    own_start = lax.axis_index("dev") * query_count
    query_global = own_start + jnp.arange(query_count, dtype=jnp.int32)
    floor_row = jnp.full((query_count,), -1.0, jnp.float32)
    key_rows, key_ids = (
        lax.all_gather(queries, "dev", axis=0, tiled=True),
        lax.all_gather(query_ids, "dev", axis=0, tiled=True),
    )
    members = lax.axis_size("dev")
    factor = 4
    width = query_count * factor
    blocks = key_rows.shape[0] // width

    def one_block(best, index):
        rows = lax.dynamic_slice_in_dim(key_rows, index * width, width, 0)
        ids = lax.dynamic_slice_in_dim(key_ids, index * width, width, 0)
        columns = index * width + jnp.arange(width, dtype=jnp.int32)
        scores, match = pair_scores(queries, query_ids, rows, ids)
        match = match & (query_global[:, None] != columns[None, :])
        return (
            jnp.maximum(best, jnp.max(jnp.where(match, scores, jnp.float32(-1.0)), axis=1)),
            None,
        )

    best_score, unused = lax.scan(one_block, floor_row, jnp.arange(blocks, dtype=jnp.int32))
    returned = lax.all_to_all(
        best_score.reshape(groups, slot), "grp", split_axis=0, concat_axis=0, tiled=True
    )
    return jnp.sum(
        jnp.where(placed, returned.reshape(query_count)[:, None], jnp.float32(0.0)), axis=0
    )


def solution(mesh):
    in_specs = (P(("grp", "dev"), None), P(("grp", "dev")))
    out_specs = P(("grp", "dev"))
    return jax.shard_map(
        per_device, mesh=mesh, in_specs=in_specs, out_specs=out_specs, check_vma=False
    )
```

profile of v0, /device:TPU:1, one launch (start us, length us, event | category | flops | bytes accessed | tf_op | source)
XLA Modules:
  0.0 182.1 jit_solution(5479063498943542516)
XLA Ops:
  6.5 0.8 fusion.15
  7.3 0.7 and_select_fusion
  8.0 1.2 reduce-window.6
  9.6 0.7 multiply_add_fusion
  10.3 1.2 fusion.5
  11.5 1.5 convolution_convert_fusion
  12.9 16.3 %all_to_all.23 = bf16[4,128,768]{2,1,0:T(8,128)(2,1)} all-to-all(bf16[4,128,768]{2,1,0:T(8,128)(2,1)S(1)} %bitcast.42), channel_id=1, replica_groups=mesh['grp'=4,'dev'=32] {'grp'}, dimensions={0} | all-to-all | bytes 1572864 | tf_op jit(solution)/shard_map/all_to_all | solution.py:36
  29.3 0.2 fusion.7
  29.6 0.6 broadcast_select_fusion
  30.1 3.2 %all-to-all-start = ((s32[4,1,128]{2,1,0:T(1,128)}), s32[4,1,128]{2,1,0:T(1,128)S(1)}, u32[]{:S(2)}, u32[]{:S(2)}) async-start(s32[4,1,128]{2,1,0:T(1,128)} %bitcast.3), calls=%async_computation | async-start | bytes 4096 | tf_op jit(solution)/shard_map/all_to_all | solution.py:39
  33.4 4.1 %all-to-all-done = s32[4,1,128]{2,1,0:T(1,128)S(1)} async-done(((s32[4,1,128]{2,1,0:T(1,128)}), s32[4,1,128]{2,1,0:T(1,128)S(1)}, u32[]{:S(2)}, u32[]{:S(2)}) %all-to-all-start) | async-done | bytes 2080 | tf_op jit(solution)/shard_map/all_to_all | solution.py:39
  37.4 28.3 %all-gather = s32[32,1,512]{2,1,0:T(1,128)S(1)} all-gather(s32[1,1,512]{2,1,0:T(1,128)S(1)} %bitcast.45), channel_id=1, replica_groups=mesh['grp'=4,'dev'=32] {'dev'}, dimensions={0}, use_global_device_ids=true | all-gather | bytes 67584 | tf_op jit(solution)/shard_map/all_gather | solution.py:50
  65.7 57.9 %all-gather.3.cloned.1.call-done = bf16[16384,768]{1,0:T(8,128)(2,1)} async-done(((bf16[512,768]{1,0:T(8,128)(2,1)}), bf16[16384,768]{1,0:T(8,128)(2,1)}) %all-gather.3.cloned.1.call-update) | async-done | bytes 25165840 | tf_op jit(solution)/shard_map/all_gather | solution.py:49
  123.7 43.0 %while.11 = (s32[]{:T(128)}, f32[512]{0:T(512)S(1)}, s32[4,128]{1,0:T(4,128)S(1)}, s32[8]{0:T(128)S(1)}, s32[16384]{0:T(1024)S(1)}, /*index=5*/bf16[16384,768]{1...) while((s32[]{:T(128)}, f32[512]{0:T(512)S(1)}, ...), condition=%wide.region_8.9_spmd.clone, body=%wide.region_6.8_spmd.clone.sunk | while | flops 1616909312 | bytes 3991753 | solution.py:68
  123.7 0.6 dynamic_slice.21
  124.9 4.0 %fusion.21 = f32[512]{0:T(512)S(1)} fusion(bf16[512,768]{1,0:T(8,128)(2,1)} %get-tuple-element.179, bf16[16384,768]{1,0:T(8,128)(2,1)} %get-tuple-element.178, s32[]{:T(128)S(6)} %select_n.59, s32[512]{0:T(512)S(1)} %iota_add_fusion.4, s32[512]{0:T(512)S(1)} %bitcast.47, s32[2048]{0:T(1024)S(1)} %iota_add_fusion.5, s32[2048]{0:T(1024)S(1)} %get-tuple-element.147, ...), kind=kOutput, calls=%fused_computation.2.clone.1 | convolution fusion | flops 1616903680 | bytes 3956740 | tf_op jit(solution)/shard_map/while/body/eval_jaxpr/qd,kd->qk/dot_general | solution.py:8
  129.0 0.6 dynamic_slice.21
  130.3 4.0 %fusion.21 = f32[512]{0:T(512)S(1)} fusion(bf16[512,768]{1,0:T(8,128)(2,1)} %get-tuple-element.179, bf16[16384,768]{1,0:T(8,128)(2,1)} %get-tuple-element.178, s32[]{:T(128)S(6)} %select_n.59, s32[512]{0:T(512)S(1)} %iota_add_fusion.4, s32[512]{0:T(512)S(1)} %bitcast.47, s32[2048]{0:T(1024)S(1)} %iota_add_fusion.5, s32[2048]{0:T(1024)S(1)} %get-tuple-element.147, ...), kind=kOutput, calls=%fused_computation.2.clone.1 | convolution fusion | flops 1616903680 | bytes 3956740 | tf_op jit(solution)/shard_map/while/body/eval_jaxpr/qd,kd->qk/dot_general | solution.py:8
  134.4 0.6 dynamic_slice.21
  135.7 4.0 %fusion.21 = f32[512]{0:T(512)S(1)} fusion(bf16[512,768]{1,0:T(8,128)(2,1)} %get-tuple-element.179, bf16[16384,768]{1,0:T(8,128)(2,1)} %get-tuple-element.178, s32[]{:T(128)S(6)} %select_n.59, s32[512]{0:T(512)S(1)} %iota_add_fusion.4, s32[512]{0:T(512)S(1)} %bitcast.47, s32[2048]{0:T(1024)S(1)} %iota_add_fusion.5, s32[2048]{0:T(1024)S(1)} %get-tuple-element.147, ...), kind=kOutput, calls=%fused_computation.2.clone.1 | convolution fusion | flops 1616903680 | bytes 3956740 | tf_op jit(solution)/shard_map/while/body/eval_jaxpr/qd,kd->qk/dot_general | solution.py:8
  139.8 0.6 dynamic_slice.21
  141.1 4.0 %fusion.21 = f32[512]{0:T(512)S(1)} fusion(bf16[512,768]{1,0:T(8,128)(2,1)} %get-tuple-element.179, bf16[16384,768]{1,0:T(8,128)(2,1)} %get-tuple-element.178, s32[]{:T(128)S(6)} %select_n.59, s32[512]{0:T(512)S(1)} %iota_add_fusion.4, s32[512]{0:T(512)S(1)} %bitcast.47, s32[2048]{0:T(1024)S(1)} %iota_add_fusion.5, s32[2048]{0:T(1024)S(1)} %get-tuple-element.147, ...), kind=kOutput, calls=%fused_computation.2.clone.1 | convolution fusion | flops 1616903680 | bytes 3956740 | tf_op jit(solution)/shard_map/while/body/eval_jaxpr/qd,kd->qk/dot_general | solution.py:8
  145.1 0.6 dynamic_slice.21
  146.4 4.0 %fusion.21 = f32[512]{0:T(512)S(1)} fusion(bf16[512,768]{1,0:T(8,128)(2,1)} %get-tuple-element.179, bf16[16384,768]{1,0:T(8,128)(2,1)} %get-tuple-element.178, s32[]{:T(128)S(6)} %select_n.59, s32[512]{0:T(512)S(1)} %iota_add_fusion.4, s32[512]{0:T(512)S(1)} %bitcast.47, s32[2048]{0:T(1024)S(1)} %iota_add_fusion.5, s32[2048]{0:T(1024)S(1)} %get-tuple-element.147, ...), kind=kOutput, calls=%fused_computation.2.clone.1 | convolution fusion | flops 1616903680 | bytes 3956740 | tf_op jit(solution)/shard_map/while/body/eval_jaxpr/qd,kd->qk/dot_general | solution.py:8
  150.5 0.6 dynamic_slice.21
  151.8 4.0 %fusion.21 = f32[512]{0:T(512)S(1)} fusion(bf16[512,768]{1,0:T(8,128)(2,1)} %get-tuple-element.179, bf16[16384,768]{1,0:T(8,128)(2,1)} %get-tuple-element.178, s32[]{:T(128)S(6)} %select_n.59, s32[512]{0:T(512)S(1)} %iota_add_fusion.4, s32[512]{0:T(512)S(1)} %bitcast.47, s32[2048]{0:T(1024)S(1)} %iota_add_fusion.5, s32[2048]{0:T(1024)S(1)} %get-tuple-element.147, ...), kind=kOutput, calls=%fused_computation.2.clone.1 | convolution fusion | flops 1616903680 | bytes 3956740 | tf_op jit(solution)/shard_map/while/body/eval_jaxpr/qd,kd->qk/dot_general | solution.py:8
  155.9 0.6 dynamic_slice.21
  157.2 4.0 %fusion.21 = f32[512]{0:T(512)S(1)} fusion(bf16[512,768]{1,0:T(8,128)(2,1)} %get-tuple-element.179, bf16[16384,768]{1,0:T(8,128)(2,1)} %get-tuple-element.178, s32[]{:T(128)S(6)} %select_n.59, s32[512]{0:T(512)S(1)} %iota_add_fusion.4, s32[512]{0:T(512)S(1)} %bitcast.47, s32[2048]{0:T(1024)S(1)} %iota_add_fusion.5, s32[2048]{0:T(1024)S(1)} %get-tuple-element.147, ...), kind=kOutput, calls=%fused_computation.2.clone.1 | convolution fusion | flops 1616903680 | bytes 3956740 | tf_op jit(solution)/shard_map/while/body/eval_jaxpr/qd,kd->qk/dot_general | solution.py:8
  161.3 0.6 dynamic_slice.21
  162.5 4.0 %fusion.21 = f32[512]{0:T(512)S(1)} fusion(bf16[512,768]{1,0:T(8,128)(2,1)} %get-tuple-element.179, bf16[16384,768]{1,0:T(8,128)(2,1)} %get-tuple-element.178, s32[]{:T(128)S(6)} %select_n.59, s32[512]{0:T(512)S(1)} %iota_add_fusion.4, s32[512]{0:T(512)S(1)} %bitcast.47, s32[2048]{0:T(1024)S(1)} %iota_add_fusion.5, s32[2048]{0:T(1024)S(1)} %get-tuple-element.147, ...), kind=kOutput, calls=%fused_computation.2.clone.1 | convolution fusion | flops 1616903680 | bytes 3956740 | tf_op jit(solution)/shard_map/while/body/eval_jaxpr/qd,kd->qk/dot_general | solution.py:8
  166.6 7.9 %all_to_all.24 = f32[4,1,128]{2,1,0:T(1,128)S(1)} all-to-all(f32[4,1,128]{2,1,0:T(1,128)S(1)} %bitcast.44), channel_id=1, replica_groups=mesh['grp'=4,'dev'=32] {'grp'}, dimensions={0} | all-to-all | bytes 4096 | tf_op jit(solution)/shard_map/all_to_all | solution.py:69
  174.5 0.7 select_reduce_fusion
  (48 shorter events, 0.9 us)
Async XLA Ops:
  6.5 22.9 %copy-start = (s32[256]{0:T(256)S(1)}, s32[256]{0:T(256)}, u32[]{:S(2)}) copy-start(s32[256]{0:T(256)} %param.5) | copy-start | bytes 3076
  6.5 117.1 %all-gather.3.cloned.1.call-start = ((), (), s32[]{:S(2)}) async-start(), calls=%async_computation.3 | async-start | bytes 25952256 | tf_op jit(solution)/shard_map/all_gather | solution.py:49
  30.1 7.3 %all-to-all-start = ((s32[4,1,128]{2,1,0:T(1,128)}), s32[4,1,128]{2,1,0:T(1,128)S(1)}, u32[]{:S(2)}, u32[]{:S(2)}) async-start(s32[4,1,128]{2,1,0:T(1,128)} %bitcast.3), calls=%async_computation | async-start | bytes 4096 | tf_op jit(solution)/shard_map/all_to_all | solution.py:39
Sparse Core Ops, SparseCore 0:
  29.4 94.2 all-gather.2
where the time goes:
time: 183 us; the launch traced here: 182 us
  waiting for transfers between devices  62 us (34%)
  blocking collectives  52.5 us (29%)
  matrix products  33.8 us (18%)
  between operations  13.4 us (7%)
  other arithmetic  6.52 us (4%)
  loops' own time  5.36 us (3%)
  local copies, waits for them, and re-layouts  5.24 us (3%)
  starting transfers between devices  3.2 us (2%)
    all_gather x1, waiting for transfers between devices, per_device(): lax.all_gather(queries, 'dev', axis=0, tiled=True)  57.9 us
    dot_general x8, matrix products, pair_scores(): jnp.einsum('qd,kd->qk', queries, key_rows, preferred_element_type=jnp.flo...  32.4 us
    all_gather x1, blocking collectives, per_device(): lax.all_gather(query_ids, 'dev', axis=0, tiled=True)  28.3 us
    all_to_all x1, blocking collectives, per_device(): lax.all_to_all(send_rows.reshape(groups, slot, -1), 'grp', split_axis=0,...  16.3 us
    all_to_all x1, blocking collectives, per_device(): lax.all_to_all(best_score.reshape(groups, slot), 'grp', split_axis=0, con...  7.91 us
    another operation x1, loops' own time, per_device(): lax.scan(one_block, floor_row, jnp.arange(blocks, dtype=jnp.int32))  5.36 us
    dynamic_slice x8, local copies, waits for them, and re-layouts, per_device(): lax.scan(one_block, floor_row, jnp.arange(blocks, dtype=jnp.int32))  4.95 us
    all_to_all x1, waiting for transfers between devices, per_device(): lax.all_to_all(send_ids.reshape(groups, slot), 'grp', split_axis=0, conca...  4.05 us
  transfers between devices with their start and end apart: 2, of which 2 were waited for; matrix products, arithmetic and copies ran while one was open for 0% of the time, Pallas kernels for 0%

commit v1 on v0

v1 whole, which is shorter than its diff:
```python
import functools

import jax
import jax.numpy as jnp
from jax import lax
from jax.experimental import pallas as pl
from jax.experimental.pallas import tpu as pltpu
from jax.sharding import PartitionSpec as P

AXES = ("grp", "dev")
ROWS = 256
TAIL = 16
HALF = ROWS + TAIL
BLOCK = HALF + ROWS
SECOND = HALF
LANES = 128
FLOOR = -1.0


def pack_kernel(own_ref, other_ref, own_ids_ref, other_ids_ref, block_ref, half_ref):
    def unit(ref):
        values = ref[...].astype(jnp.float32)
        norm = jnp.sqrt(jnp.sum(values * values, axis=1, keepdims=True) + 1e-06)
        return (values / norm).astype(jnp.bfloat16)

    own = unit(own_ref)
    own_ids = jnp.broadcast_to(own_ids_ref[...].astype(jnp.float32), (TAIL, ROWS)).astype(jnp.bfloat16)
    other_ids = jnp.broadcast_to(other_ids_ref[...].astype(jnp.float32), (TAIL, ROWS)).astype(jnp.bfloat16)
    rest = jnp.zeros((TAIL, own.shape[1] - 2 * ROWS), jnp.bfloat16)
    for ref in (block_ref, half_ref):
        ref[0:ROWS, :] = own
        ref[ROWS:HALF, 0:ROWS] = own_ids
        ref[ROWS:HALF, ROWS : 2 * ROWS] = other_ids
        ref[ROWS:HALF, 2 * ROWS :] = rest
    block_ref[SECOND:BLOCK, :] = unit(other_ref)


def pack(own, other, own_ids, other_ids):
    width = own.shape[1]
    return pl.pallas_call(
        pack_kernel,
        out_shape=(
            jax.ShapeDtypeStruct((BLOCK, width), jnp.bfloat16),
            jax.ShapeDtypeStruct((HALF, width), jnp.bfloat16),
        ),
        compiler_params=pltpu.CompilerParams(vmem_limit_bytes=16 * 1024 * 1024),
        name="pack",
    )(own, other, own_ids.reshape(1, ROWS), other_ids.reshape(1, ROWS))


def parts_of(ref):
    return [(0, 0)] if ref.shape[0] == HALF else [(0, 0), (SECOND, ROWS)]


def ids_row(ref, lane):
    return ref[ROWS:HALF, lane : lane + ROWS].astype(jnp.float32)[0:1, :]


def score_kernel(n_queries, n_keys, first, last, *refs):
    queries, refs = refs[:n_queries], refs[n_queries:]
    keys, refs = refs[:n_keys], refs[n_keys:]
    query_parts = [(ref, row, lane) for ref in queries for row, lane in parts_of(ref)]
    if first:
        best_ref, column_ref = refs
        row_index = lax.broadcasted_iota(jnp.int32, (ROWS, ROWS), 0)
        col_index = lax.broadcasted_iota(jnp.int32, (ROWS, ROWS), 1)
        for place, (ref, row, lane) in enumerate(query_parts):
            ids = jnp.broadcast_to(ids_row(ref, lane), (ROWS, ROWS))
            column = jnp.sum(jnp.where(row_index == col_index, ids, 0.0), axis=1, keepdims=True)
            column_ref[place * ROWS : (place + 1) * ROWS, :] = jnp.broadcast_to(column, (ROWS, LANES))
    elif last:
        before_ref, column_ref, out_ref, best_ref = refs
    else:
        before_ref, column_ref, best_ref = refs

    for place, (ref, row, lane) in enumerate(query_parts):
        here = slice(place * ROWS, (place + 1) * ROWS)
        rows = ref[row : row + ROWS, :]
        column = column_ref[here, :]
        best = jnp.full((ROWS, LANES), FLOOR, jnp.float32) if first else before_ref[here, :]
        for number, key_ref in enumerate(keys):
            for key_row, key_lane in parts_of(key_ref):
                scores = lax.dot_general(
                    rows,
                    key_ref[key_row : key_row + ROWS, :],
                    (((1,), (1,)), ((), ())),
                    preferred_element_type=jnp.float32,
                )
                ids = ids_row(key_ref, key_lane)
                for start in range(0, ROWS, LANES):
                    match = column == ids[:, start : start + LANES]
                    if first and place == 0 and number == 0 and key_row == 0:
                        match = match & (
                            row_index[:, start : start + LANES] != col_index[:, start : start + LANES]
                        )
                    best = jnp.maximum(best, jnp.where(match, scores[:, start : start + LANES], FLOOR))
        if last:
            out_ref[0:1, here] = jnp.max(best.T, axis=0, keepdims=True)
        else:
            best_ref[here, :] = best


def score(queries, keys, state=None, last=False):
    count = sum(len(parts_of(q)) for q in queries) * ROWS
    wide = jax.ShapeDtypeStruct((count, LANES), jnp.float32)
    first = state is None
    shapes = (wide, wide) if first else wide
    scratch = []
    if last:
        shapes = jax.ShapeDtypeStruct((1, count), jnp.float32)
        scratch = [pltpu.VMEM((8, LANES), jnp.float32)]
    key_rows = sum(len(parts_of(k)) for k in keys) * ROWS
    width = keys[0].shape[1]
    result = pl.pallas_call(
        functools.partial(score_kernel, len(queries), len(keys), first, last),
        out_shape=shapes,
        scratch_shapes=scratch,
        compiler_params=pltpu.CompilerParams(vmem_limit_bytes=32 * 1024 * 1024),
        cost_estimate=pl.CostEstimate(
            flops=2 * count * key_rows * width,
            bytes_accessed=2 * width * (count + key_rows),
            transcendentals=0,
        ),
        name="score",
    )(*queries, *keys, *(() if first else state))
    if last:
        return result
    return result if first else (result, state[1])


def per_device(embeddings, cluster_id):
    ny, nz, nx = 4, 4, 4

    def place(y, z, x, core):
        return (((y % ny) * nz + z % nz) * nx + x % nx) * 2 + core

    def fetch(value, *offsets):
        pairs = []
        for y in range(ny):
            for z in range(nz):
                for x in range(nx):
                    for core, (dy, dz, dx) in enumerate(offsets):
                        pairs.append((place(y + dy, z + dz, x + dx, core), place(y, z, x, core)))
        return lax.ppermute(value, AXES, pairs)

    def give(value, *offsets):
        return fetch(value, *(tuple(-o for o in offset) for offset in offsets))

    def swap(value):
        return lax.ppermute(value, AXES, [(i, i ^ 1) for i in range(ny * nz * nx * 2)])

    block, half = pack(embeddings, swap(embeddings), cluster_id, swap(cluster_id))

    key1 = fetch(block, (0, 0, 1), (0, 1, 0))
    key2 = fetch(block, (0, 0, -1), (0, -1, 0))
    near = fetch(block, (1, 0, 0), (-1, 0, 0))
    key3 = fetch(block, (0, 0, 2), (0, 2, 0))
    far = fetch(half, (2, 0, 0), (2, 0, 0))
    key4 = fetch(key1, (0, 1, 0), (0, 0, -1))
    key5 = fetch(key2, (0, -1, 0), (0, 0, 1))
    key6 = fetch(key3, (0, 1, 0), (0, 0, 1))
    key7 = fetch(key3, (0, -1, 0), (0, 0, -1))
    key8 = fetch(key3[:HALF], (0, 2, 0), (0, 0, 2))

    queries = [half, far, near]
    state = score(queries, [block, key1, key2, swap(key1), swap(key2)])
    state = score(queries, [key3, swap(key3), key4, swap(key4), key5, swap(key5)], state)
    state = score(queries, [key6, swap(key6)], state)
    best = score(queries, [key7, swap(key7), key8, swap(key8)], state, last=True)[0]

    from_near = give(best[2 * ROWS :], (1, 0, 0), (-1, 0, 0))
    from_far = give(best[ROWS : 2 * ROWS], (2, 0, 0), (2, 0, 0))
    mine = jnp.maximum(best[:ROWS], jnp.maximum(from_far, from_near[:ROWS]))
    return jnp.maximum(mine, swap(from_near[ROWS:]))


def solution(mesh):
    in_specs = (P(AXES, None), P(AXES))
    return jax.shard_map(
        per_device, mesh=mesh, in_specs=in_specs, out_specs=P(AXES), check_vma=False
    )
```

time: 183 us -> 87 us (0.48)
  blocking collectives: 52.5 us -> 0 us
  matrix products: 33.8 us -> 0 us
  starting transfers between devices: 3.2 us -> 25.5 us
  waiting for transfers between devices: 62 us -> 44.3 us
  Pallas kernels: 0 us -> 14.4 us
  between operations: 13.4 us -> 0.1 us
  other arithmetic: 6.52 us -> 0.57 us
  loops' own time: 5.36 us -> 0 us
  local copies, waits for them, and re-layouts: 5.24 us -> 1.71 us
    all_gather x1 -> x0, waiting for transfers between devices: 57.9 us -> none  [per_device(): lax.all_gather(queries, 'dev', axis=0, tiled=True)]
    ppermute x0 -> x23, waiting for transfers between devices: none -> 44.3 us  [the longest x12 42.7 us: fetch(): return lax.ppermute(value, AXES, pairs)]
    dot_general x9 -> x0, matrix products: 33.8 us -> none  [the longest x8 32.4 us: pair_scores(): jnp.einsum('qd,kd->qk', queries, key_rows, preferred_element_type=jnp.flo...]
    all_gather x1 -> x0, blocking collectives: 28.3 us -> none  [per_device(): lax.all_gather(query_ids, 'dev', axis=0, tiled=True)]
    ppermute x0 -> x23, starting transfers between devices: none -> 25.5 us  [the longest x12 19.3 us: fetch(): return lax.ppermute(value, AXES, pairs)]
    all_to_all x2 -> x0, blocking collectives: 24.2 us -> none  [the longest x1 16.3 us: per_device(): lax.all_to_all(send_rows.reshape(groups, slot, -1), 'grp', split_axis=0,...]
    pallas_call x0 -> x5, Pallas kernels: none -> 14.4 us  [the longest x4 14.1 us: score(): pl.pallas_call(functools.partial(score_kernel, len(queries), len(keys), f...]
    another operation x1 -> x0, loops' own time: 5.36 us -> none  [per_device(): lax.scan(one_block, floor_row, jnp.arange(blocks, dtype=jnp.int32))]
  transfers between devices with their start and end apart: 2 -> 23, of which waited for: 2 -> 8; matrix products, arithmetic and copies ran while one was open for 0% -> 0% of each run, Pallas kernels for 0% -> 13%
where the time goes in v1:
time: 87 us; the launch traced here: 86.6 us
  waiting for transfers between devices  44.3 us (51%)
  starting transfers between devices  25.5 us (29%)
  Pallas kernels  14.4 us (17%)
  local copies, waits for them, and re-layouts  1.71 us (2%)
    ppermute x12, waiting for transfers between devices, fetch(): return lax.ppermute(value, AXES, pairs)  42.7 us
    ppermute x12, starting transfers between devices, fetch(): return lax.ppermute(value, AXES, pairs)  19.3 us
    pallas_call x4, Pallas kernels, score(): pl.pallas_call(functools.partial(score_kernel, len(queries), len(keys), f...  14.1 us
    ppermute x11, starting transfers between devices, swap(): lax.ppermute(value, AXES, [(i, i ^ 1) for i in range(ny * nz * nx * 2)])  6.19 us
  transfers between devices with their start and end apart: 23, of which 8 were waited for; matrix products, arithmetic and copies ran while one was open for 0% of the time, Pallas kernels for 13%

profile of v1, /device:TPU:1, one launch (start us, length us, event | category | flops | bytes accessed | tf_op | source)
XLA Modules:
  0.0 86.6 jit_solution(7028823087364370967)
XLA Ops:
  0.0 1.4 %collective-permute-start = (bf16[256,768]{1,0:T(8,128)(2,1)}, bf16[256,768]{1,0:T(8,128)(2,1)S(1)}, u32[]{:S(2)}, u32[]{:S(2)}) collective-permute-start(bf16[256,768]{1,0:T(8,128)(2,1)} %own_ref.1), channel_id=1, source_target_pairs={{0,1},{1,0},{2,3},{3,2},{4,5},{5,4},{6,7},{7,6},{8,9},{9,8},{10,11... | collective-permute-start | bytes 1179656 | tf_op jit(solution)/shard_map/ppermute | solution.py:150
  1.4 1.6 %collective-permute-done.1 = s32[256]{0:T(256)S(1)} collective-permute-done((s32[256]{0:T(256)}, s32[256]{0:T(256)S(1)}, u32[]{:S(2)}, u32[]{:S(2)}) %collective-permute-start.1) | collective-permute-done | bytes 1056 | tf_op jit(solution)/shard_map/ppermute | solution.py:150
  3.0 0.7 copy-done.1
  3.7 1.0 %copy-done = bf16[256,768]{1,0:T(8,128)(2,1)S(1)} copy-done((bf16[256,768]{1,0:T(8,128)(2,1)S(1)}, bf16[256,768]{1,0:T(8,128)(2,1)}, u32[]{:S(2)}) %copy-start) | copy-done | bytes 393240
  5.0 3.9 %collective-permute-start.12 = (bf16[528,768]{1,0:T(8,128)(2,1)S(1)}, bf16[528,768]{1,0:T(8,128)(2,1)S(1)}, u32[]{:S(2)}, u32[]{:S(2)}) collective-permute-start(bf16[528,768]{1,0:T(8,128)(2,1)S(1)} %get-tuple-element.10.refs_3_), channel_id=1, source_target_pairs={{2,0},{9,1},{4,2},{11,3},{6,4},{13,5},{0,6},{15,7},{10,8},{17,9},{... | collective-permute-start | bytes 2433032 | tf_op jit(solution)/shard_map/ppermute | solution.py:144
  8.9 1.3 %collective-permute-start.4 = (bf16[528,768]{1,0:T(8,128)(2,1)S(1)}, bf16[528,768]{1,0:T(8,128)(2,1)S(1)}, u32[]{:S(2)}, u32[]{:S(2)}) collective-permute-start(bf16[528,768]{1,0:T(8,128)(2,1)S(1)} %get-tuple-element.10.refs_3_), channel_id=1, source_target_pairs={{4,0},{17,1},{6,2},{19,3},{0,4},{21,5},{2,6},{23,7},{12,8},{25,9},... | collective-permute-start | bytes 2433032 | tf_op jit(solution)/shard_map/ppermute | solution.py:144
  10.2 1.3 %collective-permute-start.3 = (bf16[528,768]{1,0:T(8,128)(2,1)S(1)}, bf16[528,768]{1,0:T(8,128)(2,1)S(1)}, u32[]{:S(2)}, u32[]{:S(2)}) collective-permute-start(bf16[528,768]{1,0:T(8,128)(2,1)S(1)} %get-tuple-element.10.refs_3_), channel_id=1, source_target_pairs={{32,0},{97,1},{34,2},{99,3},{36,4},{101,5},{38,6},{103,7},{40,8},{... | collective-permute-start | bytes 2433032 | tf_op jit(solution)/shard_map/ppermute | solution.py:144
  11.5 2.6 %collective-permute-start.2 = (bf16[272,768]{1,0:T(8,128)(2,1)S(1)}, bf16[272,768]{1,0:T(8,128)(2,1)S(1)}, u32[]{:S(2)}, u32[]{:S(2)}) collective-permute-start(bf16[272,768]{1,0:T(8,128)(2,1)S(1)} %get-tuple-element.9.refs_0_), channel_id=1, source_target_pairs={{64,0},{65,1},{66,2},{67,3},{68,4},{69,5},{70,6},{71,7},{72,8},{73... | collective-permute-start | bytes 1253384 | tf_op jit(solution)/shard_map/ppermute | solution.py:144
  14.1 12.7 %collective-permute-done.12.refs_4_ = bf16[528,768]{1,0:T(8,128)(2,1)S(1)} collective-permute-done((bf16[528,768]{1,0:T(8,128)(2,1)S(1)}, bf16[528,768]{1,0:T(8,128)(2,1)S(1)}, u32[]{:S(2)}, u32[]{:S(2)}) %collective-permute-start.12) | collective-permute-done | bytes 811040 | tf_op jit(solution)/shard_map/ppermute | solution.py:144
  26.8 3.2 %collective-permute-done.15.refs_5_ = bf16[528,768]{1,0:T(8,128)(2,1)S(1)} collective-permute-done((bf16[528,768]{1,0:T(8,128)(2,1)S(1)}, bf16[528,768]{1,0:T(8,128)(2,1)S(1)}, u32[]{:S(2)}, u32[]{:S(2)}) %collective-permute-start.15) | collective-permute-done | bytes 811040 | tf_op jit(solution)/shard_map/ppermute | solution.py:144
  30.0 0.4 collective-permute-start.19
  30.4 2.3 %collective-permute-done.2.refs_1_ = bf16[272,768]{1,0:T(8,128)(2,1)S(1)} collective-permute-done((bf16[272,768]{1,0:T(8,128)(2,1)S(1)}, bf16[272,768]{1,0:T(8,128)(2,1)S(1)}, u32[]{:S(2)}, u32[]{:S(2)}) %collective-permute-start.2) | collective-permute-done | bytes 417824 | tf_op jit(solution)/shard_map/ppermute | solution.py:144
  32.7 1.2 %collective-permute-start.13 = (bf16[528,768]{1,0:T(8,128)(2,1)S(1)}, bf16[528,768]{1,0:T(8,128)(2,1)S(1)}, u32[]{:S(2)}, u32[]{:S(2)}) collective-permute-start(bf16[528,768]{1,0:T(8,128)(2,1)S(1)} %collective-permute-done.12.refs_4_), channel_id=1, source_target_pairs={{8,0},{7,1},{10,2},{1,3},{12,4},{3,5},{14,6},{5,7},{16,8},{15,9},{... | collective-permute-start | bytes 2433032 | tf_op jit(solution)/shard_map/ppermute | solution.py:144
  33.9 1.5 %collective-permute-start.16 = (bf16[528,768]{1,0:T(8,128)(2,1)S(1)}, bf16[528,768]{1,0:T(8,128)(2,1)S(1)}, u32[]{:S(2)}, u32[]{:S(2)}) collective-permute-start(bf16[528,768]{1,0:T(8,128)(2,1)S(1)} %collective-permute-done.15.refs_5_), channel_id=1, source_target_pairs={{24,0},{3,1},{26,2},{5,3},{28,4},{7,5},{30,6},{1,7},{0,8},{11,9},{... | collective-permute-start | bytes 2433032 | tf_op jit(solution)/shard_map/ppermute | solution.py:144
  35.4 1.6 %collective-permute-start.7 = (bf16[272,768]{1,0:T(8,128)(2,1)S(1)}, bf16[272,768]{1,0:T(8,128)(2,1)S(1)}, u32[]{:S(2)}, u32[]{:S(2)}) collective-permute-start(bf16[272,768]{1,0:T(8,128)(2,1)S(1)} %slice.36), channel_id=1, source_target_pairs={{16,0},{5,1},{18,2},{7,3},{20,4},{1,5},{22,6},{3,7},{24,8},{13,9},... | collective-permute-start | bytes 1253384 | tf_op jit(solution)/shard_map/ppermute | solution.py:144
  37.0 13.6 %collective-permute-done.7.refs_5_ = bf16[272,768]{1,0:T(8,128)(2,1)S(1)} collective-permute-done((bf16[272,768]{1,0:T(8,128)(2,1)S(1)}, bf16[272,768]{1,0:T(8,128)(2,1)S(1)}, u32[]{:S(2)}, u32[]{:S(2)}) %collective-permute-start.7) | collective-permute-done | bytes 417824 | tf_op jit(solution)/shard_map/ppermute | solution.py:144
  50.7 1.3 %collective-permute-start.9 = (bf16[528,768]{1,0:T(8,128)(2,1)S(1)}, bf16[528,768]{1,0:T(8,128)(2,1)S(1)}, u32[]{:S(2)}, u32[]{:S(2)}) collective-permute-start(bf16[528,768]{1,0:T(8,128)(2,1)S(1)} %collective-permute-done.4.refs_3_), channel_id=1, source_target_pairs={{8,0},{3,1},{10,2},{5,3},{12,4},{7,5},{14,6},{1,7},{16,8},{11,9},{... | collective-permute-start | bytes 2433032 | tf_op jit(solution)/shard_map/ppermute | solution.py:144
  52.2 1.0 %collective-permute-start.11 = (bf16[528,768]{1,0:T(8,128)(2,1)S(1)}, bf16[528,768]{1,0:T(8,128)(2,1)S(1)}, u32[]{:S(2)}, u32[]{:S(2)}) collective-permute-start(bf16[528,768]{1,0:T(8,128)(2,1)S(1)} %collective-permute-done.4.refs_3_), channel_id=1, source_target_pairs={{0,1},{1,0},{2,3},{3,2},{4,5},{5,4},{6,7},{7,6},{8,9},{9,8},{10,11... | collective-permute-start | bytes 2433032 | tf_op jit(solution)/shard_map/ppermute | solution.py:150
  53.3 0.4 collective-permute-start.17
  53.7 8.4 %collective-permute-done.9.refs_3_ = bf16[528,768]{1,0:T(8,128)(2,1)S(1)} collective-permute-done((bf16[528,768]{1,0:T(8,128)(2,1)S(1)}, bf16[528,768]{1,0:T(8,128)(2,1)S(1)}, u32[]{:S(2)}, u32[]{:S(2)}) %collective-permute-start.9) | collective-permute-done | bytes 811040 | tf_op jit(solution)/shard_map/ppermute | solution.py:144
  62.1 1.3 %collective-permute-start.10 = (bf16[528,768]{1,0:T(8,128)(2,1)S(1)}, bf16[528,768]{1,0:T(8,128)(2,1)S(1)}, u32[]{:S(2)}, u32[]{:S(2)}) collective-permute-start(bf16[528,768]{1,0:T(8,128)(2,1)S(1)} %collective-permute-done.9.refs_3_), channel_id=1, source_target_pairs={{0,1},{1,0},{2,3},{3,2},{4,5},{5,4},{6,7},{7,6},{8,9},{9,8},{10,11... | collective-permute-start | bytes 2433032 | tf_op jit(solution)/shard_map/ppermute | solution.py:150
  63.4 0.9 %collective-permute-done.5.refs_3_ = bf16[528,768]{1,0:T(8,128)(2,1)S(1)} collective-permute-done((bf16[528,768]{1,0:T(8,128)(2,1)S(1)}, bf16[528,768]{1,0:T(8,128)(2,1)S(1)}, u32[]{:S(2)}, u32[]{:S(2)}) %collective-permute-start.5) | collective-permute-done | bytes 811040 | tf_op jit(solution)/shard_map/ppermute | solution.py:144
  64.6 4.3 %score.4 = (f32[1024,128]{1,0:T(8,128)S(1)}, f32[1024,128]{1,0:T(8,128)S(1)}) custom-call(bf16[272,768]{1,0:T(8,128)(2,1)S(1)} %get-tuple-element.9.refs_0_, bf16[272,768]{1,0:T(8,128)(2,1)S(1)} %collective-permute-done.2.refs_1_, bf16[528,768]{1,0:T(8,128)(2,1)S(1)} %collective-permute-done.3.refs_2_, bf16[528,768]{1,0:T(8,128)(2,1)S(1)} %get-tuple-element.10.refs_3_, ...), custom_call_target="tpu_custom_call" | custom-call | flops 4026531840 | bytes 5505024 | tf_op jit(solution)/shard_map/score/pallas_call | solution.py:114
  69.0 0.5 collective-permute-start.8
  69.4 5.2 %score.5.refs_5_ = f32[1024,128]{1,0:T(8,128)S(1)} custom-call(bf16[272,768]{1,0:T(8,128)(2,1)S(1)} %get-tuple-element.9.refs_0_, bf16[272,768]{1,0:T(8,128)(2,1)S(1)} %collective-permute-done.2.refs_1_, bf16[528,768]{1,0:T(8,128)(2,1)S(1)} %collective-permute-done.3.refs_2_, bf16[528,768]{1,0:T(8,128)(2,1)S(1)} %collective-permute-done.4.refs_3_, ...), custom_call_target="tpu_custom_call" | custom-call | flops 4831838208 | bytes 6291456 | tf_op jit(solution)/shard_map/score/pallas_call | solution.py:114
  74.6 1.8 %score.6.refs_7_ = f32[1024,128]{1,0:T(8,128)S(1)} custom-call(bf16[272,768]{1,0:T(8,128)(2,1)S(1)} %get-tuple-element.9.refs_0_, bf16[272,768]{1,0:T(8,128)(2,1)S(1)} %collective-permute-done.2.refs_1_, bf16[528,768]{1,0:T(8,128)(2,1)S(1)} %collective-permute-done.3.refs_2_, bf16[528,768]{1,0:T(8,128)(2,1)S(1)} %collective-permute-done.9.refs_3_, ...), custom_call_target="tpu_custom_call" | custom-call | flops 1610612736 | bytes 3145728 | tf_op jit(solution)/shard_map/score/pallas_call | solution.py:114
  76.5 2.8 %score.7 = f32[1,1024]{1,0:T(1,128)S(1)} custom-call(bf16[272,768]{1,0:T(8,128)(2,1)S(1)} %get-tuple-element.9.refs_0_, bf16[272,768]{1,0:T(8,128)(2,1)S(1)} %collective-permute-done.2.refs_1_, bf16[528,768]{1,0:T(8,128)(2,1)S(1)} %collective-permute-done.3.refs_2_, bf16[528,768]{1,0:T(8,128)(2,1)S(1)} %collective-permute-done.5.refs_3_, ...), custom_call_target="tpu_custom_call" | custom-call | flops 2415919104 | bytes 3932160 | tf_op jit(solution)/shard_map/score/pallas_call | solution.py:114
  79.3 2.8 %collective-permute-start.21 = (f32[512]{0:T(512)S(1)}, f32[512]{0:T(512)S(1)}, u32[]{:S(2)}, u32[]{:S(2)}) collective-permute-start(f32[512]{0:T(512)S(1)} %bitcast.8), channel_id=1, source_target_pairs={{96,0},{33,1},{98,2},{35,3},{100,4},{37,5},{102,6},{39,7},{104,8},... | collective-permute-start | bytes 6152 | tf_op jit(solution)/shard_map/ppermute | solution.py:144
  82.1 1.6 %collective-permute-start.20 = (f32[256]{0:T(256)S(1)}, f32[256]{0:T(256)S(1)}, u32[]{:S(2)}, u32[]{:S(2)}) collective-permute-start(f32[256]{0:T(256)S(1)} %bitcast.9), channel_id=1, source_target_pairs={{64,0},{65,1},{66,2},{67,3},{68,4},{69,5},{70,6},{71,7},{72,8},{73... | collective-permute-start | bytes 3080 | tf_op jit(solution)/shard_map/ppermute | solution.py:144
  83.7 0.8 collective-permute-start.22
  84.4 1.6 %collective-permute-done.20 = f32[256]{0:T(256)S(1)} collective-permute-done((f32[256]{0:T(256)S(1)}, f32[256]{0:T(256)S(1)}, u32[]{:S(2)}, u32[]{:S(2)}) %collective-permute-start.20) | collective-permute-done | bytes 1056 | tf_op jit(solution)/shard_map/ppermute | solution.py:144
  86.0 0.6 maximum_maximum_fusion
  (28 shorter events, 0.9 us)
Async XLA Ops:
  0.0 3.0 %collective-permute-start = (bf16[256,768]{1,0:T(8,128)(2,1)}, bf16[256,768]{1,0:T(8,128)(2,1)S(1)}, u32[]{:S(2)}, u32[]{:S(2)}) collective-permute-start(bf16[256,768]{1,0:T(8,128)(2,1)} %own_ref.1), channel_id=1, source_target_pairs={{0,1},{1,0},{2,3},{3,2},{4,5},{5,4},{6,7},{7,6},{8,9},{9,8},{10,11... | collective-permute-start | bytes 1179656 | tf_op jit(solution)/shard_map/ppermute | solution.py:150
  1.4 1.6 %collective-permute-start.1 = (s32[256]{0:T(256)}, s32[256]{0:T(256)S(1)}, u32[]{:S(2)}, u32[]{:S(2)}) collective-permute-start(s32[256]{0:T(256)} %param.3), channel_id=1, source_target_pairs={{0,1},{1,0},{2,3},{3,2},{4,5},{5,4},{6,7},{7,6},{8,9},{9,8},{10,11... | collective-permute-start | bytes 3080 | tf_op jit(solution)/shard_map/ppermute | solution.py:150
  3.0 0.7 copy-start.1
  3.7 1.0 %copy-start = (bf16[256,768]{1,0:T(8,128)(2,1)S(1)}, bf16[256,768]{1,0:T(8,128)(2,1)}, u32[]{:S(2)}) copy-start(bf16[256,768]{1,0:T(8,128)(2,1)} %own_ref.1) | copy-start | bytes 1179652
  5.0 21.8 %collective-permute-start.12 = (bf16[528,768]{1,0:T(8,128)(2,1)S(1)}, bf16[528,768]{1,0:T(8,128)(2,1)S(1)}, u32[]{:S(2)}, u32[]{:S(2)}) collective-permute-start(bf16[528,768]{1,0:T(8,128)(2,1)S(1)} %get-tuple-element.10.refs_3_), channel_id=1, source_target_pairs={{2,0},{9,1},{4,2},{11,3},{6,4},{13,5},{0,6},{15,7},{10,8},{17,9},{... | collective-permute-start | bytes 2433032 | tf_op jit(solution)/shard_map/ppermute | solution.py:144
  8.9 21.1 %collective-permute-start.15 = (bf16[528,768]{1,0:T(8,128)(2,1)S(1)}, bf16[528,768]{1,0:T(8,128)(2,1)S(1)}, u32[]{:S(2)}, u32[]{:S(2)}) collective-permute-start(bf16[528,768]{1,0:T(8,128)(2,1)S(1)} %get-tuple-element.10.refs_3_), channel_id=1, source_target_pairs={{6,0},{25,1},{0,2},{27,3},{2,4},{29,5},{4,6},{31,7},{14,8},{1,9},{... | collective-permute-start | bytes 2433032 | tf_op jit(solution)/shard_map/ppermute | solution.py:144
  8.9 25.0 %collective-permute-start.4 = (bf16[528,768]{1,0:T(8,128)(2,1)S(1)}, bf16[528,768]{1,0:T(8,128)(2,1)S(1)}, u32[]{:S(2)}, u32[]{:S(2)}) collective-permute-start(bf16[528,768]{1,0:T(8,128)(2,1)S(1)} %get-tuple-element.10.refs_3_), channel_id=1, source_target_pairs={{4,0},{17,1},{6,2},{19,3},{0,4},{21,5},{2,6},{23,7},{12,8},{25,9},... | collective-permute-start | bytes 2433032 | tf_op jit(solution)/shard_map/ppermute | solution.py:144
  10.2 25.2 %collective-permute-start.3 = (bf16[528,768]{1,0:T(8,128)(2,1)S(1)}, bf16[528,768]{1,0:T(8,128)(2,1)S(1)}, u32[]{:S(2)}, u32[]{:S(2)}) collective-permute-start(bf16[528,768]{1,0:T(8,128)(2,1)S(1)} %get-tuple-element.10.refs_3_), channel_id=1, source_target_pairs={{32,0},{97,1},{34,2},{99,3},{36,4},{101,5},{38,6},{103,7},{40,8},{... | collective-permute-start | bytes 2433032 | tf_op jit(solution)/shard_map/ppermute | solution.py:144
  11.5 21.2 %collective-permute-start.2 = (bf16[272,768]{1,0:T(8,128)(2,1)S(1)}, bf16[272,768]{1,0:T(8,128)(2,1)S(1)}, u32[]{:S(2)}, u32[]{:S(2)}) collective-permute-start(bf16[272,768]{1,0:T(8,128)(2,1)S(1)} %get-tuple-element.9.refs_0_), channel_id=1, source_target_pairs={{64,0},{65,1},{66,2},{67,3},{68,4},{69,5},{70,6},{71,7},{72,8},{73... | collective-permute-start | bytes 1253384 | tf_op jit(solution)/shard_map/ppermute | solution.py:144
  26.8 25.2 %collective-permute-start.18 = (bf16[528,768]{1,0:T(8,128)(2,1)S(1)}, bf16[528,768]{1,0:T(8,128)(2,1)S(1)}, u32[]{:S(2)}, u32[]{:S(2)}) collective-permute-start(bf16[528,768]{1,0:T(8,128)(2,1)S(1)} %collective-permute-done.12.refs_4_), channel_id=1, source_target_pairs={{0,1},{1,0},{2,3},{3,2},{4,5},{5,4},{6,7},{7,6},{8,9},{9,8},{10,11... | collective-permute-start | bytes 2433032 | tf_op jit(solution)/shard_map/ppermute | solution.py:150
  30.0 22.1 %collective-permute-start.19 = (bf16[528,768]{1,0:T(8,128)(2,1)S(1)}, bf16[528,768]{1,0:T(8,128)(2,1)S(1)}, u32[]{:S(2)}, u32[]{:S(2)}) collective-permute-start(bf16[528,768]{1,0:T(8,128)(2,1)S(1)} %collective-permute-done.15.refs_5_), channel_id=1, source_target_pairs={{0,1},{1,0},{2,3},{3,2},{4,5},{5,4},{6,7},{7,6},{8,9},{9,8},{10,11... | collective-permute-start | bytes 2433032 | tf_op jit(solution)/shard_map/ppermute | solution.py:150
  32.7 20.5 %collective-permute-start.13 = (bf16[528,768]{1,0:T(8,128)(2,1)S(1)}, bf16[528,768]{1,0:T(8,128)(2,1)S(1)}, u32[]{:S(2)}, u32[]{:S(2)}) collective-permute-start(bf16[528,768]{1,0:T(8,128)(2,1)S(1)} %collective-permute-done.12.refs_4_), channel_id=1, source_target_pairs={{8,0},{7,1},{10,2},{1,3},{12,4},{3,5},{14,6},{5,7},{16,8},{15,9},{... | collective-permute-start | bytes 2433032 | tf_op jit(solution)/shard_map/ppermute | solution.py:144
  33.9 19.4 %collective-permute-start.16 = (bf16[528,768]{1,0:T(8,128)(2,1)S(1)}, bf16[528,768]{1,0:T(8,128)(2,1)S(1)}, u32[]{:S(2)}, u32[]{:S(2)}) collective-permute-start(bf16[528,768]{1,0:T(8,128)(2,1)S(1)} %collective-permute-done.15.refs_5_), channel_id=1, source_target_pairs={{24,0},{3,1},{26,2},{5,3},{28,4},{7,5},{30,6},{1,7},{0,8},{11,9},{... | collective-permute-start | bytes 2433032 | tf_op jit(solution)/shard_map/ppermute | solution.py:144
  35.4 15.3 %collective-permute-start.7 = (bf16[272,768]{1,0:T(8,128)(2,1)S(1)}, bf16[272,768]{1,0:T(8,128)(2,1)S(1)}, u32[]{:S(2)}, u32[]{:S(2)}) collective-permute-start(bf16[272,768]{1,0:T(8,128)(2,1)S(1)} %slice.36), channel_id=1, source_target_pairs={{16,0},{5,1},{18,2},{7,3},{20,4},{1,5},{22,6},{3,7},{24,8},{13,9},... | collective-permute-start | bytes 1253384 | tf_op jit(solution)/shard_map/ppermute | solution.py:144
  50.7 11.4 %collective-permute-start.9 = (bf16[528,768]{1,0:T(8,128)(2,1)S(1)}, bf16[528,768]{1,0:T(8,128)(2,1)S(1)}, u32[]{:S(2)}, u32[]{:S(2)}) collective-permute-start(bf16[528,768]{1,0:T(8,128)(2,1)S(1)} %collective-permute-done.4.refs_3_), channel_id=1, source_target_pairs={{8,0},{3,1},{10,2},{5,3},{12,4},{7,5},{14,6},{1,7},{16,8},{11,9},{... | collective-permute-start | bytes 2433032 | tf_op jit(solution)/shard_map/ppermute | solution.py:144
  52.0 12.3 %collective-permute-start.5 = (bf16[528,768]{1,0:T(8,128)(2,1)S(1)}, bf16[528,768]{1,0:T(8,128)(2,1)S(1)}, u32[]{:S(2)}, u32[]{:S(2)}) collective-permute-start(bf16[528,768]{1,0:T(8,128)(2,1)S(1)} %collective-permute-done.4.refs_3_), channel_id=1, source_target_pairs={{24,0},{7,1},{26,2},{1,3},{28,4},{3,5},{30,6},{5,7},{0,8},{15,9},{... | collective-permute-start | bytes 2433032 | tf_op jit(solution)/shard_map/ppermute | solution.py:144
  52.2 16.8 %collective-permute-start.11 = (bf16[528,768]{1,0:T(8,128)(2,1)S(1)}, bf16[528,768]{1,0:T(8,128)(2,1)S(1)}, u32[]{:S(2)}, u32[]{:S(2)}) collective-permute-start(bf16[528,768]{1,0:T(8,128)(2,1)S(1)} %collective-permute-done.4.refs_3_), channel_id=1, source_target_pairs={{0,1},{1,0},{2,3},{3,2},{4,5},{5,4},{6,7},{7,6},{8,9},{9,8},{10,11... | collective-permute-start | bytes 2433032 | tf_op jit(solution)/shard_map/ppermute | solution.py:150
  53.2 16.2 %collective-permute-start.14 = (bf16[528,768]{1,0:T(8,128)(2,1)S(1)}, bf16[528,768]{1,0:T(8,128)(2,1)S(1)}, u32[]{:S(2)}, u32[]{:S(2)}) collective-permute-start(bf16[528,768]{1,0:T(8,128)(2,1)S(1)} %collective-permute-done.13.refs_5_), channel_id=1, source_target_pairs={{0,1},{1,0},{2,3},{3,2},{4,5},{5,4},{6,7},{7,6},{8,9},{9,8},{10,11... | collective-permute-start | bytes 2433032 | tf_op jit(solution)/shard_map/ppermute | solution.py:150
  53.3 16.2 %collective-permute-start.17 = (bf16[528,768]{1,0:T(8,128)(2,1)S(1)}, bf16[528,768]{1,0:T(8,128)(2,1)S(1)}, u32[]{:S(2)}, u32[]{:S(2)}) collective-permute-start(bf16[528,768]{1,0:T(8,128)(2,1)S(1)} %collective-permute-done.16.refs_7_), channel_id=1, source_target_pairs={{0,1},{1,0},{2,3},{3,2},{4,5},{5,4},{6,7},{7,6},{8,9},{9,8},{10,11... | collective-permute-start | bytes 2433032 | tf_op jit(solution)/shard_map/ppermute | solution.py:150
  62.1 12.5 %collective-permute-start.10 = (bf16[528,768]{1,0:T(8,128)(2,1)S(1)}, bf16[528,768]{1,0:T(8,128)(2,1)S(1)}, u32[]{:S(2)}, u32[]{:S(2)}) collective-permute-start(bf16[528,768]{1,0:T(8,128)(2,1)S(1)} %collective-permute-done.9.refs_3_), channel_id=1, source_target_pairs={{0,1},{1,0},{2,3},{3,2},{4,5},{5,4},{6,7},{7,6},{8,9},{9,8},{10,11... | collective-permute-start | bytes 2433032 | tf_op jit(solution)/shard_map/ppermute | solution.py:150
  64.3 12.1 %collective-permute-start.6 = (bf16[528,768]{1,0:T(8,128)(2,1)S(1)}, bf16[528,768]{1,0:T(8,128)(2,1)S(1)}, u32[]{:S(2)}, u32[]{:S(2)}) collective-permute-start(bf16[528,768]{1,0:T(8,128)(2,1)S(1)} %collective-permute-done.5.refs_3_), channel_id=1, source_target_pairs={{0,1},{1,0},{2,3},{3,2},{4,5},{5,4},{6,7},{7,6},{8,9},{9,8},{10,11... | collective-permute-start | bytes 2433032 | tf_op jit(solution)/shard_map/ppermute | solution.py:150
  69.0 7.5 %collective-permute-start.8 = (bf16[272,768]{1,0:T(8,128)(2,1)S(1)}, bf16[272,768]{1,0:T(8,128)(2,1)S(1)}, u32[]{:S(2)}, u32[]{:S(2)}) collective-permute-start(bf16[272,768]{1,0:T(8,128)(2,1)S(1)} %collective-permute-done.7.refs_5_), channel_id=1, source_target_pairs={{0,1},{1,0},{2,3},{3,2},{4,5},{5,4},{6,7},{7,6},{8,9},{9,8},{10,11... | collective-permute-start | bytes 1253384 | tf_op jit(solution)/shard_map/ppermute | solution.py:150
  79.3 4.4 %collective-permute-start.21 = (f32[512]{0:T(512)S(1)}, f32[512]{0:T(512)S(1)}, u32[]{:S(2)}, u32[]{:S(2)}) collective-permute-start(f32[512]{0:T(512)S(1)} %bitcast.8), channel_id=1, source_target_pairs={{96,0},{33,1},{98,2},{35,3},{100,4},{37,5},{102,6},{39,7},{104,8},... | collective-permute-start | bytes 6152 | tf_op jit(solution)/shard_map/ppermute | solution.py:144
  82.1 3.9 %collective-permute-start.20 = (f32[256]{0:T(256)S(1)}, f32[256]{0:T(256)S(1)}, u32[]{:S(2)}, u32[]{:S(2)}) collective-permute-start(f32[256]{0:T(256)S(1)} %bitcast.9), channel_id=1, source_target_pairs={{64,0},{65,1},{66,2},{67,3},{68,4},{69,5},{70,6},{71,7},{72,8},{73... | collective-permute-start | bytes 3080 | tf_op jit(solution)/shard_map/ppermute | solution.py:144
  83.7 2.4 %collective-permute-start.22 = (f32[256]{0:T(256)S(1)}, f32[256]{0:T(256)S(1)}, u32[]{:S(2)}, u32[]{:S(2)}) collective-permute-start(f32[256]{0:T(256)S(1)} %slice.35), channel_id=1, source_target_pairs={{0,1},{1,0},{2,3},{3,2},{4,5},{5,4},{6,7},{7,6},{8,9},{9,8},{10,11... | collective-permute-start | bytes 3080 | tf_op jit(solution)/shard_map/ppermute | solution.py:150

commit v2 on v1

--- a/solution.py
+++ b/solution.py
@@ -48,18 +48,21 @@
     )(own, other, own_ids.reshape(1, ROWS), other_ids.reshape(1, ROWS))
 
 
-def parts_of(ref):
-    return [(0, 0)] if ref.shape[0] == HALF else [(0, 0), (SECOND, ROWS)]
+OWN, OTHER = (0, 0), (SECOND, ROWS)
+
+
+def whole(block):
+    return (block, (OWN,) if block.shape[0] == HALF else (OWN, OTHER))
 
 
 def ids_row(ref, lane):
     return ref[ROWS:HALF, lane : lane + ROWS].astype(jnp.float32)[0:1, :]
 
 
-def score_kernel(n_queries, n_keys, first, last, *refs):
-    queries, refs = refs[:n_queries], refs[n_queries:]
-    keys, refs = refs[:n_keys], refs[n_keys:]
-    query_parts = [(ref, row, lane) for ref in queries for row, lane in parts_of(ref)]
+def score_kernel(query_parts, key_parts, n_blocks, first, last, *refs):
+    blocks, refs = refs[:n_blocks], refs[n_blocks:]
+    query_parts = [(blocks[at], row, lane) for at, (row, lane) in query_parts]
+    key_parts = [(blocks[at], row, lane) for at, (row, lane) in key_parts]
     if first:
         best_ref, column_ref = refs
         row_index = lax.broadcasted_iota(jnp.int32, (ROWS, ROWS), 0)
@@ -69,7 +72,7 @@
             column = jnp.sum(jnp.where(row_index == col_index, ids, 0.0), axis=1, keepdims=True)
             column_ref[place * ROWS : (place + 1) * ROWS, :] = jnp.broadcast_to(column, (ROWS, LANES))
     elif last:
-        before_ref, column_ref, out_ref, best_ref = refs
+        before_ref, column_ref, out_ref = refs
     else:
         before_ref, column_ref, best_ref = refs
 
@@ -78,22 +81,21 @@
         rows = ref[row : row + ROWS, :]
         column = column_ref[here, :]
         best = jnp.full((ROWS, LANES), FLOOR, jnp.float32) if first else before_ref[here, :]
-        for number, key_ref in enumerate(keys):
-            for key_row, key_lane in parts_of(key_ref):
-                scores = lax.dot_general(
-                    rows,
-                    key_ref[key_row : key_row + ROWS, :],
-                    (((1,), (1,)), ((), ())),
-                    preferred_element_type=jnp.float32,
-                )
-                ids = ids_row(key_ref, key_lane)
-                for start in range(0, ROWS, LANES):
-                    match = column == ids[:, start : start + LANES]
-                    if first and place == 0 and number == 0 and key_row == 0:
-                        match = match & (
-                            row_index[:, start : start + LANES] != col_index[:, start : start + LANES]
-                        )
-                    best = jnp.maximum(best, jnp.where(match, scores[:, start : start + LANES], FLOOR))
+        for number, (key_ref, key_row, key_lane) in enumerate(key_parts):
+            scores = lax.dot_general(
+                rows,
+                key_ref[key_row : key_row + ROWS, :],
+                (((1,), (1,)), ((), ())),
+                preferred_element_type=jnp.float32,
+            )
+            ids = ids_row(key_ref, key_lane)
+            for start in range(0, ROWS, LANES):
+                match = column == ids[:, start : start + LANES]
+                if first and place == 0 and number == 0:
+                    match = match & (
+                        row_index[:, start : start + LANES] != col_index[:, start : start + LANES]
+                    )
+                best = jnp.maximum(best, jnp.where(match, scores[:, start : start + LANES], FLOOR))
         if last:
             out_ref[0:1, here] = jnp.max(best.T, axis=0, keepdims=True)
         else:
@@ -101,20 +103,27 @@
 
 
 def score(queries, keys, state=None, last=False):
-    count = sum(len(parts_of(q)) for q in queries) * ROWS
+    blocks = []
+
+    def listed(pieces):
+        found = []
+        for block, parts in pieces:
+            at = next((i for i, b in enumerate(blocks) if b is block), len(blocks))
+            if at == len(blocks):
+                blocks.append(block)
+            found += [(at, part) for part in parts]
+        return found
+
+    query_parts, key_parts = listed(queries), listed(keys)
+    count, key_rows, width = len(query_parts) * ROWS, len(key_parts) * ROWS, blocks[0].shape[1]
     wide = jax.ShapeDtypeStruct((count, LANES), jnp.float32)
     first = state is None
     shapes = (wide, wide) if first else wide
-    scratch = []
     if last:
         shapes = jax.ShapeDtypeStruct((1, count), jnp.float32)
-        scratch = [pltpu.VMEM((8, LANES), jnp.float32)]
-    key_rows = sum(len(parts_of(k)) for k in keys) * ROWS
-    width = keys[0].shape[1]
     result = pl.pallas_call(
-        functools.partial(score_kernel, len(queries), len(keys), first, last),
+        functools.partial(score_kernel, query_parts, key_parts, len(blocks), first, last),
         out_shape=shapes,
-        scratch_shapes=scratch,
         compiler_params=pltpu.CompilerParams(vmem_limit_bytes=32 * 1024 * 1024),
         cost_estimate=pl.CostEstimate(
             flops=2 * count * key_rows * width,
@@ -122,7 +131,7 @@
             transcendentals=0,
         ),
         name="score",
-    )(*queries, *keys, *(() if first else state))
+    )(*blocks, *(() if first else state))
     if last:
         return result
     return result if first else (result, state[1])
@@ -154,22 +163,24 @@
     key1 = fetch(block, (0, 0, 1), (0, 1, 0))
     key2 = fetch(block, (0, 0, -1), (0, -1, 0))
     near = fetch(block, (1, 0, 0), (-1, 0, 0))
-    key3 = fetch(block, (0, 0, 2), (0, 2, 0))
     far = fetch(half, (2, 0, 0), (2, 0, 0))
     key4 = fetch(key1, (0, 1, 0), (0, 0, -1))
     key5 = fetch(key2, (0, -1, 0), (0, 0, 1))
-    key6 = fetch(key3, (0, 1, 0), (0, 0, 1))
-    key7 = fetch(key3, (0, -1, 0), (0, 0, -1))
-    key8 = fetch(key3[:HALF], (0, 2, 0), (0, 0, 2))
+    key3 = fetch(key1, (0, 0, 1), (0, 1, 0))
+    key6 = fetch(key4, (0, 1, 0), (0, 0, -1))
+    key7 = fetch(key5, (0, -1, 0), (0, 0, 1))
+    key8 = fetch(key7[:HALF], (0, 0, -1), (0, -1, 0))
 
-    queries = [half, far, near]
-    state = score(queries, [block, key1, key2, swap(key1), swap(key2)])
-    state = score(queries, [key3, swap(key3), key4, swap(key4), key5, swap(key5)], state)
-    state = score(queries, [key6, swap(key6)], state)
-    best = score(queries, [key7, swap(key7), key8, swap(key8)], state, last=True)[0]
+    queries = [(block, (OWN,)), whole(far), whole(near), (block, (OTHER,)), whole(swap(far)), whole(swap(near))]
+    state = score(queries, [(block, (OWN,)), whole(key1), whole(key2)])
+    state = score(queries, [whole(key4), whole(key5)], state)
+    state = score(queries, [whole(key3)], state)
+    state = score(queries, [whole(key6), whole(key7)], state)
+    best = score(queries, [whole(key8)], state, last=True)[0]
+    best = jnp.maximum(best[: 4 * ROWS], swap(best[4 * ROWS :]))
 
+    from_far = give(best[ROWS : 2 * ROWS], (2, 0, 0), (2, 0, 0))
     from_near = give(best[2 * ROWS :], (1, 0, 0), (-1, 0, 0))
-    from_far = give(best[ROWS : 2 * ROWS], (2, 0, 0), (2, 0, 0))
     mine = jnp.maximum(best[:ROWS], jnp.maximum(from_far, from_near[:ROWS]))
     return jnp.maximum(mine, swap(from_near[ROWS:]))
 

time: 87 us -> 72.7 us (0.84)
  waiting for transfers between devices: 44.3 us -> 32.7 us
  starting transfers between devices: 25.5 us -> 22.7 us
    ppermute x12, waiting for transfers between devices: 42.7 us -> 30 us  [fetch(): return lax.ppermute(value, AXES, pairs)]
    ppermute x12, starting transfers between devices: 19.3 us -> 17.3 us  [fetch(): return lax.ppermute(value, AXES, pairs)]
    ppermute x11 -> x6, waiting for transfers between devices: 1.58 us -> 2.72 us  [swap(): lax.ppermute(value, AXES, [(i, i ^ 1) for i in range(ny * nz * nx * 2)])]
    ppermute x11 -> x6, starting transfers between devices: 6.19 us -> 5.42 us  [swap(): lax.ppermute(value, AXES, [(i, i ^ 1) for i in range(ny * nz * nx * 2)])]
    pallas_call x4 -> x5, Pallas kernels: 14.1 us -> 14.5 us  [score(): pl.pallas_call(functools.partial(score_kernel, query_parts, key_parts, le...]
  transfers between devices with their start and end apart: 23 -> 18, of which waited for: 8 -> 8; matrix products, arithmetic and copies ran while one was open for 0% -> 0% of each run, Pallas kernels for 13% -> 18%
where the time goes in v2:
time: 72.7 us; the launch traced here: 72.6 us
  waiting for transfers between devices  32.7 us (45%)
  starting transfers between devices  22.7 us (31%)
  Pallas kernels  14.8 us (20%)
  local copies, waits for them, and re-layouts  1.72 us (2%)
    ppermute x12, waiting for transfers between devices, fetch(): return lax.ppermute(value, AXES, pairs)  30 us
    ppermute x12, starting transfers between devices, fetch(): return lax.ppermute(value, AXES, pairs)  17.3 us
    pallas_call x5, Pallas kernels, score(): pl.pallas_call(functools.partial(score_kernel, query_parts, key_parts, le...  14.5 us
    ppermute x6, starting transfers between devices, swap(): lax.ppermute(value, AXES, [(i, i ^ 1) for i in range(ny * nz * nx * 2)])  5.42 us
    ppermute x6, waiting for transfers between devices, swap(): lax.ppermute(value, AXES, [(i, i ^ 1) for i in range(ny * nz * nx * 2)])  2.72 us
    unnamed x4, local copies, waits for them, and re-layouts  1.67 us
  transfers between devices with their start and end apart: 18, of which 8 were waited for; matrix products, arithmetic and copies ran while one was open for 0% of the time, Pallas kernels for 18%

profile of v2, /device:TPU:1, one launch (start us, length us, event | category | flops | bytes accessed | tf_op | source)
XLA Modules:
  0.0 72.6 jit_solution(9697554921730085341)
XLA Ops:
  0.0 1.4 %collective-permute-start = (bf16[256,768]{1,0:T(8,128)(2,1)}, bf16[256,768]{1,0:T(8,128)(2,1)S(1)}, u32[]{:S(2)}, u32[]{:S(2)}) collective-permute-start(bf16[256,768]{1,0:T(8,128)(2,1)} %own_ref.1), channel_id=1, source_target_pairs={{0,1},{1,0},{2,3},{3,2},{4,5},{5,4},{6,7},{7,6},{8,9},{9,8},{10,11... | collective-permute-start | bytes 1179656 | tf_op jit(solution)/shard_map/ppermute | solution.py:159
  1.4 1.6 %collective-permute-done.1 = s32[256]{0:T(256)S(1)} collective-permute-done((s32[256]{0:T(256)}, s32[256]{0:T(256)S(1)}, u32[]{:S(2)}, u32[]{:S(2)}) %collective-permute-start.1) | collective-permute-done | bytes 1056 | tf_op jit(solution)/shard_map/ppermute | solution.py:159
  3.0 0.7 copy-done.1
  3.7 1.0 %copy-done = bf16[256,768]{1,0:T(8,128)(2,1)S(1)} copy-done((bf16[256,768]{1,0:T(8,128)(2,1)S(1)}, bf16[256,768]{1,0:T(8,128)(2,1)}, u32[]{:S(2)}) %copy-start) | copy-done | bytes 393240
  4.7 0.3 pack.1
  5.0 1.8 %collective-permute-start.6 = (bf16[528,768]{1,0:T(8,128)(2,1)S(1)}, bf16[528,768]{1,0:T(8,128)(2,1)S(1)}, u32[]{:S(2)}, u32[]{:S(2)}) collective-permute-start(bf16[528,768]{1,0:T(8,128)(2,1)S(1)} %get-tuple-element.9.refs_0_), channel_id=1, source_target_pairs={{6,0},{25,1},{0,2},{27,3},{2,4},{29,5},{4,6},{31,7},{14,8},{1,9},{... | collective-permute-start | bytes 2433032 | tf_op jit(solution)/shard_map/ppermute | solution.py:153
  6.8 2.2 %collective-permute-start.10 = (bf16[528,768]{1,0:T(8,128)(2,1)S(1)}, bf16[528,768]{1,0:T(8,128)(2,1)S(1)}, u32[]{:S(2)}, u32[]{:S(2)}) collective-permute-start(bf16[528,768]{1,0:T(8,128)(2,1)S(1)} %get-tuple-element.9.refs_0_), channel_id=1, source_target_pairs={{2,0},{9,1},{4,2},{11,3},{6,4},{13,5},{0,6},{15,7},{10,8},{17,9},{... | collective-permute-start | bytes 2433032 | tf_op jit(solution)/shard_map/ppermute | solution.py:153
  9.0 1.3 %collective-permute-start.3 = (bf16[528,768]{1,0:T(8,128)(2,1)S(1)}, bf16[528,768]{1,0:T(8,128)(2,1)S(1)}, u32[]{:S(2)}, u32[]{:S(2)}) collective-permute-start(bf16[528,768]{1,0:T(8,128)(2,1)S(1)} %get-tuple-element.9.refs_0_), channel_id=1, source_target_pairs={{32,0},{97,1},{34,2},{99,3},{36,4},{101,5},{38,6},{103,7},{40,8},{... | collective-permute-start | bytes 2433032 | tf_op jit(solution)/shard_map/ppermute | solution.py:153
  10.3 8.3 %collective-permute-done.6.refs_6_ = bf16[528,768]{1,0:T(8,128)(2,1)S(1)} collective-permute-done((bf16[528,768]{1,0:T(8,128)(2,1)S(1)}, bf16[528,768]{1,0:T(8,128)(2,1)S(1)}, u32[]{:S(2)}, u32[]{:S(2)}) %collective-permute-start.6) | collective-permute-done | bytes 811040 | tf_op jit(solution)/shard_map/ppermute | solution.py:153
  18.5 2.8 %collective-permute-start.7 = (bf16[528,768]{1,0:T(8,128)(2,1)S(1)}, bf16[528,768]{1,0:T(8,128)(2,1)S(1)}, u32[]{:S(2)}, u32[]{:S(2)}) collective-permute-start(bf16[528,768]{1,0:T(8,128)(2,1)S(1)} %collective-permute-done.6.refs_6_), channel_id=1, source_target_pairs={{24,0},{3,1},{26,2},{5,3},{28,4},{7,5},{30,6},{1,7},{0,8},{11,9},{... | collective-permute-start | bytes 2433032 | tf_op jit(solution)/shard_map/ppermute | solution.py:153
  21.3 2.9 %collective-permute-start.2 = (bf16[272,768]{1,0:T(8,128)(2,1)S(1)}, bf16[272,768]{1,0:T(8,128)(2,1)S(1)}, u32[]{:S(2)}, u32[]{:S(2)}) collective-permute-start(bf16[272,768]{1,0:T(8,128)(2,1)S(1)} %get-tuple-element.10), channel_id=1, source_target_pairs={{64,0},{65,1},{66,2},{67,3},{68,4},{69,5},{70,6},{71,7},{72,8},{73... | collective-permute-start | bytes 1253384 | tf_op jit(solution)/shard_map/ppermute | solution.py:153
  24.2 2.0 %collective-permute-start.5 = (bf16[528,768]{1,0:T(8,128)(2,1)S(1)}, bf16[528,768]{1,0:T(8,128)(2,1)S(1)}, u32[]{:S(2)}, u32[]{:S(2)}) collective-permute-start(bf16[528,768]{1,0:T(8,128)(2,1)S(1)} %collective-permute-done.3.refs_2_), channel_id=1, source_target_pairs={{0,1},{1,0},{2,3},{3,2},{4,5},{5,4},{6,7},{7,6},{8,9},{9,8},{10,11... | collective-permute-start | bytes 2433032 | tf_op jit(solution)/shard_map/ppermute | solution.py:159
  26.2 8.2 %collective-permute-done.2.refs_1_ = bf16[272,768]{1,0:T(8,128)(2,1)S(1)} collective-permute-done((bf16[272,768]{1,0:T(8,128)(2,1)S(1)}, bf16[272,768]{1,0:T(8,128)(2,1)S(1)}, u32[]{:S(2)}, u32[]{:S(2)}) %collective-permute-start.2) | collective-permute-done | bytes 417824 | tf_op jit(solution)/shard_map/ppermute | solution.py:153
  34.4 0.4 collective-permute-start.4
  34.9 0.3 collective-permute-start.8
  35.1 1.7 %collective-permute-start.13 = (bf16[528,768]{1,0:T(8,128)(2,1)S(1)}, bf16[528,768]{1,0:T(8,128)(2,1)S(1)}, u32[]{:S(2)}, u32[]{:S(2)}) collective-permute-start(bf16[528,768]{1,0:T(8,128)(2,1)S(1)} %collective-permute-done.10.refs_5_), channel_id=1, source_target_pairs={{2,0},{9,1},{4,2},{11,3},{6,4},{13,5},{0,6},{15,7},{10,8},{17,9},{... | collective-permute-start | bytes 2433032 | tf_op jit(solution)/shard_map/ppermute | solution.py:153
  36.9 0.9 %collective-permute-start.12 = (bf16[528,768]{1,0:T(8,128)(2,1)S(1)}, bf16[528,768]{1,0:T(8,128)(2,1)S(1)}, u32[]{:S(2)}, u32[]{:S(2)}) collective-permute-start(bf16[528,768]{1,0:T(8,128)(2,1)S(1)} %collective-permute-done.11.refs_5_), channel_id=1, source_target_pairs={{8,0},{7,1},{10,2},{1,3},{12,4},{3,5},{14,6},{5,7},{16,8},{15,9},{... | collective-permute-start | bytes 2433032 | tf_op jit(solution)/shard_map/ppermute | solution.py:153
  37.8 4.3 %score.5 = (f32[2048,128]{1,0:T(8,128)S(1)}, f32[2048,128]{1,0:T(8,128)S(1)}) custom-call(bf16[528,768]{1,0:T(8,128)(2,1)S(1)} %get-tuple-element.9.refs_0_, bf16[272,768]{1,0:T(8,128)(2,1)S(1)} %collective-permute-done.2.refs_1_, bf16[528,768]{1,0:T(8,128)(2,1)S(1)} %collective-permute-done.3.refs_2_, bf16[272,768]{1,0:T(8,128)(2,1)S(1)} %collective-permute-done.4.refs_3_, ...), custom_call_target="tpu_custom_call" | custom-call | flops 4026531840 | bytes 5111808 | tf_op jit(solution)/shard_map/score/pallas_call | solution.py:124
  42.2 3.5 %score.6.refs_6_ = f32[2048,128]{1,0:T(8,128)S(1)} custom-call(bf16[528,768]{1,0:T(8,128)(2,1)S(1)} %get-tuple-element.9.refs_0_, bf16[272,768]{1,0:T(8,128)(2,1)S(1)} %collective-permute-done.2.refs_1_, bf16[528,768]{1,0:T(8,128)(2,1)S(1)} %collective-permute-done.3.refs_2_, bf16[272,768]{1,0:T(8,128)(2,1)S(1)} %collective-permute-done.4.refs_3_, ...), custom_call_target="tpu_custom_call" | custom-call | flops 3221225472 | bytes 4718592 | tf_op jit(solution)/shard_map/score/pallas_call | solution.py:124
  45.7 8.8 %collective-permute-done.8.refs_6_ = bf16[528,768]{1,0:T(8,128)(2,1)S(1)} collective-permute-done((bf16[528,768]{1,0:T(8,128)(2,1)S(1)}, bf16[528,768]{1,0:T(8,128)(2,1)S(1)}, u32[]{:S(2)}, u32[]{:S(2)}) %collective-permute-start.8) | collective-permute-done | bytes 811040 | tf_op jit(solution)/shard_map/ppermute | solution.py:153
  54.5 0.3 collective-permute-start.9
  54.8 1.9 %score.7.refs_7_ = f32[2048,128]{1,0:T(8,128)S(1)} custom-call(bf16[528,768]{1,0:T(8,128)(2,1)S(1)} %get-tuple-element.9.refs_0_, bf16[272,768]{1,0:T(8,128)(2,1)S(1)} %collective-permute-done.2.refs_1_, bf16[528,768]{1,0:T(8,128)(2,1)S(1)} %collective-permute-done.3.refs_2_, bf16[272,768]{1,0:T(8,128)(2,1)S(1)} %collective-permute-done.4.refs_3_, ...), custom_call_target="tpu_custom_call" | custom-call | flops 1610612736 | bytes 3932160 | tf_op jit(solution)/shard_map/score/pallas_call | solution.py:124
  56.7 3.6 %score.8.refs_6_ = f32[2048,128]{1,0:T(8,128)S(1)} custom-call(bf16[528,768]{1,0:T(8,128)(2,1)S(1)} %get-tuple-element.9.refs_0_, bf16[272,768]{1,0:T(8,128)(2,1)S(1)} %collective-permute-done.2.refs_1_, bf16[528,768]{1,0:T(8,128)(2,1)S(1)} %collective-permute-done.3.refs_2_, bf16[272,768]{1,0:T(8,128)(2,1)S(1)} %collective-permute-done.4.refs_3_, ...), custom_call_target="tpu_custom_call" | custom-call | flops 3221225472 | bytes 4718592 | tf_op jit(solution)/shard_map/score/pallas_call | solution.py:124
  60.3 2.6 %collective-permute-done.9.refs_5_ = bf16[272,768]{1,0:T(8,128)(2,1)S(1)} collective-permute-done((bf16[272,768]{1,0:T(8,128)(2,1)S(1)}, bf16[272,768]{1,0:T(8,128)(2,1)S(1)}, u32[]{:S(2)}, u32[]{:S(2)}) %collective-permute-start.9) | collective-permute-done | bytes 417824 | tf_op jit(solution)/shard_map/ppermute | solution.py:153
  62.9 1.2 %score.9 = f32[1,2048]{1,0:T(1,128)S(1)} custom-call(bf16[528,768]{1,0:T(8,128)(2,1)S(1)} %get-tuple-element.9.refs_0_, bf16[272,768]{1,0:T(8,128)(2,1)S(1)} %collective-permute-done.2.refs_1_, bf16[528,768]{1,0:T(8,128)(2,1)S(1)} %collective-permute-done.3.refs_2_, bf16[272,768]{1,0:T(8,128)(2,1)S(1)} %collective-permute-done.4.refs_3_, ...), custom_call_target="tpu_custom_call" | custom-call | flops 805306368 | bytes 3538944 | tf_op jit(solution)/shard_map/score/pallas_call | solution.py:124
  64.2 1.2 %collective-permute-done.14 = f32[1024]{0:T(1024)S(1)} collective-permute-done((f32[1024]{0:T(1024)S(1)}, f32[1024]{0:T(1024)S(1)}, u32[]{:S(2)}, u32[]{:S(2)}) %collective-permute-start.14) | collective-permute-done | bytes 4128 | tf_op jit(solution)/shard_map/ppermute | solution.py:159
  65.3 2.7 %collective-permute-start.16 = (f32[512]{0:T(512)S(1)}, f32[512]{0:T(512)S(1)}, u32[]{:S(2)}, u32[]{:S(2)}) collective-permute-start(f32[512]{0:T(512)S(1)} %slice.37), channel_id=1, source_target_pairs={{96,0},{33,1},{98,2},{35,3},{100,4},{37,5},{102,6},{39,7},{104,8},... | collective-permute-start | bytes 6152 | tf_op jit(solution)/shard_map/ppermute | solution.py:153
  68.1 0.4 collective-permute-start.15
  68.4 0.4 collective-permute-done.16
  68.8 1.5 %collective-permute-start.17 = (f32[256]{0:T(256)S(1)}, f32[256]{0:T(256)S(1)}, u32[]{:S(2)}, u32[]{:S(2)}) collective-permute-start(f32[256]{0:T(256)S(1)} %slice.39), channel_id=1, source_target_pairs={{0,1},{1,0},{2,3},{3,2},{4,5},{5,4},{6,7},{7,6},{8,9},{9,8},{10,11... | collective-permute-start | bytes 3080 | tf_op jit(solution)/shard_map/ppermute | solution.py:159
  70.3 1.7 %collective-permute-done.15 = f32[256]{0:T(256)S(1)} collective-permute-done((f32[256]{0:T(256)S(1)}, f32[256]{0:T(256)S(1)}, u32[]{:S(2)}, u32[]{:S(2)}) %collective-permute-start.15) | collective-permute-done | bytes 1056 | tf_op jit(solution)/shard_map/ppermute | solution.py:153
  72.0 0.6 maximum_maximum_fusion
  (21 shorter events, 0.2 us)
Async XLA Ops:
  0.0 3.0 %collective-permute-start = (bf16[256,768]{1,0:T(8,128)(2,1)}, bf16[256,768]{1,0:T(8,128)(2,1)S(1)}, u32[]{:S(2)}, u32[]{:S(2)}) collective-permute-start(bf16[256,768]{1,0:T(8,128)(2,1)} %own_ref.1), channel_id=1, source_target_pairs={{0,1},{1,0},{2,3},{3,2},{4,5},{5,4},{6,7},{7,6},{8,9},{9,8},{10,11... | collective-permute-start | bytes 1179656 | tf_op jit(solution)/shard_map/ppermute | solution.py:159
  1.4 1.6 %collective-permute-start.1 = (s32[256]{0:T(256)}, s32[256]{0:T(256)S(1)}, u32[]{:S(2)}, u32[]{:S(2)}) collective-permute-start(s32[256]{0:T(256)} %param.3), channel_id=1, source_target_pairs={{0,1},{1,0},{2,3},{3,2},{4,5},{5,4},{6,7},{7,6},{8,9},{9,8},{10,11... | collective-permute-start | bytes 3080 | tf_op jit(solution)/shard_map/ppermute | solution.py:159
  3.0 0.7 copy-start.1
  3.7 1.0 %copy-start = (bf16[256,768]{1,0:T(8,128)(2,1)S(1)}, bf16[256,768]{1,0:T(8,128)(2,1)}, u32[]{:S(2)}) copy-start(bf16[256,768]{1,0:T(8,128)(2,1)} %own_ref.1) | copy-start | bytes 1179652
  5.0 13.6 %collective-permute-start.6 = (bf16[528,768]{1,0:T(8,128)(2,1)S(1)}, bf16[528,768]{1,0:T(8,128)(2,1)S(1)}, u32[]{:S(2)}, u32[]{:S(2)}) collective-permute-start(bf16[528,768]{1,0:T(8,128)(2,1)S(1)} %get-tuple-element.9.refs_0_), channel_id=1, source_target_pairs={{6,0},{25,1},{0,2},{27,3},{2,4},{29,5},{4,6},{31,7},{14,8},{1,9},{... | collective-permute-start | bytes 2433032 | tf_op jit(solution)/shard_map/ppermute | solution.py:153
  6.8 17.5 %collective-permute-start.10 = (bf16[528,768]{1,0:T(8,128)(2,1)S(1)}, bf16[528,768]{1,0:T(8,128)(2,1)S(1)}, u32[]{:S(2)}, u32[]{:S(2)}) collective-permute-start(bf16[528,768]{1,0:T(8,128)(2,1)S(1)} %get-tuple-element.9.refs_0_), channel_id=1, source_target_pairs={{2,0},{9,1},{4,2},{11,3},{6,4},{13,5},{0,6},{15,7},{10,8},{17,9},{... | collective-permute-start | bytes 2433032 | tf_op jit(solution)/shard_map/ppermute | solution.py:153
  9.0 15.3 %collective-permute-start.3 = (bf16[528,768]{1,0:T(8,128)(2,1)S(1)}, bf16[528,768]{1,0:T(8,128)(2,1)S(1)}, u32[]{:S(2)}, u32[]{:S(2)}) collective-permute-start(bf16[528,768]{1,0:T(8,128)(2,1)S(1)} %get-tuple-element.9.refs_0_), channel_id=1, source_target_pairs={{32,0},{97,1},{34,2},{99,3},{36,4},{101,5},{38,6},{103,7},{40,8},{... | collective-permute-start | bytes 2433032 | tf_op jit(solution)/shard_map/ppermute | solution.py:153
  18.5 16.3 %collective-permute-start.7 = (bf16[528,768]{1,0:T(8,128)(2,1)S(1)}, bf16[528,768]{1,0:T(8,128)(2,1)S(1)}, u32[]{:S(2)}, u32[]{:S(2)}) collective-permute-start(bf16[528,768]{1,0:T(8,128)(2,1)S(1)} %collective-permute-done.6.refs_6_), channel_id=1, source_target_pairs={{24,0},{3,1},{26,2},{5,3},{28,4},{7,5},{30,6},{1,7},{0,8},{11,9},{... | collective-permute-start | bytes 2433032 | tf_op jit(solution)/shard_map/ppermute | solution.py:153
  21.3 13.1 %collective-permute-start.2 = (bf16[272,768]{1,0:T(8,128)(2,1)S(1)}, bf16[272,768]{1,0:T(8,128)(2,1)S(1)}, u32[]{:S(2)}, u32[]{:S(2)}) collective-permute-start(bf16[272,768]{1,0:T(8,128)(2,1)S(1)} %get-tuple-element.10), channel_id=1, source_target_pairs={{64,0},{65,1},{66,2},{67,3},{68,4},{69,5},{70,6},{71,7},{72,8},{73... | collective-permute-start | bytes 1253384 | tf_op jit(solution)/shard_map/ppermute | solution.py:153
  24.2 12.7 %collective-permute-start.11 = (bf16[528,768]{1,0:T(8,128)(2,1)S(1)}, bf16[528,768]{1,0:T(8,128)(2,1)S(1)}, u32[]{:S(2)}, u32[]{:S(2)}) collective-permute-start(bf16[528,768]{1,0:T(8,128)(2,1)S(1)} %collective-permute-done.10.refs_5_), channel_id=1, source_target_pairs={{8,0},{7,1},{10,2},{1,3},{12,4},{3,5},{14,6},{5,7},{16,8},{15,9},{... | collective-permute-start | bytes 2433032 | tf_op jit(solution)/shard_map/ppermute | solution.py:153
  24.2 13.6 %collective-permute-start.5 = (bf16[528,768]{1,0:T(8,128)(2,1)S(1)}, bf16[528,768]{1,0:T(8,128)(2,1)S(1)}, u32[]{:S(2)}, u32[]{:S(2)}) collective-permute-start(bf16[528,768]{1,0:T(8,128)(2,1)S(1)} %collective-permute-done.3.refs_2_), channel_id=1, source_target_pairs={{0,1},{1,0},{2,3},{3,2},{4,5},{5,4},{6,7},{7,6},{8,9},{9,8},{10,11... | collective-permute-start | bytes 2433032 | tf_op jit(solution)/shard_map/ppermute | solution.py:159
  34.4 3.4 %collective-permute-start.4 = (bf16[272,768]{1,0:T(8,128)(2,1)S(1)}, bf16[272,768]{1,0:T(8,128)(2,1)S(1)}, u32[]{:S(2)}, u32[]{:S(2)}) collective-permute-start(bf16[272,768]{1,0:T(8,128)(2,1)S(1)} %collective-permute-done.2.refs_1_), channel_id=1, source_target_pairs={{0,1},{1,0},{2,3},{3,2},{4,5},{5,4},{6,7},{7,6},{8,9},{9,8},{10,11... | collective-permute-start | bytes 1253384 | tf_op jit(solution)/shard_map/ppermute | solution.py:159
  34.9 19.6 %collective-permute-start.8 = (bf16[528,768]{1,0:T(8,128)(2,1)S(1)}, bf16[528,768]{1,0:T(8,128)(2,1)S(1)}, u32[]{:S(2)}, u32[]{:S(2)}) collective-permute-start(bf16[528,768]{1,0:T(8,128)(2,1)S(1)} %collective-permute-done.7.refs_6_), channel_id=1, source_target_pairs={{24,0},{3,1},{26,2},{5,3},{28,4},{7,5},{30,6},{1,7},{0,8},{11,9},{... | collective-permute-start | bytes 2433032 | tf_op jit(solution)/shard_map/ppermute | solution.py:153
  35.1 19.7 %collective-permute-start.13 = (bf16[528,768]{1,0:T(8,128)(2,1)S(1)}, bf16[528,768]{1,0:T(8,128)(2,1)S(1)}, u32[]{:S(2)}, u32[]{:S(2)}) collective-permute-start(bf16[528,768]{1,0:T(8,128)(2,1)S(1)} %collective-permute-done.10.refs_5_), channel_id=1, source_target_pairs={{2,0},{9,1},{4,2},{11,3},{6,4},{13,5},{0,6},{15,7},{10,8},{17,9},{... | collective-permute-start | bytes 2433032 | tf_op jit(solution)/shard_map/ppermute | solution.py:153
  36.9 19.8 %collective-permute-start.12 = (bf16[528,768]{1,0:T(8,128)(2,1)S(1)}, bf16[528,768]{1,0:T(8,128)(2,1)S(1)}, u32[]{:S(2)}, u32[]{:S(2)}) collective-permute-start(bf16[528,768]{1,0:T(8,128)(2,1)S(1)} %collective-permute-done.11.refs_5_), channel_id=1, source_target_pairs={{8,0},{7,1},{10,2},{1,3},{12,4},{3,5},{14,6},{5,7},{16,8},{15,9},{... | collective-permute-start | bytes 2433032 | tf_op jit(solution)/shard_map/ppermute | solution.py:153
  54.5 8.4 %collective-permute-start.9 = (bf16[272,768]{1,0:T(8,128)(2,1)S(1)}, bf16[272,768]{1,0:T(8,128)(2,1)S(1)}, u32[]{:S(2)}, u32[]{:S(2)}) collective-permute-start(bf16[272,768]{1,0:T(8,128)(2,1)S(1)} %slice.40), channel_id=1, source_target_pairs={{6,0},{25,1},{0,2},{27,3},{2,4},{29,5},{4,6},{31,7},{14,8},{1,9},{... | collective-permute-start | bytes 1253384 | tf_op jit(solution)/shard_map/ppermute | solution.py:153
  64.1 1.2 %collective-permute-start.14 = (f32[1024]{0:T(1024)S(1)}, f32[1024]{0:T(1024)S(1)}, u32[]{:S(2)}, u32[]{:S(2)}) collective-permute-start(f32[1024]{0:T(1024)S(1)} %bitcast.7), channel_id=1, source_target_pairs={{0,1},{1,0},{2,3},{3,2},{4,5},{5,4},{6,7},{7,6},{8,9},{9,8},{10,11... | collective-permute-start | bytes 12296 | tf_op jit(solution)/shard_map/ppermute | solution.py:159
  65.3 3.5 %collective-permute-start.16 = (f32[512]{0:T(512)S(1)}, f32[512]{0:T(512)S(1)}, u32[]{:S(2)}, u32[]{:S(2)}) collective-permute-start(f32[512]{0:T(512)S(1)} %slice.37), channel_id=1, source_target_pairs={{96,0},{33,1},{98,2},{35,3},{100,4},{37,5},{102,6},{39,7},{104,8},... | collective-permute-start | bytes 6152 | tf_op jit(solution)/shard_map/ppermute | solution.py:153
  68.1 3.9 %collective-permute-start.15 = (f32[256]{0:T(256)S(1)}, f32[256]{0:T(256)S(1)}, u32[]{:S(2)}, u32[]{:S(2)}) collective-permute-start(f32[256]{0:T(256)S(1)} %slice.36), channel_id=1, source_target_pairs={{64,0},{65,1},{66,2},{67,3},{68,4},{69,5},{70,6},{71,7},{72,8},{73... | collective-permute-start | bytes 3080 | tf_op jit(solution)/shard_map/ppermute | solution.py:153
  68.8 3.2 %collective-permute-start.17 = (f32[256]{0:T(256)S(1)}, f32[256]{0:T(256)S(1)}, u32[]{:S(2)}, u32[]{:S(2)}) collective-permute-start(f32[256]{0:T(256)S(1)} %slice.39), channel_id=1, source_target_pairs={{0,1},{1,0},{2,3},{3,2},{4,5},{5,4},{6,7},{7,6},{8,9},{9,8},{10,11... | collective-permute-start | bytes 3080 | tf_op jit(solution)/shard_map/ppermute | solution.py:159

commit v3 on v2

v3 whole, which is shorter than its diff:
```python
import functools

import jax
import jax.numpy as jnp
from jax import lax
from jax.experimental import pallas as pl
from jax.experimental.pallas import tpu as pltpu
from jax.sharding import PartitionSpec as P

AXES = ("grp", "dev")
ROWS = 256
TAIL = 16
HALF = ROWS + TAIL
BLOCK = HALF + ROWS
SECOND = HALF
LANES = 128
FLOOR = -1.0


def unit(rows):
    values = rows.astype(jnp.float32)
    norm = jnp.sqrt(jnp.sum(values * values, axis=1, keepdims=True) + 1e-06)
    return (values / norm).astype(jnp.bfloat16)


def spread(ids):
    return jnp.broadcast_to(ids.astype(jnp.float32), (TAIL, ROWS)).astype(jnp.bfloat16)


def own_kernel(rows_ref, ids_ref, half_ref):
    half_ref[0:ROWS, :] = unit(rows_ref[...])
    half_ref[ROWS:HALF, 0:ROWS] = spread(ids_ref[...])
    half_ref[ROWS:HALF, ROWS:] = jnp.zeros((TAIL, half_ref.shape[1] - ROWS), jnp.bfloat16)


def chip_kernel(half_ref, rows_ref, ids_ref, block_ref):
    block_ref[0:HALF, :] = half_ref[...]
    block_ref[ROWS:HALF, ROWS : 2 * ROWS] = spread(ids_ref[...])
    block_ref[SECOND:BLOCK, :] = unit(rows_ref[...])


def call(kernel, name, rows, width, *operands):
    return pl.pallas_call(
        kernel,
        out_shape=jax.ShapeDtypeStruct((rows, width), jnp.bfloat16),
        compiler_params=pltpu.CompilerParams(vmem_limit_bytes=16 * 1024 * 1024),
        name=name,
    )(*operands)


OWN, OTHER = (0, 0), (SECOND, ROWS)


def whole(block):
    return (block, (OWN,) if block.shape[0] == HALF else (OWN, OTHER))


def ids_row(ref, lane):
    return ref[ROWS:HALF, lane : lane + ROWS].astype(jnp.float32)[0:1, :]


def score_kernel(groups, key_parts, n_blocks, first, last, collect, *refs):
    blocks, refs = refs[:n_blocks], list(refs[n_blocks:])
    key_parts = [(blocks[at], row, lane) for at, (row, lane) in key_parts]
    row_index = lax.broadcasted_iota(jnp.int32, (ROWS, ROWS), 0)
    col_index = lax.broadcasted_iota(jnp.int32, (ROWS, ROWS), 1)
    states = [(None, None) if first else (refs.pop(0), refs.pop(0)) for _ in groups]
    results = [(refs.pop(0), refs.pop(0) if first else column_ref) for _, column_ref in states]
    tops = {}
    for group, (query_parts, own_key) in enumerate(groups):
        before_ref, (best_ref, column_ref) = states[group][0], results[group]
        for place, (at, (row, lane)) in enumerate(query_parts):
            here = slice(place * ROWS, (place + 1) * ROWS)
            rows = blocks[at][row : row + ROWS, :]
            if first:
                ids = jnp.broadcast_to(ids_row(blocks[at], lane), (ROWS, ROWS))
                column = jnp.sum(jnp.where(row_index == col_index, ids, 0.0), axis=1, keepdims=True)
                column = jnp.broadcast_to(column, (ROWS, LANES))
                column_ref[here, :] = column
                best = jnp.full((ROWS, LANES), FLOOR, jnp.float32)
            else:
                column, best = column_ref[here, :], before_ref[here, :]
            for number, (key_ref, key_row, key_lane) in enumerate(key_parts):
                scores = lax.dot_general(
                    rows,
                    key_ref[key_row : key_row + ROWS, :],
                    (((1,), (1,)), ((), ())),
                    preferred_element_type=jnp.float32,
                )
                ids = ids_row(key_ref, key_lane)
                for start in range(0, ROWS, LANES):
                    lanes = slice(start, start + LANES)
                    match = column == ids[:, lanes]
                    if own_key and place == 0 and number == 0:
                        match = match & (row_index[:, lanes] != col_index[:, lanes])
                    kept = jnp.where(match, scores[:, lanes], FLOOR)
                    best = jnp.maximum(best, kept)
                    if number >= collect:
                        top = jnp.max(kept.reshape(ROWS // 8, 8, LANES), axis=0)
                        at_top = (number, start)
                        tops[at_top] = jnp.maximum(tops[at_top], top) if at_top in tops else top
            if last:
                best_ref[0:1, here] = jnp.max(best.T, axis=0, keepdims=True)
            else:
                best_ref[here, :] = best
    for (number, start), top in tops.items():
        at = (number - collect) * ROWS + start
        refs[0][0:1, at : at + LANES] = jnp.max(top, axis=0, keepdims=True)


def score(groups, keys, states=None, last=False, collect=None, own_key=False):
    blocks = []

    def listed(pieces):
        found = []
        for block, parts in pieces:
            at = next((i for i, b in enumerate(blocks) if b is block), len(blocks))
            if at == len(blocks):
                blocks.append(block)
            found += [(at, part) for part in parts]
        return found

    listed_groups = [(listed(group), own_key and i == 0) for i, group in enumerate(groups)]
    key_parts = listed(keys)
    counts = [len(parts) * ROWS for parts, _ in listed_groups]
    count, key_rows, width = sum(counts), len(key_parts) * ROWS, blocks[0].shape[1]
    skipped = len(key_parts) if collect is None else sum(len(parts) for _, parts in keys[:collect])
    first = states is None
    shapes = []
    for rows in counts:
        wide = jax.ShapeDtypeStruct((rows, LANES), jnp.float32)
        shapes.append(jax.ShapeDtypeStruct((1, rows), jnp.float32) if last else wide)
        if first:
            shapes.append(wide)
    if collect is not None:
        shapes.append(jax.ShapeDtypeStruct((1, key_rows - skipped * ROWS), jnp.float32))
    result = pl.pallas_call(
        functools.partial(score_kernel, listed_groups, key_parts, len(blocks), first, last, skipped),
        out_shape=tuple(shapes),
        compiler_params=pltpu.CompilerParams(vmem_limit_bytes=32 * 1024 * 1024),
        cost_estimate=pl.CostEstimate(
            flops=2 * count * key_rows * width,
            bytes_accessed=2 * width * (count + key_rows),
            transcendentals=0,
        ),
        name="score",
    )(*blocks, *(() if first else (x for state in states for x in state)))
    if first:
        states = [(result[2 * i], result[2 * i + 1]) for i in range(len(groups))]
    else:
        states = [(result[i], states[i][1]) for i in range(len(groups))]
    return states, (None if collect is None else result[-1][0])


def per_device(embeddings, cluster_id):
    ny, nz, nx = 4, 4, 4

    def place(y, z, x, core):
        return (((y % ny) * nz + z % nz) * nx + x % nx) * 2 + core

    def fetch(value, *offsets):
        pairs = []
        for y in range(ny):
            for z in range(nz):
                for x in range(nx):
                    for core, (dy, dz, dx) in enumerate(offsets):
                        pairs.append((place(y + dy, z + dz, x + dx, core), place(y, z, x, core)))
        return lax.ppermute(value, AXES, pairs)

    def give(value, *offsets):
        return fetch(value, *(tuple(-o for o in offset) for offset in offsets))

    def swap(value):
        return lax.ppermute(value, AXES, [(i, i ^ 1) for i in range(ny * nz * nx * 2)])

    width = embeddings.shape[1]
    ids = cluster_id.reshape(1, ROWS)
    half = call(own_kernel, "own", HALF, width, embeddings, ids)
    block = call(chip_kernel, "chip", BLOCK, width, half, swap(embeddings), swap(cluster_id).reshape(1, ROWS))

    key1 = fetch(block, (0, 0, 1), (0, 1, 0))
    key2 = fetch(block, (0, 0, 2), (0, 2, 0))
    near = fetch(block, (1, 0, 0), (-1, 0, 0))
    far = fetch(half, (2, 0, 0), (2, 0, 0))
    key3 = fetch(key1, (0, 1, 0), (0, 0, -1))
    key4 = fetch(key2, (0, -1, 0), (0, 0, 1))
    key5 = fetch(key2[:HALF], (0, 2, 0), (0, 0, 2))

    groups = [[(block, (OWN, OTHER))], [whole(near), (swap(near), (OTHER, OWN)), whole(far), whole(swap(far))]]
    keys = [(block, (OWN,)), whole(key1), whole(key2)]
    states, top1 = score(groups, keys, collect=1, own_key=True)
    states, top4 = score(groups, [whole(key4)], states, collect=0)
    states, top3 = score(groups, [whole(key3)], states, collect=0)
    (best, best2), _ = score(groups, [whole(key5)], states, last=True)
    best, best2 = best[0].reshape(1, 2 * ROWS), best2[0].reshape(3, 2 * ROWS)
    best, best2 = [best[0], best2[0], best2[1]], best2[2]
    homes = [give(top1[: 2 * ROWS], (0, 0, 1), (0, 1, 0)), give(top3, (0, 1, 1), (0, 1, -1)), give(top4, (0, -1, 2), (0, 2, 1))]

    from_far = give(best2, (2, 0, 0), (2, 0, 0))
    from_up = give(best[1], (1, 0, 0), (-1, 0, 0))
    from_down = give(best[2], (-1, 0, 0), (1, 0, 0))
    home = functools.reduce(jnp.maximum, [best[0], *homes, from_far, from_up, from_down])
    return jnp.maximum(home[:ROWS], swap(home[ROWS:]))


def solution(mesh):
    in_specs = (P(AXES, None), P(AXES))
    return jax.shard_map(
        per_device, mesh=mesh, in_specs=in_specs, out_specs=P(AXES), check_vma=False
    )
```

time: 72.7 us -> 67.3 us (0.926)
  starting transfers between devices: 22.7 us -> 39.7 us
  waiting for transfers between devices: 32.7 us -> 16 us
  Pallas kernels: 14.8 us -> 9.78 us
    ppermute x12 -> x13, waiting for transfers between devices: 30 us -> 14.8 us  [fetch(): return lax.ppermute(value, AXES, pairs)]
    ppermute x6 -> x5, starting transfers between devices: 5.42 us -> 14.2 us  [swap(): lax.ppermute(value, AXES, [(i, i ^ 1) for i in range(ny * nz * nx * 2)])]
    ppermute x12 -> x13, starting transfers between devices: 17.3 us -> 25.4 us  [fetch(): return lax.ppermute(value, AXES, pairs)]
    pallas_call x6, Pallas kernels: 14.8 us -> 9.78 us  [the longest x4 9.42 us: score(): pl.pallas_call(functools.partial(score_kernel, listed_groups, key_parts,...]
    ppermute x6 -> x5, waiting for transfers between devices: 2.72 us -> 1.2 us  [swap(): lax.ppermute(value, AXES, [(i, i ^ 1) for i in range(ny * nz * nx * 2)])]
  transfers between devices with their start and end apart: 18 -> 18, of which waited for: 8 -> 6; matrix products, arithmetic and copies ran while one was open for 0% -> 0% of each run, Pallas kernels for 18% -> 12%
where the time goes in v3:
time: 67.3 us; the launch traced here: 67.2 us
  starting transfers between devices  39.7 us (59%)
  waiting for transfers between devices  16 us (24%)
  Pallas kernels  9.78 us (15%)
  local copies, waits for them, and re-layouts  1.04 us (2%)
    ppermute x13, starting transfers between devices, fetch(): return lax.ppermute(value, AXES, pairs)  25.4 us
    ppermute x13, waiting for transfers between devices, fetch(): return lax.ppermute(value, AXES, pairs)  14.8 us
    ppermute x5, starting transfers between devices, swap(): lax.ppermute(value, AXES, [(i, i ^ 1) for i in range(ny * nz * nx * 2)])  14.2 us
    pallas_call x4, Pallas kernels, score(): pl.pallas_call(functools.partial(score_kernel, listed_groups, key_parts,...  9.42 us
  transfers between devices with their start and end apart: 18, of which 6 were waited for; matrix products, arithmetic and copies ran while one was open for 0% of the time, Pallas kernels for 12%

profile of v3, /device:TPU:1, one launch (start us, length us, event | category | flops | bytes accessed | tf_op | source)
XLA Modules:
  0.0 67.2 jit_solution(5299988906080738113)
XLA Ops:
  0.0 1.4 %collective-permute-start = (bf16[256,768]{1,0:T(8,128)(2,1)}, bf16[256,768]{1,0:T(8,128)(2,1)S(1)}, u32[]{:S(2)}, u32[]{:S(2)}) collective-permute-start(bf16[256,768]{1,0:T(8,128)(2,1)} %rows_ref.1), channel_id=1, source_target_pairs={{0,1},{1,0},{2,3},{3,2},{4,5},{5,4},{6,7},{7,6},{8,9},{9,8},{10,11... | collective-permute-start | bytes 1179656 | tf_op jit(solution)/shard_map/ppermute | solution.py:174
  1.4 1.0 %copy-done = bf16[256,768]{1,0:T(8,128)(2,1)S(1)} copy-done((bf16[256,768]{1,0:T(8,128)(2,1)S(1)}, bf16[256,768]{1,0:T(8,128)(2,1)}, u32[]{:S(2)}) %copy-start) | copy-done | bytes 393240
  2.4 0.2 own.1.half_ref
  2.6 0.4 collective-permute-done.1
  3.0 0.0 collective-permute-done.rows_ref
  3.0 0.2 chip.1.refs_0_
  3.2 1.4 %collective-permute-start.2 = (bf16[528,768]{1,0:T(8,128)(2,1)S(1)}, bf16[528,768]{1,0:T(8,128)(2,1)S(1)}, u32[]{:S(2)}, u32[]{:S(2)}) collective-permute-start(bf16[528,768]{1,0:T(8,128)(2,1)S(1)} %chip.1.refs_0_), channel_id=1, source_target_pairs={{32,0},{97,1},{34,2},{99,3},{36,4},{101,5},{38,6},{103,7},{40,8},{... | collective-permute-start | bytes 2433032 | tf_op jit(solution)/shard_map/ppermute | solution.py:168
  4.6 3.6 %collective-permute-start.6 = (bf16[528,768]{1,0:T(8,128)(2,1)S(1)}, bf16[528,768]{1,0:T(8,128)(2,1)S(1)}, u32[]{:S(2)}, u32[]{:S(2)}) collective-permute-start(bf16[528,768]{1,0:T(8,128)(2,1)S(1)} %chip.1.refs_0_), channel_id=1, source_target_pairs={{4,0},{17,1},{6,2},{19,3},{0,4},{21,5},{2,6},{23,7},{12,8},{25,9},... | collective-permute-start | bytes 2433032 | tf_op jit(solution)/shard_map/ppermute | solution.py:168
  8.2 0.4 collective-permute-start.8
  8.7 2.6 %collective-permute-start.4 = (bf16[272,768]{1,0:T(8,128)(2,1)S(1)}, bf16[272,768]{1,0:T(8,128)(2,1)S(1)}, u32[]{:S(2)}, u32[]{:S(2)}) collective-permute-start(bf16[272,768]{1,0:T(8,128)(2,1)S(1)} %own.1.half_ref), channel_id=1, source_target_pairs={{64,0},{65,1},{66,2},{67,3},{68,4},{69,5},{70,6},{71,7},{72,8},{73... | collective-permute-start | bytes 1253384 | tf_op jit(solution)/shard_map/ppermute | solution.py:168
  11.3 5.1 %collective-permute-done.2.refs_1_ = bf16[528,768]{1,0:T(8,128)(2,1)S(1)} collective-permute-done((bf16[528,768]{1,0:T(8,128)(2,1)S(1)}, bf16[528,768]{1,0:T(8,128)(2,1)S(1)}, u32[]{:S(2)}, u32[]{:S(2)}) %collective-permute-start.2) | collective-permute-done | bytes 811040 | tf_op jit(solution)/shard_map/ppermute | solution.py:168
  16.4 9.1 %collective-permute-start.3 = (bf16[528,768]{1,0:T(8,128)(2,1)S(1)}, bf16[528,768]{1,0:T(8,128)(2,1)S(1)}, u32[]{:S(2)}, u32[]{:S(2)}) collective-permute-start(bf16[528,768]{1,0:T(8,128)(2,1)S(1)} %collective-permute-done.2.refs_1_), channel_id=1, source_target_pairs={{0,1},{1,0},{2,3},{3,2},{4,5},{5,4},{6,7},{7,6},{8,9},{9,8},{10,11... | collective-permute-start | bytes 2433032 | tf_op jit(solution)/shard_map/ppermute | solution.py:174
  25.4 0.0 collective-permute-done.6.refs_6_
  25.5 2.5 %collective-permute-start.10 = (bf16[528,768]{1,0:T(8,128)(2,1)S(1)}, bf16[528,768]{1,0:T(8,128)(2,1)S(1)}, u32[]{:S(2)}, u32[]{:S(2)}) collective-permute-start(bf16[528,768]{1,0:T(8,128)(2,1)S(1)} %collective-permute-done.6.refs_6_), channel_id=1, source_target_pairs={{24,0},{3,1},{26,2},{5,3},{28,4},{7,5},{30,6},{1,7},{0,8},{11,9},{... | collective-permute-start | bytes 2433032 | tf_op jit(solution)/shard_map/ppermute | solution.py:168
  27.9 0.0 collective-permute-start.5
  27.9 0.9 %collective-permute-start.9 = (bf16[528,768]{1,0:T(8,128)(2,1)S(1)}, bf16[528,768]{1,0:T(8,128)(2,1)S(1)}, u32[]{:S(2)}, u32[]{:S(2)}) collective-permute-start(bf16[528,768]{1,0:T(8,128)(2,1)S(1)} %collective-permute-done.8.refs_5_), channel_id=1, source_target_pairs={{8,0},{7,1},{10,2},{1,3},{12,4},{3,5},{14,6},{5,7},{16,8},{15,9},{... | collective-permute-start | bytes 2433032 | tf_op jit(solution)/shard_map/ppermute | solution.py:168
  28.9 2.5 %collective-permute-start.7 = (bf16[272,768]{1,0:T(8,128)(2,1)S(1)}, bf16[272,768]{1,0:T(8,128)(2,1)S(1)}, u32[]{:S(2)}, u32[]{:S(2)}) collective-permute-start(bf16[272,768]{1,0:T(8,128)(2,1)S(1)} %slice.35), channel_id=1, source_target_pairs={{16,0},{5,1},{18,2},{7,3},{20,4},{1,5},{22,6},{3,7},{24,8},{13,9},... | collective-permute-start | bytes 1253384 | tf_op jit(solution)/shard_map/ppermute | solution.py:168
  31.4 4.4 %score.4 = (f32[512,128]{1,0:T(8,128)S(1)}, f32[512,128]{1,0:T(8,128)S(1)}, f32[1536,128]{1,0:T(8,128)S(1)}, f32[1536,128]{1,0:T(8,128)S(1)}, f32[1,1024]{1,0:T(1,128)S(1)}) custom-call(bf16[528,768]{1,0:T(8,128)(2,1)S(1)} %chip.1.refs_0_, bf16[528,768]{1,0:T(8,128)(2,1)S(1)} %collective-permute-done.2.refs_1_, ...), custom_call_target="tpu_custom_call" | custom-call | flops 4026531840 | bytes 5111808 | tf_op jit(solution)/shard_map/score/pallas_call | solution.py:137
  35.8 5.8 %collective-permute-done.10.refs_5_ = bf16[528,768]{1,0:T(8,128)(2,1)S(1)} collective-permute-done((bf16[528,768]{1,0:T(8,128)(2,1)S(1)}, bf16[528,768]{1,0:T(8,128)(2,1)S(1)}, u32[]{:S(2)}, u32[]{:S(2)}) %collective-permute-start.10) | collective-permute-done | bytes 811040 | tf_op jit(solution)/shard_map/ppermute | solution.py:168
  41.6 1.9 %score.5 = (f32[512,128]{1,0:T(8,128)S(1)}, f32[1536,128]{1,0:T(8,128)S(1)}, f32[1,512]{1,0:T(1,128)S(1)}) custom-call(bf16[528,768]{1,0:T(8,128)(2,1)S(1)} %chip.1.refs_0_, bf16[528,768]{1,0:T(8,128)(2,1)S(1)} %collective-permute-done.2.refs_1_, bf16[528,768]{1,0:T(8,128)(2,1)S(1)} %collective-permute-done.3.refs_2_, ...), custom_call_target="tpu_custom_call" | custom-call | flops 1610612736 | bytes 3932160 | tf_op jit(solution)/shard_map/score/pallas_call | solution.py:137
  43.5 1.9 %score.6 = (f32[512,128]{1,0:T(8,128)S(1)}, f32[1536,128]{1,0:T(8,128)S(1)}, f32[1,512]{1,0:T(1,128)S(1)}) custom-call(bf16[528,768]{1,0:T(8,128)(2,1)S(1)} %chip.1.refs_0_, bf16[528,768]{1,0:T(8,128)(2,1)S(1)} %collective-permute-done.2.refs_1_, bf16[528,768]{1,0:T(8,128)(2,1)S(1)} %collective-permute-done.3.refs_2_, ...), custom_call_target="tpu_custom_call" | custom-call | flops 1610612736 | bytes 3932160 | tf_op jit(solution)/shard_map/score/pallas_call | solution.py:137
  45.4 1.2 %score.7 = (f32[1,512]{1,0:T(1,128)S(1)}, f32[1,1536]{1,0:T(1,128)S(1)}) custom-call(bf16[528,768]{1,0:T(8,128)(2,1)S(1)} %chip.1.refs_0_, bf16[528,768]{1,0:T(8,128)(2,1)S(1)} %collective-permute-done.2.refs_1_, bf16[528,768]{1,0:T(8,128)(2,1)S(1)} %collective-permute-done.3.refs_2_, bf16[272,768]{1,0:T(8,128)(2,1)S(1)} %collective-permute-done.4.refs_3_, ...), custom_call_target="tpu_custom_call" | custom-call | flops 805306368 | bytes 3538944 | tf_op jit(solution)/shard_map/score/pallas_call | solution.py:137
  46.7 2.4 %collective-permute-start.14 = (f32[512]{0:T(512)S(1)}, f32[512]{0:T(512)S(1)}, u32[]{:S(2)}, u32[]{:S(2)}) collective-permute-start(f32[512]{0:T(512)S(1)} %bitcast.17), channel_id=1, source_target_pairs={{64,0},{65,1},{66,2},{67,3},{68,4},{69,5},{70,6},{71,7},{72,8},{73... | collective-permute-start | bytes 6152 | tf_op jit(solution)/shard_map/ppermute | solution.py:168
  49.0 1.4 %collective-permute-start.15 = (f32[512]{0:T(512)S(1)}, f32[512]{0:T(512)S(1)}, u32[]{:S(2)}, u32[]{:S(2)}) collective-permute-start(f32[512]{0:T(512)S(1)} %bitcast.16), channel_id=1, source_target_pairs={{96,0},{33,1},{98,2},{35,3},{100,4},{37,5},{102,6},{39,7},{104,8},... | collective-permute-start | bytes 6152 | tf_op jit(solution)/shard_map/ppermute | solution.py:168
  50.4 0.3 collective-permute-start.16
  50.7 4.6 %collective-permute-start.12 = (f32[512]{0:T(512)S(1)}, f32[512]{0:T(512)S(1)}, u32[]{:S(2)}, u32[]{:S(2)}) collective-permute-start(f32[512]{0:T(512)S(1)} %bitcast.13), channel_id=1, source_target_pairs={{30,0},{27,1},{24,2},{29,3},{26,4},{31,5},{28,6},{25,7},{6,8},{3,9... | collective-permute-start | bytes 6152 | tf_op jit(solution)/shard_map/ppermute | solution.py:168
  55.3 2.7 %collective-permute-start.13 = (f32[512]{0:T(512)S(1)}, f32[512]{0:T(512)S(1)}, u32[]{:S(2)}, u32[]{:S(2)}) collective-permute-start(f32[512]{0:T(512)S(1)} %bitcast.12), channel_id=1, source_target_pairs={{12,0},{23,1},{14,2},{17,3},{8,4},{19,5},{10,6},{21,7},{20,8},{31,... | collective-permute-start | bytes 6152 | tf_op jit(solution)/shard_map/ppermute | solution.py:168
  58.1 3.3 %collective-permute-done.13 = f32[512]{0:T(512)S(1)} collective-permute-done((f32[512]{0:T(512)S(1)}, f32[512]{0:T(512)S(1)}, u32[]{:S(2)}, u32[]{:S(2)}) %collective-permute-start.13) | collective-permute-done | bytes 2080 | tf_op jit(solution)/shard_map/ppermute | solution.py:168
  61.4 0.6 collective-permute-done.11
  62.0 3.7 %collective-permute-start.17 = (f32[256]{0:T(256)S(1)}, f32[256]{0:T(256)S(1)}, u32[]{:S(2)}, u32[]{:S(2)}) collective-permute-start(f32[256]{0:T(256)S(1)} %slice.34), channel_id=1, source_target_pairs={{0,1},{1,0},{2,3},{3,2},{4,5},{5,4},{6,7},{7,6},{8,9},{9,8},{10,11... | collective-permute-start | bytes 3080 | tf_op jit(solution)/shard_map/ppermute | solution.py:174
  65.8 0.8 %collective-permute-done.17 = f32[256]{0:T(256)S(1)} collective-permute-done((f32[256]{0:T(256)S(1)}, f32[256]{0:T(256)S(1)}, u32[]{:S(2)}, u32[]{:S(2)}) %collective-permute-start.17) | collective-permute-done | bytes 1056 | tf_op jit(solution)/shard_map/ppermute | solution.py:174
  66.6 0.6 slice_maximum_fusion
  (20 shorter events, 0.1 us)
Async XLA Ops:
  0.0 1.4 %copy-start.1 = (s32[256]{0:T(256)S(1)}, s32[256]{0:T(256)}, u32[]{:S(2)}) copy-start(s32[256]{0:T(256)} %param.3) | copy-start | bytes 3076
  0.0 3.0 %collective-permute-start = (bf16[256,768]{1,0:T(8,128)(2,1)}, bf16[256,768]{1,0:T(8,128)(2,1)S(1)}, u32[]{:S(2)}, u32[]{:S(2)}) collective-permute-start(bf16[256,768]{1,0:T(8,128)(2,1)} %rows_ref.1), channel_id=1, source_target_pairs={{0,1},{1,0},{2,3},{3,2},{4,5},{5,4},{6,7},{7,6},{8,9},{9,8},{10,11... | collective-permute-start | bytes 1179656 | tf_op jit(solution)/shard_map/ppermute | solution.py:174
  1.4 1.6 %collective-permute-start.1 = (s32[256]{0:T(256)}, s32[256]{0:T(256)S(1)}, u32[]{:S(2)}, u32[]{:S(2)}) collective-permute-start(s32[256]{0:T(256)} %param.3), channel_id=1, source_target_pairs={{0,1},{1,0},{2,3},{3,2},{4,5},{5,4},{6,7},{7,6},{8,9},{9,8},{10,11... | collective-permute-start | bytes 3080 | tf_op jit(solution)/shard_map/ppermute | solution.py:174
  1.4 1.0 %copy-start = (bf16[256,768]{1,0:T(8,128)(2,1)S(1)}, bf16[256,768]{1,0:T(8,128)(2,1)}, u32[]{:S(2)}) copy-start(bf16[256,768]{1,0:T(8,128)(2,1)} %rows_ref.1) | copy-start | bytes 1179652
  3.2 13.2 %collective-permute-start.2 = (bf16[528,768]{1,0:T(8,128)(2,1)S(1)}, bf16[528,768]{1,0:T(8,128)(2,1)S(1)}, u32[]{:S(2)}, u32[]{:S(2)}) collective-permute-start(bf16[528,768]{1,0:T(8,128)(2,1)S(1)} %chip.1.refs_0_), channel_id=1, source_target_pairs={{32,0},{97,1},{34,2},{99,3},{36,4},{101,5},{38,6},{103,7},{40,8},{... | collective-permute-start | bytes 2433032 | tf_op jit(solution)/shard_map/ppermute | solution.py:168
  4.6 20.8 %collective-permute-start.6 = (bf16[528,768]{1,0:T(8,128)(2,1)S(1)}, bf16[528,768]{1,0:T(8,128)(2,1)S(1)}, u32[]{:S(2)}, u32[]{:S(2)}) collective-permute-start(bf16[528,768]{1,0:T(8,128)(2,1)S(1)} %chip.1.refs_0_), channel_id=1, source_target_pairs={{4,0},{17,1},{6,2},{19,3},{0,4},{21,5},{2,6},{23,7},{12,8},{25,9},... | collective-permute-start | bytes 2433032 | tf_op jit(solution)/shard_map/ppermute | solution.py:168
  8.2 19.7 %collective-permute-start.8 = (bf16[528,768]{1,0:T(8,128)(2,1)S(1)}, bf16[528,768]{1,0:T(8,128)(2,1)S(1)}, u32[]{:S(2)}, u32[]{:S(2)}) collective-permute-start(bf16[528,768]{1,0:T(8,128)(2,1)S(1)} %chip.1.refs_0_), channel_id=1, source_target_pairs={{2,0},{9,1},{4,2},{11,3},{6,4},{13,5},{0,6},{15,7},{10,8},{17,9},{... | collective-permute-start | bytes 2433032 | tf_op jit(solution)/shard_map/ppermute | solution.py:168
  8.7 19.3 %collective-permute-start.4 = (bf16[272,768]{1,0:T(8,128)(2,1)S(1)}, bf16[272,768]{1,0:T(8,128)(2,1)S(1)}, u32[]{:S(2)}, u32[]{:S(2)}) collective-permute-start(bf16[272,768]{1,0:T(8,128)(2,1)S(1)} %own.1.half_ref), channel_id=1, source_target_pairs={{64,0},{65,1},{66,2},{67,3},{68,4},{69,5},{70,6},{71,7},{72,8},{73... | collective-permute-start | bytes 1253384 | tf_op jit(solution)/shard_map/ppermute | solution.py:168
  16.4 15.0 %collective-permute-start.3 = (bf16[528,768]{1,0:T(8,128)(2,1)S(1)}, bf16[528,768]{1,0:T(8,128)(2,1)S(1)}, u32[]{:S(2)}, u32[]{:S(2)}) collective-permute-start(bf16[528,768]{1,0:T(8,128)(2,1)S(1)} %collective-permute-done.2.refs_1_), channel_id=1, source_target_pairs={{0,1},{1,0},{2,3},{3,2},{4,5},{5,4},{6,7},{7,6},{8,9},{9,8},{10,11... | collective-permute-start | bytes 2433032 | tf_op jit(solution)/shard_map/ppermute | solution.py:174
  25.5 16.2 %collective-permute-start.10 = (bf16[528,768]{1,0:T(8,128)(2,1)S(1)}, bf16[528,768]{1,0:T(8,128)(2,1)S(1)}, u32[]{:S(2)}, u32[]{:S(2)}) collective-permute-start(bf16[528,768]{1,0:T(8,128)(2,1)S(1)} %collective-permute-done.6.refs_6_), channel_id=1, source_target_pairs={{24,0},{3,1},{26,2},{5,3},{28,4},{7,5},{30,6},{1,7},{0,8},{11,9},{... | collective-permute-start | bytes 2433032 | tf_op jit(solution)/shard_map/ppermute | solution.py:168
  27.9 3.5 %collective-permute-start.5 = (bf16[272,768]{1,0:T(8,128)(2,1)S(1)}, bf16[272,768]{1,0:T(8,128)(2,1)S(1)}, u32[]{:S(2)}, u32[]{:S(2)}) collective-permute-start(bf16[272,768]{1,0:T(8,128)(2,1)S(1)} %collective-permute-done.4.refs_3_), channel_id=1, source_target_pairs={{0,1},{1,0},{2,3},{3,2},{4,5},{5,4},{6,7},{7,6},{8,9},{9,8},{10,11... | collective-permute-start | bytes 1253384 | tf_op jit(solution)/shard_map/ppermute | solution.py:174
  27.9 15.6 %collective-permute-start.9 = (bf16[528,768]{1,0:T(8,128)(2,1)S(1)}, bf16[528,768]{1,0:T(8,128)(2,1)S(1)}, u32[]{:S(2)}, u32[]{:S(2)}) collective-permute-start(bf16[528,768]{1,0:T(8,128)(2,1)S(1)} %collective-permute-done.8.refs_5_), channel_id=1, source_target_pairs={{8,0},{7,1},{10,2},{1,3},{12,4},{3,5},{14,6},{5,7},{16,8},{15,9},{... | collective-permute-start | bytes 2433032 | tf_op jit(solution)/shard_map/ppermute | solution.py:168
  28.9 16.6 %collective-permute-start.7 = (bf16[272,768]{1,0:T(8,128)(2,1)S(1)}, bf16[272,768]{1,0:T(8,128)(2,1)S(1)}, u32[]{:S(2)}, u32[]{:S(2)}) collective-permute-start(bf16[272,768]{1,0:T(8,128)(2,1)S(1)} %slice.35), channel_id=1, source_target_pairs={{16,0},{5,1},{18,2},{7,3},{20,4},{1,5},{22,6},{3,7},{24,8},{13,9},... | collective-permute-start | bytes 1253384 | tf_op jit(solution)/shard_map/ppermute | solution.py:168
  46.7 11.4 %collective-permute-start.14 = (f32[512]{0:T(512)S(1)}, f32[512]{0:T(512)S(1)}, u32[]{:S(2)}, u32[]{:S(2)}) collective-permute-start(f32[512]{0:T(512)S(1)} %bitcast.17), channel_id=1, source_target_pairs={{64,0},{65,1},{66,2},{67,3},{68,4},{69,5},{70,6},{71,7},{72,8},{73... | collective-permute-start | bytes 6152 | tf_op jit(solution)/shard_map/ppermute | solution.py:168
  49.0 9.1 %collective-permute-start.15 = (f32[512]{0:T(512)S(1)}, f32[512]{0:T(512)S(1)}, u32[]{:S(2)}, u32[]{:S(2)}) collective-permute-start(f32[512]{0:T(512)S(1)} %bitcast.16), channel_id=1, source_target_pairs={{96,0},{33,1},{98,2},{35,3},{100,4},{37,5},{102,6},{39,7},{104,8},... | collective-permute-start | bytes 6152 | tf_op jit(solution)/shard_map/ppermute | solution.py:168
  50.4 7.7 %collective-permute-start.16 = (f32[512]{0:T(512)S(1)}, f32[512]{0:T(512)S(1)}, u32[]{:S(2)}, u32[]{:S(2)}) collective-permute-start(f32[512]{0:T(512)S(1)} %bitcast.15), channel_id=1, source_target_pairs={{32,0},{97,1},{34,2},{99,3},{36,4},{101,5},{38,6},{103,7},{40,8},{... | collective-permute-start | bytes 6152 | tf_op jit(solution)/shard_map/ppermute | solution.py:168
  50.7 7.4 %collective-permute-start.12 = (f32[512]{0:T(512)S(1)}, f32[512]{0:T(512)S(1)}, u32[]{:S(2)}, u32[]{:S(2)}) collective-permute-start(f32[512]{0:T(512)S(1)} %bitcast.13), channel_id=1, source_target_pairs={{30,0},{27,1},{24,2},{29,3},{26,4},{31,5},{28,6},{25,7},{6,8},{3,9... | collective-permute-start | bytes 6152 | tf_op jit(solution)/shard_map/ppermute | solution.py:168
  55.3 6.0 %collective-permute-start.13 = (f32[512]{0:T(512)S(1)}, f32[512]{0:T(512)S(1)}, u32[]{:S(2)}, u32[]{:S(2)}) collective-permute-start(f32[512]{0:T(512)S(1)} %bitcast.12), channel_id=1, source_target_pairs={{12,0},{23,1},{14,2},{17,3},{8,4},{19,5},{10,6},{21,7},{20,8},{31,... | collective-permute-start | bytes 6152 | tf_op jit(solution)/shard_map/ppermute | solution.py:168
  58.1 3.9 %collective-permute-start.11 = (f32[512]{0:T(512)S(1)}, f32[512]{0:T(512)S(1)}, u32[]{:S(2)}, u32[]{:S(2)}) collective-permute-start(f32[512]{0:T(512)S(1)} %bitcast.14), channel_id=1, source_target_pairs={{6,0},{25,1},{0,2},{27,3},{2,4},{29,5},{4,6},{31,7},{14,8},{1,9},{... | collective-permute-start | bytes 6152 | tf_op jit(solution)/shard_map/ppermute | solution.py:168
  62.0 4.6 %collective-permute-start.17 = (f32[256]{0:T(256)S(1)}, f32[256]{0:T(256)S(1)}, u32[]{:S(2)}, u32[]{:S(2)}) collective-permute-start(f32[256]{0:T(256)S(1)} %slice.34), channel_id=1, source_target_pairs={{0,1},{1,0},{2,3},{3,2},{4,5},{5,4},{6,7},{7,6},{8,9},{9,8},{10,11... | collective-permute-start | bytes 3080 | tf_op jit(solution)/shard_map/ppermute | solution.py:174

commit v4 on v3

--- a/solution.py
+++ b/solution.py
@@ -178,28 +178,35 @@
     half = call(own_kernel, "own", HALF, width, embeddings, ids)
     block = call(chip_kernel, "chip", BLOCK, width, half, swap(embeddings), swap(cluster_id).reshape(1, ROWS))
 
+    after = lax.optimization_barrier
+
     key1 = fetch(block, (0, 0, 1), (0, 1, 0))
     key2 = fetch(block, (0, 0, 2), (0, 2, 0))
     near = fetch(block, (1, 0, 0), (-1, 0, 0))
-    far = fetch(half, (2, 0, 0), (2, 0, 0))
-    key3 = fetch(key1, (0, 1, 0), (0, 0, -1))
-    key4 = fetch(key2, (0, -1, 0), (0, 0, 1))
+    key4 = fetch(key2, (0, -1, 0), (0, 0, -1))
+    key3 = fetch(key1, (0, -1, 0), (0, 0, 1))
+    far = fetch(near, (1, 0, 0), (-1, 0, 0))
     key5 = fetch(key2[:HALF], (0, 2, 0), (0, 0, 2))
 
-    groups = [[(block, (OWN, OTHER))], [whole(near), (swap(near), (OTHER, OWN)), whole(far), whole(swap(far))]]
     keys = [(block, (OWN,)), whole(key1), whole(key2)]
-    states, top1 = score(groups, keys, collect=1, own_key=True)
+    first = [(block, (OWN, OTHER)), whole(near), (swap(near), (OTHER, OWN))]
+    (state,), top = score([first], keys, collect=1, own_key=True)
+    far, state = after((far, state))
+    second = [whole(far)]
+    (state2,), top2 = score([second], keys, collect=1)
+    groups, states = [first, second], [state, state2]
+    home1 = give(jnp.maximum(top, top2)[: 2 * ROWS], (0, 0, 1), (0, 1, 0))
     states, top4 = score(groups, [whole(key4)], states, collect=0)
+    home4 = give(top4, (0, -1, 2), (0, 2, -1))
     states, top3 = score(groups, [whole(key3)], states, collect=0)
+    home3 = give(top3, (0, -1, 1), (0, 1, 1))
+    key5, home1, home4 = after((key5, home1, home4))
     (best, best2), _ = score(groups, [whole(key5)], states, last=True)
-    best, best2 = best[0].reshape(1, 2 * ROWS), best2[0].reshape(3, 2 * ROWS)
-    best, best2 = [best[0], best2[0], best2[1]], best2[2]
-    homes = [give(top1[: 2 * ROWS], (0, 0, 1), (0, 1, 0)), give(top3, (0, 1, 1), (0, 1, -1)), give(top4, (0, -1, 2), (0, 2, 1))]
-
+    best, best2 = best[0].reshape(3, 2 * ROWS), best2[0][0]
     from_far = give(best2, (2, 0, 0), (2, 0, 0))
     from_up = give(best[1], (1, 0, 0), (-1, 0, 0))
     from_down = give(best[2], (-1, 0, 0), (1, 0, 0))
-    home = functools.reduce(jnp.maximum, [best[0], *homes, from_far, from_up, from_down])
+    home = functools.reduce(jnp.maximum, [best[0], home1, home4, home3, from_far, from_up, from_down])
     return jnp.maximum(home[:ROWS], swap(home[ROWS:]))
 
 

time: 67.3 us -> 59.8 us (0.89)
  starting transfers between devices: 39.7 us -> 24.8 us
  waiting for transfers between devices: 16 us -> 23.1 us
    ppermute x5 -> x4, starting transfers between devices: 14.2 us -> 6.44 us  [swap(): lax.ppermute(value, AXES, [(i, i ^ 1) for i in range(ny * nz * nx * 2)])]
    ppermute x13, waiting for transfers between devices: 14.8 us -> 21.9 us  [fetch(): return lax.ppermute(value, AXES, pairs)]
    ppermute x13, starting transfers between devices: 25.4 us -> 18.4 us  [fetch(): return lax.ppermute(value, AXES, pairs)]
    pallas_call x4 -> x5, Pallas kernels: 9.42 us -> 9.54 us  [score(): pl.pallas_call(functools.partial(score_kernel, listed_groups, key_parts,...]
  transfers between devices with their start and end apart: 18 -> 17, of which waited for: 6 -> 8; matrix products, arithmetic and copies ran while one was open for 0% -> 0% of each run, Pallas kernels for 12% -> 16%
where the time goes in v4:
time: 59.8 us; the launch traced here: 59.6 us
  starting transfers between devices  24.8 us (41%)
  waiting for transfers between devices  23.1 us (39%)
  Pallas kernels  9.9 us (17%)
  local copies, waits for them, and re-layouts  1.04 us (2%)
    ppermute x13, waiting for transfers between devices, fetch(): return lax.ppermute(value, AXES, pairs)  21.9 us
    ppermute x13, starting transfers between devices, fetch(): return lax.ppermute(value, AXES, pairs)  18.4 us
    pallas_call x5, Pallas kernels, score(): pl.pallas_call(functools.partial(score_kernel, listed_groups, key_parts,...  9.54 us
    ppermute x4, starting transfers between devices, swap(): lax.ppermute(value, AXES, [(i, i ^ 1) for i in range(ny * nz * nx * 2)])  6.44 us
    ppermute x4, waiting for transfers between devices, swap(): lax.ppermute(value, AXES, [(i, i ^ 1) for i in range(ny * nz * nx * 2)])  1.2 us
  transfers between devices with their start and end apart: 17, of which 8 were waited for; matrix products, arithmetic and copies ran while one was open for 0% of the time, Pallas kernels for 16%

profile of v4, /device:TPU:1, one launch (start us, length us, event | category | flops | bytes accessed | tf_op | source)
XLA Modules:
  0.0 59.6 jit_solution(7420214351966045701)
XLA Ops:
  0.0 1.4 %collective-permute-start = (bf16[256,768]{1,0:T(8,128)(2,1)}, bf16[256,768]{1,0:T(8,128)(2,1)S(1)}, u32[]{:S(2)}, u32[]{:S(2)}) collective-permute-start(bf16[256,768]{1,0:T(8,128)(2,1)} %rows_ref.1), channel_id=1, source_target_pairs={{0,1},{1,0},{2,3},{3,2},{4,5},{5,4},{6,7},{7,6},{8,9},{9,8},{10,11... | collective-permute-start | bytes 1179656 | tf_op jit(solution)/shard_map/ppermute | solution.py:174
  1.4 1.0 %copy-done = bf16[256,768]{1,0:T(8,128)(2,1)S(1)} copy-done((bf16[256,768]{1,0:T(8,128)(2,1)S(1)}, bf16[256,768]{1,0:T(8,128)(2,1)}, u32[]{:S(2)}) %copy-start) | copy-done | bytes 393240
  2.4 0.2 own.1.half_ref
  2.6 0.4 collective-permute-done.1
  3.0 0.2 chip.1.refs_0_.refs_1_
  3.2 1.4 %collective-permute-start.2 = (bf16[528,768]{1,0:T(8,128)(2,1)S(1)}, bf16[528,768]{1,0:T(8,128)(2,1)S(1)}, u32[]{:S(2)}, u32[]{:S(2)}) collective-permute-start(bf16[528,768]{1,0:T(8,128)(2,1)S(1)} %chip.1.refs_0_.refs_1_), channel_id=1, source_target_pairs={{32,0},{97,1},{34,2},{99,3},{36,4},{101,5},{38,6},{103,7},{40,8},{... | collective-permute-start | bytes 2433032 | tf_op jit(solution)/shard_map/ppermute | solution.py:168
  4.6 3.6 %collective-permute-start.6 = (bf16[528,768]{1,0:T(8,128)(2,1)S(1)}, bf16[528,768]{1,0:T(8,128)(2,1)S(1)}, u32[]{:S(2)}, u32[]{:S(2)}) collective-permute-start(bf16[528,768]{1,0:T(8,128)(2,1)S(1)} %chip.1.refs_0_.refs_1_), channel_id=1, source_target_pairs={{4,0},{17,1},{6,2},{19,3},{0,4},{21,5},{2,6},{23,7},{12,8},{25,9},... | collective-permute-start | bytes 2433032 | tf_op jit(solution)/shard_map/ppermute | solution.py:168
  8.2 0.4 collective-permute-start.5
  8.7 7.3 %collective-permute-done.2.refs_1_ = bf16[528,768]{1,0:T(8,128)(2,1)S(1)} collective-permute-done((bf16[528,768]{1,0:T(8,128)(2,1)S(1)}, bf16[528,768]{1,0:T(8,128)(2,1)S(1)}, u32[]{:S(2)}, u32[]{:S(2)}) %collective-permute-start.2) | collective-permute-done | bytes 811040 | tf_op jit(solution)/shard_map/ppermute | solution.py:168
  16.0 0.5 collective-permute-start.3
  16.5 0.8 %collective-permute-start.4 = (bf16[528,768]{1,0:T(8,128)(2,1)S(1)}, bf16[528,768]{1,0:T(8,128)(2,1)S(1)}, u32[]{:S(2)}, u32[]{:S(2)}) collective-permute-start(bf16[528,768]{1,0:T(8,128)(2,1)S(1)} %collective-permute-done.2.refs_1_), channel_id=1, source_target_pairs={{32,0},{97,1},{34,2},{99,3},{36,4},{101,5},{38,6},{103,7},{40,8},{... | collective-permute-start | bytes 2433032 | tf_op jit(solution)/shard_map/ppermute | solution.py:168
  17.3 0.9 %collective-permute-done.6.refs_4_.refs_3_ = bf16[528,768]{1,0:T(8,128)(2,1)S(1)} collective-permute-done((bf16[528,768]{1,0:T(8,128)(2,1)S(1)}, bf16[528,768]{1,0:T(8,128)(2,1)S(1)}, u32[]{:S(2)}, u32[]{:S(2)}) %collective-permute-start.6) | collective-permute-done | bytes 811040 | tf_op jit(solution)/shard_map/ppermute | solution.py:168
  18.2 0.9 %collective-permute-start.9 = (bf16[528,768]{1,0:T(8,128)(2,1)S(1)}, bf16[528,768]{1,0:T(8,128)(2,1)S(1)}, u32[]{:S(2)}, u32[]{:S(2)}) collective-permute-start(bf16[528,768]{1,0:T(8,128)(2,1)S(1)} %collective-permute-done.6.refs_4_.refs_3_), channel_id=1, source_target_pairs={{24,0},{7,1},{26,2},{1,3},{28,4},{3,5},{30,6},{5,7},{0,8},{15,9},{... | collective-permute-start | bytes 2433032 | tf_op jit(solution)/shard_map/ppermute | solution.py:168
  19.1 8.6 %collective-permute-done.5.refs_3_.refs_2_ = bf16[528,768]{1,0:T(8,128)(2,1)S(1)} collective-permute-done((bf16[528,768]{1,0:T(8,128)(2,1)S(1)}, bf16[528,768]{1,0:T(8,128)(2,1)S(1)}, u32[]{:S(2)}, u32[]{:S(2)}) %collective-permute-start.5) | collective-permute-done | bytes 811040 | tf_op jit(solution)/shard_map/ppermute | solution.py:168
  27.6 2.5 %collective-permute-start.11 = (bf16[528,768]{1,0:T(8,128)(2,1)S(1)}, bf16[528,768]{1,0:T(8,128)(2,1)S(1)}, u32[]{:S(2)}, u32[]{:S(2)}) collective-permute-start(bf16[528,768]{1,0:T(8,128)(2,1)S(1)} %collective-permute-done.5.refs_3_.refs_2_), channel_id=1, source_target_pairs={{24,0},{3,1},{26,2},{5,3},{28,4},{7,5},{30,6},{1,7},{0,8},{11,9},{... | collective-permute-start | bytes 2433032 | tf_op jit(solution)/shard_map/ppermute | solution.py:168
  30.1 0.6 %collective-permute-start.7 = (bf16[272,768]{1,0:T(8,128)(2,1)S(1)}, bf16[272,768]{1,0:T(8,128)(2,1)S(1)}, u32[]{:S(2)}, u32[]{:S(2)}) collective-permute-start(bf16[272,768]{1,0:T(8,128)(2,1)S(1)} %slice.35), channel_id=1, source_target_pairs={{16,0},{5,1},{18,2},{7,3},{20,4},{1,5},{22,6},{3,7},{24,8},{13,9},... | collective-permute-start | bytes 1253384 | tf_op jit(solution)/shard_map/ppermute | solution.py:168
  30.8 3.3 %score.5 = (f32[1536,128]{1,0:T(8,128)S(1)}, f32[1536,128]{1,0:T(8,128)S(1)}, f32[1,1024]{1,0:T(1,128)S(1)}) custom-call(bf16[528,768]{1,0:T(8,128)(2,1)S(1)} %chip.1.refs_0_.refs_1_, bf16[528,768]{1,0:T(8,128)(2,1)S(1)} %collective-permute-done.2.refs_1_, bf16[528,768]{1,0:T(8,128)(2,1)S(1)} %collective-permute-done.3.refs_2_, ...), custom_call_target="tpu_custom_call" | custom-call | flops 3019898880 | bytes 4325376 | tf_op jit(solution)/shard_map/score/pallas_call | solution.py:137
  34.1 1.2 %score.6 = (f32[512,128]{1,0:T(8,128)S(1)}, f32[512,128]{1,0:T(8,128)S(1)}, f32[1,1024]{1,0:T(1,128)S(1)}) custom-call(bf16[528,768]{1,0:T(8,128)(2,1)S(1)} %collective-permute-done.4.refs_0_.refs_3_, bf16[528,768]{1,0:T(8,128)(2,1)S(1)} %chip.1.refs_0_.refs_1_, bf16[528,768]{1,0:T(8,128)(2,1)S(1)} %collective-permute-done.5.refs_3_.refs_2_, ...), custom_call_target="tpu_custom_call" | custom-call | flops 1006632960 | bytes 2752512 | tf_op jit(solution)/shard_map/score/pallas_call | solution.py:137
  35.4 0.3 collective-permute-start.8
  35.7 1.9 %score.7 = (f32[1536,128]{1,0:T(8,128)S(1)}, f32[512,128]{1,0:T(8,128)S(1)}, f32[1,512]{1,0:T(1,128)S(1)}) custom-call(bf16[528,768]{1,0:T(8,128)(2,1)S(1)} %chip.1.refs_0_.refs_1_, bf16[528,768]{1,0:T(8,128)(2,1)S(1)} %collective-permute-done.2.refs_1_, bf16[528,768]{1,0:T(8,128)(2,1)S(1)} %collective-permute-done.3.refs_2_, ...), custom_call_target="tpu_custom_call" | custom-call | flops 1610612736 | bytes 3932160 | tf_op jit(solution)/shard_map/score/pallas_call | solution.py:137
  37.6 3.6 %collective-permute-start.10 = (f32[512]{0:T(512)S(1)}, f32[512]{0:T(512)S(1)}, u32[]{:S(2)}, u32[]{:S(2)}) collective-permute-start(f32[512]{0:T(512)S(1)} %bitcast.13), channel_id=1, source_target_pairs={{12,0},{19,1},{14,2},{21,3},{8,4},{23,5},{10,6},{17,7},{20,8},{27,... | collective-permute-start | bytes 6152 | tf_op jit(solution)/shard_map/ppermute | solution.py:168
  41.2 2.6 %collective-permute-done.11.refs_4_ = bf16[528,768]{1,0:T(8,128)(2,1)S(1)} collective-permute-done((bf16[528,768]{1,0:T(8,128)(2,1)S(1)}, bf16[528,768]{1,0:T(8,128)(2,1)S(1)}, u32[]{:S(2)}, u32[]{:S(2)}) %collective-permute-start.11) | collective-permute-done | bytes 811040 | tf_op jit(solution)/shard_map/ppermute | solution.py:168
  43.8 1.9 %score.8 = (f32[1536,128]{1,0:T(8,128)S(1)}, f32[512,128]{1,0:T(8,128)S(1)}, f32[1,512]{1,0:T(1,128)S(1)}) custom-call(bf16[528,768]{1,0:T(8,128)(2,1)S(1)} %chip.1.refs_0_.refs_1_, bf16[528,768]{1,0:T(8,128)(2,1)S(1)} %collective-permute-done.2.refs_1_, bf16[528,768]{1,0:T(8,128)(2,1)S(1)} %collective-permute-done.3.refs_2_, ...), custom_call_target="tpu_custom_call" | custom-call | flops 1610612736 | bytes 3932160 | tf_op jit(solution)/shard_map/score/pallas_call | solution.py:137
  45.8 1.2 %score.9 = (f32[1,1536]{1,0:T(1,128)S(1)}, f32[1,512]{1,0:T(1,128)S(1)}) custom-call(bf16[528,768]{1,0:T(8,128)(2,1)S(1)} %chip.1.refs_0_.refs_1_, bf16[528,768]{1,0:T(8,128)(2,1)S(1)} %collective-permute-done.2.refs_1_, bf16[528,768]{1,0:T(8,128)(2,1)S(1)} %collective-permute-done.3.refs_2_, bf16[528,768]{1,0:T(8,128)(2,1)S(1)} %collective-permute-done.4.refs_0_.refs_3_, ...), custom_call_target="tpu_custom_call" | custom-call | flops 805306368 | bytes 3538944 | tf_op jit(solution)/shard_map/score/pallas_call | solution.py:137
  47.0 1.4 %collective-permute-start.15 = (f32[512]{0:T(512)S(1)}, f32[512]{0:T(512)S(1)}, u32[]{:S(2)}, u32[]{:S(2)}) collective-permute-start(f32[512]{0:T(512)S(1)} %bitcast.17), channel_id=1, source_target_pairs={{32,0},{97,1},{34,2},{99,3},{36,4},{101,5},{38,6},{103,7},{40,8},{... | collective-permute-start | bytes 6152 | tf_op jit(solution)/shard_map/ppermute | solution.py:168
  48.4 1.4 %collective-permute-start.14 = (f32[512]{0:T(512)S(1)}, f32[512]{0:T(512)S(1)}, u32[]{:S(2)}, u32[]{:S(2)}) collective-permute-start(f32[512]{0:T(512)S(1)} %bitcast.16), channel_id=1, source_target_pairs={{96,0},{33,1},{98,2},{35,3},{100,4},{37,5},{102,6},{39,7},{104,8},... | collective-permute-start | bytes 6152 | tf_op jit(solution)/shard_map/ppermute | solution.py:168
  49.7 1.4 %collective-permute-start.13 = (f32[512]{0:T(512)S(1)}, f32[512]{0:T(512)S(1)}, u32[]{:S(2)}, u32[]{:S(2)}) collective-permute-start(f32[512]{0:T(512)S(1)} %bitcast.12), channel_id=1, source_target_pairs={{64,0},{65,1},{66,2},{67,3},{68,4},{69,5},{70,6},{71,7},{72,8},{73... | collective-permute-start | bytes 6152 | tf_op jit(solution)/shard_map/ppermute | solution.py:168
  51.2 0.8 %collective-permute-done.12 = f32[512]{0:T(512)S(1)} collective-permute-done((f32[512]{0:T(512)S(1)}, f32[512]{0:T(512)S(1)}, u32[]{:S(2)}, u32[]{:S(2)}) %collective-permute-start.12) | collective-permute-done | bytes 2080 | tf_op jit(solution)/shard_map/ppermute | solution.py:168
  51.9 1.8 %collective-permute-done.13 = f32[512]{0:T(512)S(1)} collective-permute-done((f32[512]{0:T(512)S(1)}, f32[512]{0:T(512)S(1)}, u32[]{:S(2)}, u32[]{:S(2)}) %collective-permute-start.13) | collective-permute-done | bytes 2080 | tf_op jit(solution)/shard_map/ppermute | solution.py:168
  53.7 4.5 %collective-permute-start.16 = (f32[256]{0:T(256)S(1)}, f32[256]{0:T(256)S(1)}, u32[]{:S(2)}, u32[]{:S(2)}) collective-permute-start(f32[256]{0:T(256)S(1)} %slice.34), channel_id=1, source_target_pairs={{0,1},{1,0},{2,3},{3,2},{4,5},{5,4},{6,7},{7,6},{8,9},{9,8},{10,11... | collective-permute-start | bytes 3080 | tf_op jit(solution)/shard_map/ppermute | solution.py:174
  58.2 0.8 %collective-permute-done.16 = f32[256]{0:T(256)S(1)} collective-permute-done((f32[256]{0:T(256)S(1)}, f32[256]{0:T(256)S(1)}, u32[]{:S(2)}, u32[]{:S(2)}) %collective-permute-start.16) | collective-permute-done | bytes 1056 | tf_op jit(solution)/shard_map/ppermute | solution.py:174
  59.1 0.6 slice_maximum_fusion.1
  (19 shorter events, 0.2 us)
Async XLA Ops:
  0.0 1.4 %copy-start.1 = (s32[256]{0:T(256)S(1)}, s32[256]{0:T(256)}, u32[]{:S(2)}) copy-start(s32[256]{0:T(256)} %param.3) | copy-start | bytes 3076
  0.0 3.0 %collective-permute-start = (bf16[256,768]{1,0:T(8,128)(2,1)}, bf16[256,768]{1,0:T(8,128)(2,1)S(1)}, u32[]{:S(2)}, u32[]{:S(2)}) collective-permute-start(bf16[256,768]{1,0:T(8,128)(2,1)} %rows_ref.1), channel_id=1, source_target_pairs={{0,1},{1,0},{2,3},{3,2},{4,5},{5,4},{6,7},{7,6},{8,9},{9,8},{10,11... | collective-permute-start | bytes 1179656 | tf_op jit(solution)/shard_map/ppermute | solution.py:174
  1.4 1.6 %collective-permute-start.1 = (s32[256]{0:T(256)}, s32[256]{0:T(256)S(1)}, u32[]{:S(2)}, u32[]{:S(2)}) collective-permute-start(s32[256]{0:T(256)} %param.3), channel_id=1, source_target_pairs={{0,1},{1,0},{2,3},{3,2},{4,5},{5,4},{6,7},{7,6},{8,9},{9,8},{10,11... | collective-permute-start | bytes 3080 | tf_op jit(solution)/shard_map/ppermute | solution.py:174
  1.4 1.0 %copy-start = (bf16[256,768]{1,0:T(8,128)(2,1)S(1)}, bf16[256,768]{1,0:T(8,128)(2,1)}, u32[]{:S(2)}) copy-start(bf16[256,768]{1,0:T(8,128)(2,1)} %rows_ref.1) | copy-start | bytes 1179652
  3.2 12.8 %collective-permute-start.2 = (bf16[528,768]{1,0:T(8,128)(2,1)S(1)}, bf16[528,768]{1,0:T(8,128)(2,1)S(1)}, u32[]{:S(2)}, u32[]{:S(2)}) collective-permute-start(bf16[528,768]{1,0:T(8,128)(2,1)S(1)} %chip.1.refs_0_.refs_1_), channel_id=1, source_target_pairs={{32,0},{97,1},{34,2},{99,3},{36,4},{101,5},{38,6},{103,7},{40,8},{... | collective-permute-start | bytes 2433032 | tf_op jit(solution)/shard_map/ppermute | solution.py:168
  4.6 13.5 %collective-permute-start.6 = (bf16[528,768]{1,0:T(8,128)(2,1)S(1)}, bf16[528,768]{1,0:T(8,128)(2,1)S(1)}, u32[]{:S(2)}, u32[]{:S(2)}) collective-permute-start(bf16[528,768]{1,0:T(8,128)(2,1)S(1)} %chip.1.refs_0_.refs_1_), channel_id=1, source_target_pairs={{4,0},{17,1},{6,2},{19,3},{0,4},{21,5},{2,6},{23,7},{12,8},{25,9},... | collective-permute-start | bytes 2433032 | tf_op jit(solution)/shard_map/ppermute | solution.py:168
  8.2 19.4 %collective-permute-start.5 = (bf16[528,768]{1,0:T(8,128)(2,1)S(1)}, bf16[528,768]{1,0:T(8,128)(2,1)S(1)}, u32[]{:S(2)}, u32[]{:S(2)}) collective-permute-start(bf16[528,768]{1,0:T(8,128)(2,1)S(1)} %chip.1.refs_0_.refs_1_), channel_id=1, source_target_pairs={{2,0},{9,1},{4,2},{11,3},{6,4},{13,5},{0,6},{15,7},{10,8},{17,9},{... | collective-permute-start | bytes 2433032 | tf_op jit(solution)/shard_map/ppermute | solution.py:168
  16.0 14.7 %collective-permute-start.3 = (bf16[528,768]{1,0:T(8,128)(2,1)S(1)}, bf16[528,768]{1,0:T(8,128)(2,1)S(1)}, u32[]{:S(2)}, u32[]{:S(2)}) collective-permute-start(bf16[528,768]{1,0:T(8,128)(2,1)S(1)} %collective-permute-done.2.refs_1_), channel_id=1, source_target_pairs={{0,1},{1,0},{2,3},{3,2},{4,5},{5,4},{6,7},{7,6},{8,9},{9,8},{10,11... | collective-permute-start | bytes 2433032 | tf_op jit(solution)/shard_map/ppermute | solution.py:174
  16.5 17.6 %collective-permute-start.4 = (bf16[528,768]{1,0:T(8,128)(2,1)S(1)}, bf16[528,768]{1,0:T(8,128)(2,1)S(1)}, u32[]{:S(2)}, u32[]{:S(2)}) collective-permute-start(bf16[528,768]{1,0:T(8,128)(2,1)S(1)} %collective-permute-done.2.refs_1_), channel_id=1, source_target_pairs={{32,0},{97,1},{34,2},{99,3},{36,4},{101,5},{38,6},{103,7},{40,8},{... | collective-permute-start | bytes 2433032 | tf_op jit(solution)/shard_map/ppermute | solution.py:168
  18.2 17.5 %collective-permute-start.9 = (bf16[528,768]{1,0:T(8,128)(2,1)S(1)}, bf16[528,768]{1,0:T(8,128)(2,1)S(1)}, u32[]{:S(2)}, u32[]{:S(2)}) collective-permute-start(bf16[528,768]{1,0:T(8,128)(2,1)S(1)} %collective-permute-done.6.refs_4_.refs_3_), channel_id=1, source_target_pairs={{24,0},{7,1},{26,2},{1,3},{28,4},{3,5},{30,6},{5,7},{0,8},{15,9},{... | collective-permute-start | bytes 2433032 | tf_op jit(solution)/shard_map/ppermute | solution.py:168
  27.6 16.2 %collective-permute-start.11 = (bf16[528,768]{1,0:T(8,128)(2,1)S(1)}, bf16[528,768]{1,0:T(8,128)(2,1)S(1)}, u32[]{:S(2)}, u32[]{:S(2)}) collective-permute-start(bf16[528,768]{1,0:T(8,128)(2,1)S(1)} %collective-permute-done.5.refs_3_.refs_2_), channel_id=1, source_target_pairs={{24,0},{3,1},{26,2},{5,3},{28,4},{7,5},{30,6},{1,7},{0,8},{11,9},{... | collective-permute-start | bytes 2433032 | tf_op jit(solution)/shard_map/ppermute | solution.py:168
  30.1 15.6 %collective-permute-start.7 = (bf16[272,768]{1,0:T(8,128)(2,1)S(1)}, bf16[272,768]{1,0:T(8,128)(2,1)S(1)}, u32[]{:S(2)}, u32[]{:S(2)}) collective-permute-start(bf16[272,768]{1,0:T(8,128)(2,1)S(1)} %slice.35), channel_id=1, source_target_pairs={{16,0},{5,1},{18,2},{7,3},{20,4},{1,5},{22,6},{3,7},{24,8},{13,9},... | collective-permute-start | bytes 1253384 | tf_op jit(solution)/shard_map/ppermute | solution.py:168
  35.4 10.4 %collective-permute-start.8 = (f32[512]{0:T(512)S(1)}, f32[512]{0:T(512)S(1)}, u32[]{:S(2)}, u32[]{:S(2)}) collective-permute-start(f32[512]{0:T(512)S(1)} %bitcast.15), channel_id=1, source_target_pairs={{6,0},{25,1},{0,2},{27,3},{2,4},{29,5},{4,6},{31,7},{14,8},{1,9},{... | collective-permute-start | bytes 6152 | tf_op jit(solution)/shard_map/ppermute | solution.py:168
  37.6 8.2 %collective-permute-start.10 = (f32[512]{0:T(512)S(1)}, f32[512]{0:T(512)S(1)}, u32[]{:S(2)}, u32[]{:S(2)}) collective-permute-start(f32[512]{0:T(512)S(1)} %bitcast.13), channel_id=1, source_target_pairs={{12,0},{19,1},{14,2},{21,3},{8,4},{23,5},{10,6},{17,7},{20,8},{27,... | collective-permute-start | bytes 6152 | tf_op jit(solution)/shard_map/ppermute | solution.py:168
  45.7 6.2 %collective-permute-start.12 = (f32[512]{0:T(512)S(1)}, f32[512]{0:T(512)S(1)}, u32[]{:S(2)}, u32[]{:S(2)}) collective-permute-start(f32[512]{0:T(512)S(1)} %bitcast.11), channel_id=1, source_target_pairs={{14,0},{31,1},{8,2},{25,3},{10,4},{27,5},{12,6},{29,7},{22,8},{7,9... | collective-permute-start | bytes 6152 | tf_op jit(solution)/shard_map/ppermute | solution.py:168
  47.0 4.9 %collective-permute-start.15 = (f32[512]{0:T(512)S(1)}, f32[512]{0:T(512)S(1)}, u32[]{:S(2)}, u32[]{:S(2)}) collective-permute-start(f32[512]{0:T(512)S(1)} %bitcast.17), channel_id=1, source_target_pairs={{32,0},{97,1},{34,2},{99,3},{36,4},{101,5},{38,6},{103,7},{40,8},{... | collective-permute-start | bytes 6152 | tf_op jit(solution)/shard_map/ppermute | solution.py:168
  48.4 3.6 %collective-permute-start.14 = (f32[512]{0:T(512)S(1)}, f32[512]{0:T(512)S(1)}, u32[]{:S(2)}, u32[]{:S(2)}) collective-permute-start(f32[512]{0:T(512)S(1)} %bitcast.16), channel_id=1, source_target_pairs={{96,0},{33,1},{98,2},{35,3},{100,4},{37,5},{102,6},{39,7},{104,8},... | collective-permute-start | bytes 6152 | tf_op jit(solution)/shard_map/ppermute | solution.py:168
  49.7 3.9 %collective-permute-start.13 = (f32[512]{0:T(512)S(1)}, f32[512]{0:T(512)S(1)}, u32[]{:S(2)}, u32[]{:S(2)}) collective-permute-start(f32[512]{0:T(512)S(1)} %bitcast.12), channel_id=1, source_target_pairs={{64,0},{65,1},{66,2},{67,3},{68,4},{69,5},{70,6},{71,7},{72,8},{73... | collective-permute-start | bytes 6152 | tf_op jit(solution)/shard_map/ppermute | solution.py:168
  53.7 5.4 %collective-permute-start.16 = (f32[256]{0:T(256)S(1)}, f32[256]{0:T(256)S(1)}, u32[]{:S(2)}, u32[]{:S(2)}) collective-permute-start(f32[256]{0:T(256)S(1)} %slice.34), channel_id=1, source_target_pairs={{0,1},{1,0},{2,3},{3,2},{4,5},{5,4},{6,7},{7,6},{8,9},{9,8},{10,11... | collective-permute-start | bytes 3080 | tf_op jit(solution)/shard_map/ppermute | solution.py:174

commit v5 on v4

--- a/solution.py
+++ b/solution.py
@@ -184,26 +184,27 @@
     key2 = fetch(block, (0, 0, 2), (0, 2, 0))
     near = fetch(block, (1, 0, 0), (-1, 0, 0))
     key4 = fetch(key2, (0, -1, 0), (0, 0, -1))
+    far = fetch(near, (1, 0, 0), (-1, 0, 0))
+
+    first = [(block, (OWN, OTHER)), whole(near), (swap(near), (OTHER, OWN))]
+    second = [whole(far)]
+    (state,), _ = score([first], [(block, (OWN,)), whole(key2)], own_key=True)
     key3 = fetch(key1, (0, -1, 0), (0, 0, 1))
-    far = fetch(near, (1, 0, 0), (-1, 0, 0))
-    key5 = fetch(key2[:HALF], (0, 2, 0), (0, 0, 2))
-
-    keys = [(block, (OWN,)), whole(key1), whole(key2)]
-    first = [(block, (OWN, OTHER)), whole(near), (swap(near), (OTHER, OWN))]
-    (state,), top = score([first], keys, collect=1, own_key=True)
+    (state,), top1 = score([first], [whole(key1)], [state], collect=0)
+    key4, state = after((key4, state))
+    key5 = fetch(key4[:HALF], (0, -1, 0), (0, 0, -1))
+    (state,), top4 = score([first], [whole(key4)], [state], collect=0)
     far, state = after((far, state))
-    second = [whole(far)]
-    (state2,), top2 = score([second], keys, collect=1)
-    groups, states = [first, second], [state, state2]
-    home1 = give(jnp.maximum(top, top2)[: 2 * ROWS], (0, 0, 1), (0, 1, 0))
-    states, top4 = score(groups, [whole(key4)], states, collect=0)
-    home4 = give(top4, (0, -1, 2), (0, 2, -1))
-    states, top3 = score(groups, [whole(key3)], states, collect=0)
+    (state2,), tops = score([second], [(block, (OWN,)), whole(key2), whole(key1), whole(key4)], collect=2)
+    home1 = give(jnp.maximum(top1, tops[: 2 * ROWS]), (0, 0, 1), (0, 1, 0))
+    home4 = give(jnp.maximum(top4, tops[2 * ROWS :]), (0, -1, 2), (0, 2, -1))
+    (state, state2), top3 = score([first, second], [whole(key3)], [state, state2], collect=0)
     home3 = give(top3, (0, -1, 1), (0, 1, 1))
-    key5, home1, home4 = after((key5, home1, home4))
-    (best, best2), _ = score(groups, [whole(key5)], states, last=True)
-    best, best2 = best[0].reshape(3, 2 * ROWS), best2[0][0]
-    from_far = give(best2, (2, 0, 0), (2, 0, 0))
+    ((best2, _),), _ = score([second], [whole(key5)], [state2], last=True)
+    ((best, _),), _ = score([first], [whole(key5)], [state], last=True)
+    best = best[0].reshape(3, 2 * ROWS)
+
+    from_far = give(best2[0], (2, 0, 0), (2, 0, 0))
     from_up = give(best[1], (1, 0, 0), (-1, 0, 0))
     from_down = give(best[2], (-1, 0, 0), (1, 0, 0))
     home = functools.reduce(jnp.maximum, [best[0], home1, home4, home3, from_far, from_up, from_down])

time: 59.8 us -> 57.2 us (0.957)
  waiting for transfers between devices: 23.1 us -> 20.7 us
  starting transfers between devices: 24.8 us -> 24.1 us
    ppermute x4, starting transfers between devices: 6.44 us -> 3.61 us  [swap(): lax.ppermute(value, AXES, [(i, i ^ 1) for i in range(ny * nz * nx * 2)])]
    ppermute x13, waiting for transfers between devices: 21.9 us -> 19.5 us  [fetch(): return lax.ppermute(value, AXES, pairs)]
    ppermute x13, starting transfers between devices: 18.4 us -> 20.5 us  [fetch(): return lax.ppermute(value, AXES, pairs)]
    pallas_call x5 -> x7, Pallas kernels: 9.54 us -> 10.1 us  [score(): pl.pallas_call(functools.partial(score_kernel, listed_groups, key_parts,...]
  transfers between devices with their start and end apart: 17 -> 17, of which waited for: 8 -> 7; matrix products, arithmetic and copies ran while one was open for 0% -> 0% of each run, Pallas kernels for 16% -> 18%
where the time goes in v5:
time: 57.2 us; the launch traced here: 57 us
  starting transfers between devices  24.1 us (42%)
  waiting for transfers between devices  20.7 us (36%)
  Pallas kernels  10.4 us (18%)
  local copies, waits for them, and re-layouts  1.04 us (2%)
  other arithmetic  0.58 us (1%)
    ppermute x13, starting transfers between devices, fetch(): return lax.ppermute(value, AXES, pairs)  20.5 us
    ppermute x13, waiting for transfers between devices, fetch(): return lax.ppermute(value, AXES, pairs)  19.5 us
    pallas_call x7, Pallas kernels, score(): pl.pallas_call(functools.partial(score_kernel, listed_groups, key_parts,...  10.1 us
    ppermute x4, starting transfers between devices, swap(): lax.ppermute(value, AXES, [(i, i ^ 1) for i in range(ny * nz * nx * 2)])  3.61 us
    ppermute x4, waiting for transfers between devices, swap(): lax.ppermute(value, AXES, [(i, i ^ 1) for i in range(ny * nz * nx * 2)])  1.2 us
  transfers between devices with their start and end apart: 17, of which 7 were waited for; matrix products, arithmetic and copies ran while one was open for 0% of the time, Pallas kernels for 18%

profile of v5, /device:TPU:1, one launch (start us, length us, event | category | flops | bytes accessed | tf_op | source)
XLA Modules:
  0.0 57.0 jit_solution(5555316062860130434)
XLA Ops:
  0.0 1.4 %collective-permute-start = (bf16[256,768]{1,0:T(8,128)(2,1)}, bf16[256,768]{1,0:T(8,128)(2,1)S(1)}, u32[]{:S(2)}, u32[]{:S(2)}) collective-permute-start(bf16[256,768]{1,0:T(8,128)(2,1)} %rows_ref.1), channel_id=1, source_target_pairs={{0,1},{1,0},{2,3},{3,2},{4,5},{5,4},{6,7},{7,6},{8,9},{9,8},{10,11... | collective-permute-start | bytes 1179656 | tf_op jit(solution)/shard_map/ppermute | solution.py:174
  1.4 1.0 %copy-done = bf16[256,768]{1,0:T(8,128)(2,1)S(1)} copy-done((bf16[256,768]{1,0:T(8,128)(2,1)S(1)}, bf16[256,768]{1,0:T(8,128)(2,1)}, u32[]{:S(2)}) %copy-start) | copy-done | bytes 393240
  2.4 0.2 own.1.half_ref
  2.6 0.4 collective-permute-done.1
  3.0 0.2 chip.1.refs_0_.refs_1_
  3.2 1.4 %collective-permute-start.2 = (bf16[528,768]{1,0:T(8,128)(2,1)S(1)}, bf16[528,768]{1,0:T(8,128)(2,1)S(1)}, u32[]{:S(2)}, u32[]{:S(2)}) collective-permute-start(bf16[528,768]{1,0:T(8,128)(2,1)S(1)} %chip.1.refs_0_.refs_1_), channel_id=1, source_target_pairs={{32,0},{97,1},{34,2},{99,3},{36,4},{101,5},{38,6},{103,7},{40,8},{... | collective-permute-start | bytes 2433032 | tf_op jit(solution)/shard_map/ppermute | solution.py:168
  4.6 3.6 %collective-permute-start.4 = (bf16[528,768]{1,0:T(8,128)(2,1)S(1)}, bf16[528,768]{1,0:T(8,128)(2,1)S(1)}, u32[]{:S(2)}, u32[]{:S(2)}) collective-permute-start(bf16[528,768]{1,0:T(8,128)(2,1)S(1)} %chip.1.refs_0_.refs_1_), channel_id=1, source_target_pairs={{4,0},{17,1},{6,2},{19,3},{0,4},{21,5},{2,6},{23,7},{12,8},{25,9},... | collective-permute-start | bytes 2433032 | tf_op jit(solution)/shard_map/ppermute | solution.py:168
  8.2 0.4 collective-permute-start.6
  8.7 7.3 %collective-permute-done.2.refs_1_ = bf16[528,768]{1,0:T(8,128)(2,1)S(1)} collective-permute-done((bf16[528,768]{1,0:T(8,128)(2,1)S(1)}, bf16[528,768]{1,0:T(8,128)(2,1)S(1)}, u32[]{:S(2)}, u32[]{:S(2)}) %collective-permute-start.2) | collective-permute-done | bytes 811040 | tf_op jit(solution)/shard_map/ppermute | solution.py:168
  16.0 0.5 collective-permute-start.3
  16.5 1.7 %collective-permute-done.4.refs_3_.refs_2_ = bf16[528,768]{1,0:T(8,128)(2,1)S(1)} collective-permute-done((bf16[528,768]{1,0:T(8,128)(2,1)S(1)}, bf16[528,768]{1,0:T(8,128)(2,1)S(1)}, u32[]{:S(2)}, u32[]{:S(2)}) %collective-permute-start.4) | collective-permute-done | bytes 811040 | tf_op jit(solution)/shard_map/ppermute | solution.py:168
  18.2 0.9 %collective-permute-start.5 = (bf16[528,768]{1,0:T(8,128)(2,1)S(1)}, bf16[528,768]{1,0:T(8,128)(2,1)S(1)}, u32[]{:S(2)}, u32[]{:S(2)}) collective-permute-start(bf16[528,768]{1,0:T(8,128)(2,1)S(1)} %collective-permute-done.4.refs_3_.refs_2_), channel_id=1, source_target_pairs={{24,0},{7,1},{26,2},{1,3},{28,4},{3,5},{30,6},{5,7},{0,8},{15,9},{... | collective-permute-start | bytes 2433032 | tf_op jit(solution)/shard_map/ppermute | solution.py:168
  19.1 1.3 %collective-permute-start.8 = (bf16[528,768]{1,0:T(8,128)(2,1)S(1)}, bf16[528,768]{1,0:T(8,128)(2,1)S(1)}, u32[]{:S(2)}, u32[]{:S(2)}) collective-permute-start(bf16[528,768]{1,0:T(8,128)(2,1)S(1)} %collective-permute-done.2.refs_1_), channel_id=1, source_target_pairs={{32,0},{97,1},{34,2},{99,3},{36,4},{101,5},{38,6},{103,7},{40,8},{... | collective-permute-start | bytes 2433032 | tf_op jit(solution)/shard_map/ppermute | solution.py:168
  20.4 7.3 %collective-permute-done.6.refs_3_ = bf16[528,768]{1,0:T(8,128)(2,1)S(1)} collective-permute-done((bf16[528,768]{1,0:T(8,128)(2,1)S(1)}, bf16[528,768]{1,0:T(8,128)(2,1)S(1)}, u32[]{:S(2)}, u32[]{:S(2)}) %collective-permute-start.6) | collective-permute-done | bytes 811040 | tf_op jit(solution)/shard_map/ppermute | solution.py:168
  27.6 2.5 %collective-permute-start.9 = (bf16[528,768]{1,0:T(8,128)(2,1)S(1)}, bf16[528,768]{1,0:T(8,128)(2,1)S(1)}, u32[]{:S(2)}, u32[]{:S(2)}) collective-permute-start(bf16[528,768]{1,0:T(8,128)(2,1)S(1)} %collective-permute-done.6.refs_3_), channel_id=1, source_target_pairs={{24,0},{3,1},{26,2},{5,3},{28,4},{7,5},{30,6},{1,7},{0,8},{11,9},{... | collective-permute-start | bytes 2433032 | tf_op jit(solution)/shard_map/ppermute | solution.py:168
  30.1 2.1 %score.7 = (f32[1536,128]{1,0:T(8,128)S(1)}, f32[1536,128]{1,0:T(8,128)S(1)}) custom-call(bf16[528,768]{1,0:T(8,128)(2,1)S(1)} %chip.1.refs_0_.refs_1_, bf16[528,768]{1,0:T(8,128)(2,1)S(1)} %collective-permute-done.2.refs_1_, bf16[528,768]{1,0:T(8,128)(2,1)S(1)} %collective-permute-done.3.refs_2_, bf16[528,768]{1,0:T(8,128)(2,1)S(1)} %collective-permute-done.4.refs_3_.refs_2_), custom_call_target="tpu_custom_call" | custom-call | flops 1811939328 | bytes 3538944 | tf_op jit(solution)/shard_map/score/pallas_call | solution.py:137
  32.2 1.4 %score.8 = (f32[1536,128]{1,0:T(8,128)S(1)}, f32[1,512]{1,0:T(1,128)S(1)}) custom-call(bf16[528,768]{1,0:T(8,128)(2,1)S(1)} %chip.1.refs_0_.refs_1_, bf16[528,768]{1,0:T(8,128)(2,1)S(1)} %collective-permute-done.2.refs_1_, bf16[528,768]{1,0:T(8,128)(2,1)S(1)} %collective-permute-done.3.refs_2_, bf16[528,768]{1,0:T(8,128)(2,1)S(1)} %collective-permute-done.6.refs_3_, ...), custom_call_target="tpu_custom_call" | custom-call | flops 1207959552 | bytes 3145728 | tf_op jit(solution)/shard_map/score/pallas_call | solution.py:137
  33.8 1.7 %score.10 = (f32[512,128]{1,0:T(8,128)S(1)}, f32[512,128]{1,0:T(8,128)S(1)}, f32[1,1024]{1,0:T(1,128)S(1)}) custom-call(bf16[528,768]{1,0:T(8,128)(2,1)S(1)} %collective-permute-done.8.refs_0_.refs_3_, bf16[528,768]{1,0:T(8,128)(2,1)S(1)} %chip.1.refs_0_.refs_1_, bf16[528,768]{1,0:T(8,128)(2,1)S(1)} %collective-permute-done.4.refs_3_.refs_2_, ...), custom_call_target="tpu_custom_call" | custom-call | flops 1409286144 | bytes 3538944 | tf_op jit(solution)/shard_map/score/pallas_call | solution.py:137
  35.5 1.5 %score.9 = (f32[1536,128]{1,0:T(8,128)S(1)}, f32[1,512]{1,0:T(1,128)S(1)}) custom-call(bf16[528,768]{1,0:T(8,128)(2,1)S(1)} %chip.1.refs_0_.refs_1_, bf16[528,768]{1,0:T(8,128)(2,1)S(1)} %collective-permute-done.2.refs_1_, bf16[528,768]{1,0:T(8,128)(2,1)S(1)} %collective-permute-done.3.refs_2_, bf16[528,768]{1,0:T(8,128)(2,1)S(1)} %collective-permute-done.5.refs_3_.refs_4_, ...), custom_call_target="tpu_custom_call" | custom-call | flops 1207959552 | bytes 3145728 | tf_op jit(solution)/shard_map/score/pallas_call | solution.py:137
  37.0 0.3 collective-permute-start.10
  37.3 5.7 %collective-permute-start.11 = (f32[512]{0:T(512)S(1)}, f32[512]{0:T(512)S(1)}, u32[]{:S(2)}, u32[]{:S(2)}) collective-permute-start(f32[512]{0:T(512)S(1)} %bitcast.14), channel_id=1, source_target_pairs={{12,0},{19,1},{14,2},{21,3},{8,4},{23,5},{10,6},{17,7},{20,8},{27,... | collective-permute-start | bytes 6152 | tf_op jit(solution)/shard_map/ppermute | solution.py:168
  43.0 1.9 %score.11 = (f32[1536,128]{1,0:T(8,128)S(1)}, f32[512,128]{1,0:T(8,128)S(1)}, f32[1,512]{1,0:T(1,128)S(1)}) custom-call(bf16[528,768]{1,0:T(8,128)(2,1)S(1)} %chip.1.refs_0_.refs_1_, bf16[528,768]{1,0:T(8,128)(2,1)S(1)} %collective-permute-done.2.refs_1_, bf16[528,768]{1,0:T(8,128)(2,1)S(1)} %collective-permute-done.3.refs_2_, ...), custom_call_target="tpu_custom_call" | custom-call | flops 1610612736 | bytes 3932160 | tf_op jit(solution)/shard_map/score/pallas_call | solution.py:137
  45.0 0.5 score.13
  45.5 2.7 %collective-permute-start.13 = (f32[512]{0:T(512)S(1)}, f32[512]{0:T(512)S(1)}, u32[]{:S(2)}, u32[]{:S(2)}) collective-permute-start(f32[512]{0:T(512)S(1)} %bitcast.9), channel_id=1, source_target_pairs={{64,0},{65,1},{66,2},{67,3},{68,4},{69,5},{70,6},{71,7},{72,8},{73... | collective-permute-start | bytes 6152 | tf_op jit(solution)/shard_map/ppermute | solution.py:168
  48.2 0.9 %score.12 = f32[1,1536]{1,0:T(1,128)S(1)} custom-call(bf16[528,768]{1,0:T(8,128)(2,1)S(1)} %chip.1.refs_0_.refs_1_, bf16[528,768]{1,0:T(8,128)(2,1)S(1)} %collective-permute-done.2.refs_1_, bf16[528,768]{1,0:T(8,128)(2,1)S(1)} %collective-permute-done.3.refs_2_, bf16[272,768]{1,0:T(8,128)(2,1)S(1)} %collective-permute-done.7.refs_3_.refs_1_, ...), custom_call_target="tpu_custom_call" | custom-call | flops 603979776 | bytes 2752512 | tf_op jit(solution)/shard_map/score/pallas_call | solution.py:137
  49.1 1.1 %collective-permute-start.14 = (f32[512]{0:T(512)S(1)}, f32[512]{0:T(512)S(1)}, u32[]{:S(2)}, u32[]{:S(2)}) collective-permute-start(f32[512]{0:T(512)S(1)} %bitcast.17), channel_id=1, source_target_pairs={{96,0},{33,1},{98,2},{35,3},{100,4},{37,5},{102,6},{39,7},{104,8},... | collective-permute-start | bytes 6152 | tf_op jit(solution)/shard_map/ppermute | solution.py:168
  50.3 0.4 collective-permute-start.15
  50.7 1.2 %collective-permute-done.14 = f32[512]{0:T(512)S(1)} collective-permute-done((f32[512]{0:T(512)S(1)}, f32[512]{0:T(512)S(1)}, u32[]{:S(2)}, u32[]{:S(2)}) %collective-permute-start.14) | collective-permute-done | bytes 2080 | tf_op jit(solution)/shard_map/ppermute | solution.py:168
  51.9 2.0 %collective-permute-done.15 = f32[512]{0:T(512)S(1)} collective-permute-done((f32[512]{0:T(512)S(1)}, f32[512]{0:T(512)S(1)}, u32[]{:S(2)}, u32[]{:S(2)}) %collective-permute-start.15) | collective-permute-done | bytes 2080 | tf_op jit(solution)/shard_map/ppermute | solution.py:168
  54.0 1.7 %collective-permute-start.16 = (f32[256]{0:T(256)S(1)}, f32[256]{0:T(256)S(1)}, u32[]{:S(2)}, u32[]{:S(2)}) collective-permute-start(f32[256]{0:T(256)S(1)} %slice.36), channel_id=1, source_target_pairs={{0,1},{1,0},{2,3},{3,2},{4,5},{5,4},{6,7},{7,6},{8,9},{9,8},{10,11... | collective-permute-start | bytes 3080 | tf_op jit(solution)/shard_map/ppermute | solution.py:174
  55.7 0.8 %collective-permute-done.16 = f32[256]{0:T(256)S(1)} collective-permute-done((f32[256]{0:T(256)S(1)}, f32[256]{0:T(256)S(1)}, u32[]{:S(2)}, u32[]{:S(2)}) %collective-permute-start.16) | collective-permute-done | bytes 1056 | tf_op jit(solution)/shard_map/ppermute | solution.py:174
  56.5 0.6 slice_maximum_fusion.2
  (21 shorter events, 0.3 us)
Async XLA Ops:
  0.0 1.4 %copy-start.1 = (s32[256]{0:T(256)S(1)}, s32[256]{0:T(256)}, u32[]{:S(2)}) copy-start(s32[256]{0:T(256)} %param.3) | copy-start | bytes 3076
  0.0 3.0 %collective-permute-start = (bf16[256,768]{1,0:T(8,128)(2,1)}, bf16[256,768]{1,0:T(8,128)(2,1)S(1)}, u32[]{:S(2)}, u32[]{:S(2)}) collective-permute-start(bf16[256,768]{1,0:T(8,128)(2,1)} %rows_ref.1), channel_id=1, source_target_pairs={{0,1},{1,0},{2,3},{3,2},{4,5},{5,4},{6,7},{7,6},{8,9},{9,8},{10,11... | collective-permute-start | bytes 1179656 | tf_op jit(solution)/shard_map/ppermute | solution.py:174
  1.4 1.6 %collective-permute-start.1 = (s32[256]{0:T(256)}, s32[256]{0:T(256)S(1)}, u32[]{:S(2)}, u32[]{:S(2)}) collective-permute-start(s32[256]{0:T(256)} %param.3), channel_id=1, source_target_pairs={{0,1},{1,0},{2,3},{3,2},{4,5},{5,4},{6,7},{7,6},{8,9},{9,8},{10,11... | collective-permute-start | bytes 3080 | tf_op jit(solution)/shard_map/ppermute | solution.py:174
  1.4 1.0 %copy-start = (bf16[256,768]{1,0:T(8,128)(2,1)S(1)}, bf16[256,768]{1,0:T(8,128)(2,1)}, u32[]{:S(2)}) copy-start(bf16[256,768]{1,0:T(8,128)(2,1)} %rows_ref.1) | copy-start | bytes 1179652
  3.2 12.8 %collective-permute-start.2 = (bf16[528,768]{1,0:T(8,128)(2,1)S(1)}, bf16[528,768]{1,0:T(8,128)(2,1)S(1)}, u32[]{:S(2)}, u32[]{:S(2)}) collective-permute-start(bf16[528,768]{1,0:T(8,128)(2,1)S(1)} %chip.1.refs_0_.refs_1_), channel_id=1, source_target_pairs={{32,0},{97,1},{34,2},{99,3},{36,4},{101,5},{38,6},{103,7},{40,8},{... | collective-permute-start | bytes 2433032 | tf_op jit(solution)/shard_map/ppermute | solution.py:168
  4.6 13.5 %collective-permute-start.4 = (bf16[528,768]{1,0:T(8,128)(2,1)S(1)}, bf16[528,768]{1,0:T(8,128)(2,1)S(1)}, u32[]{:S(2)}, u32[]{:S(2)}) collective-permute-start(bf16[528,768]{1,0:T(8,128)(2,1)S(1)} %chip.1.refs_0_.refs_1_), channel_id=1, source_target_pairs={{4,0},{17,1},{6,2},{19,3},{0,4},{21,5},{2,6},{23,7},{12,8},{25,9},... | collective-permute-start | bytes 2433032 | tf_op jit(solution)/shard_map/ppermute | solution.py:168
  8.2 19.4 %collective-permute-start.6 = (bf16[528,768]{1,0:T(8,128)(2,1)S(1)}, bf16[528,768]{1,0:T(8,128)(2,1)S(1)}, u32[]{:S(2)}, u32[]{:S(2)}) collective-permute-start(bf16[528,768]{1,0:T(8,128)(2,1)S(1)} %chip.1.refs_0_.refs_1_), channel_id=1, source_target_pairs={{2,0},{9,1},{4,2},{11,3},{6,4},{13,5},{0,6},{15,7},{10,8},{17,9},{... | collective-permute-start | bytes 2433032 | tf_op jit(solution)/shard_map/ppermute | solution.py:168
  16.0 14.1 %collective-permute-start.3 = (bf16[528,768]{1,0:T(8,128)(2,1)S(1)}, bf16[528,768]{1,0:T(8,128)(2,1)S(1)}, u32[]{:S(2)}, u32[]{:S(2)}) collective-permute-start(bf16[528,768]{1,0:T(8,128)(2,1)S(1)} %collective-permute-done.2.refs_1_), channel_id=1, source_target_pairs={{0,1},{1,0},{2,3},{3,2},{4,5},{5,4},{6,7},{7,6},{8,9},{9,8},{10,11... | collective-permute-start | bytes 2433032 | tf_op jit(solution)/shard_map/ppermute | solution.py:174
  18.2 15.5 %collective-permute-start.5 = (bf16[528,768]{1,0:T(8,128)(2,1)S(1)}, bf16[528,768]{1,0:T(8,128)(2,1)S(1)}, u32[]{:S(2)}, u32[]{:S(2)}) collective-permute-start(bf16[528,768]{1,0:T(8,128)(2,1)S(1)} %collective-permute-done.4.refs_3_.refs_2_), channel_id=1, source_target_pairs={{24,0},{7,1},{26,2},{1,3},{28,4},{3,5},{30,6},{5,7},{0,8},{15,9},{... | collective-permute-start | bytes 2433032 | tf_op jit(solution)/shard_map/ppermute | solution.py:168
  19.1 14.7 %collective-permute-start.8 = (bf16[528,768]{1,0:T(8,128)(2,1)S(1)}, bf16[528,768]{1,0:T(8,128)(2,1)S(1)}, u32[]{:S(2)}, u32[]{:S(2)}) collective-permute-start(bf16[528,768]{1,0:T(8,128)(2,1)S(1)} %collective-permute-done.2.refs_1_), channel_id=1, source_target_pairs={{32,0},{97,1},{34,2},{99,3},{36,4},{101,5},{38,6},{103,7},{40,8},{... | collective-permute-start | bytes 2433032 | tf_op jit(solution)/shard_map/ppermute | solution.py:168
  27.6 15.3 %collective-permute-start.9 = (bf16[528,768]{1,0:T(8,128)(2,1)S(1)}, bf16[528,768]{1,0:T(8,128)(2,1)S(1)}, u32[]{:S(2)}, u32[]{:S(2)}) collective-permute-start(bf16[528,768]{1,0:T(8,128)(2,1)S(1)} %collective-permute-done.6.refs_3_), channel_id=1, source_target_pairs={{24,0},{3,1},{26,2},{5,3},{28,4},{7,5},{30,6},{1,7},{0,8},{11,9},{... | collective-permute-start | bytes 2433032 | tf_op jit(solution)/shard_map/ppermute | solution.py:168
  33.7 11.2 %collective-permute-start.7 = (bf16[272,768]{1,0:T(8,128)(2,1)S(1)}, bf16[272,768]{1,0:T(8,128)(2,1)S(1)}, u32[]{:S(2)}, u32[]{:S(2)}) collective-permute-start(bf16[272,768]{1,0:T(8,128)(2,1)S(1)} %slice.29), channel_id=1, source_target_pairs={{24,0},{7,1},{26,2},{1,3},{28,4},{3,5},{30,6},{5,7},{0,8},{15,9},{... | collective-permute-start | bytes 1253384 | tf_op jit(solution)/shard_map/ppermute | solution.py:168
  37.0 13.3 %collective-permute-start.10 = (f32[512]{0:T(512)S(1)}, f32[512]{0:T(512)S(1)}, u32[]{:S(2)}, u32[]{:S(2)}) collective-permute-start(f32[512]{0:T(512)S(1)} %bitcast.15), channel_id=1, source_target_pairs={{6,0},{25,1},{0,2},{27,3},{2,4},{29,5},{4,6},{31,7},{14,8},{1,9},{... | collective-permute-start | bytes 6152 | tf_op jit(solution)/shard_map/ppermute | solution.py:168
  37.3 13.4 %collective-permute-start.11 = (f32[512]{0:T(512)S(1)}, f32[512]{0:T(512)S(1)}, u32[]{:S(2)}, u32[]{:S(2)}) collective-permute-start(f32[512]{0:T(512)S(1)} %bitcast.14), channel_id=1, source_target_pairs={{12,0},{19,1},{14,2},{21,3},{8,4},{23,5},{10,6},{17,7},{20,8},{27,... | collective-permute-start | bytes 6152 | tf_op jit(solution)/shard_map/ppermute | solution.py:168
  44.9 5.8 %collective-permute-start.12 = (f32[512]{0:T(512)S(1)}, f32[512]{0:T(512)S(1)}, u32[]{:S(2)}, u32[]{:S(2)}) collective-permute-start(f32[512]{0:T(512)S(1)} %bitcast.12), channel_id=1, source_target_pairs={{14,0},{31,1},{8,2},{25,3},{10,4},{27,5},{12,6},{29,7},{22,8},{7,9... | collective-permute-start | bytes 6152 | tf_op jit(solution)/shard_map/ppermute | solution.py:168
  45.5 5.2 %collective-permute-start.13 = (f32[512]{0:T(512)S(1)}, f32[512]{0:T(512)S(1)}, u32[]{:S(2)}, u32[]{:S(2)}) collective-permute-start(f32[512]{0:T(512)S(1)} %bitcast.9), channel_id=1, source_target_pairs={{64,0},{65,1},{66,2},{67,3},{68,4},{69,5},{70,6},{71,7},{72,8},{73... | collective-permute-start | bytes 6152 | tf_op jit(solution)/shard_map/ppermute | solution.py:168
  49.1 2.8 %collective-permute-start.14 = (f32[512]{0:T(512)S(1)}, f32[512]{0:T(512)S(1)}, u32[]{:S(2)}, u32[]{:S(2)}) collective-permute-start(f32[512]{0:T(512)S(1)} %bitcast.17), channel_id=1, source_target_pairs={{96,0},{33,1},{98,2},{35,3},{100,4},{37,5},{102,6},{39,7},{104,8},... | collective-permute-start | bytes 6152 | tf_op jit(solution)/shard_map/ppermute | solution.py:168
  50.3 3.6 %collective-permute-start.15 = (f32[512]{0:T(512)S(1)}, f32[512]{0:T(512)S(1)}, u32[]{:S(2)}, u32[]{:S(2)}) collective-permute-start(f32[512]{0:T(512)S(1)} %bitcast.16), channel_id=1, source_target_pairs={{32,0},{97,1},{34,2},{99,3},{36,4},{101,5},{38,6},{103,7},{40,8},{... | collective-permute-start | bytes 6152 | tf_op jit(solution)/shard_map/ppermute | solution.py:168
  54.0 2.5 %collective-permute-start.16 = (f32[256]{0:T(256)S(1)}, f32[256]{0:T(256)S(1)}, u32[]{:S(2)}, u32[]{:S(2)}) collective-permute-start(f32[256]{0:T(256)S(1)} %slice.36), channel_id=1, source_target_pairs={{0,1},{1,0},{2,3},{3,2},{4,5},{5,4},{6,7},{7,6},{8,9},{9,8},{10,11... | collective-permute-start | bytes 3080 | tf_op jit(solution)/shard_map/ppermute | solution.py:174

commit v6 on v5

--- a/solution.py
+++ b/solution.py
@@ -186,28 +186,32 @@
     key4 = fetch(key2, (0, -1, 0), (0, 0, -1))
     far = fetch(near, (1, 0, 0), (-1, 0, 0))
 
-    first = [(block, (OWN, OTHER)), whole(near), (swap(near), (OTHER, OWN))]
-    second = [whole(far)]
-    (state,), _ = score([first], [(block, (OWN,)), whole(key2)], own_key=True)
+    own = [(block, (OWN, OTHER))]
+    sides = [whole(near), (swap(near), (OTHER, OWN))]
+    beyond = [whole(far)]
+    keys = [(block, (OWN,)), whole(key2)]
+    (state_o,), _ = score([own], keys, own_key=True)
+    key1, state_o = after((key1, state_o))
     key3 = fetch(key1, (0, -1, 0), (0, 0, 1))
-    (state,), top1 = score([first], [whole(key1)], [state], collect=0)
-    key4, state = after((key4, state))
+    (state_s,), _ = score([sides], keys)
+    (state_o, state_s), top1 = score([own, sides], [whole(key1)], [state_o, state_s], collect=0)
+    key4, state_s = after((key4, state_s))
     key5 = fetch(key4[:HALF], (0, -1, 0), (0, 0, -1))
-    (state,), top4 = score([first], [whole(key4)], [state], collect=0)
-    far, state = after((far, state))
-    (state2,), tops = score([second], [(block, (OWN,)), whole(key2), whole(key1), whole(key4)], collect=2)
+    (state_o, state_s), top4 = score([own, sides], [whole(key4)], [state_o, state_s], collect=0)
+    (state_b,), tops = score([beyond], keys + [whole(key1), whole(key4)], collect=2)
     home1 = give(jnp.maximum(top1, tops[: 2 * ROWS]), (0, 0, 1), (0, 1, 0))
     home4 = give(jnp.maximum(top4, tops[2 * ROWS :]), (0, -1, 2), (0, 2, -1))
-    (state, state2), top3 = score([first, second], [whole(key3)], [state, state2], collect=0)
+    (state_o, state_s, state_b), top3 = score([own, sides, beyond], [whole(key3)], [state_o, state_s, state_b], collect=0)
     home3 = give(top3, (0, -1, 1), (0, 1, 1))
-    ((best2, _),), _ = score([second], [whole(key5)], [state2], last=True)
-    ((best, _),), _ = score([first], [whole(key5)], [state], last=True)
-    best = best[0].reshape(3, 2 * ROWS)
-
-    from_far = give(best2[0], (2, 0, 0), (2, 0, 0))
-    from_up = give(best[1], (1, 0, 0), (-1, 0, 0))
-    from_down = give(best[2], (-1, 0, 0), (1, 0, 0))
-    home = functools.reduce(jnp.maximum, [best[0], home1, home4, home3, from_far, from_up, from_down])
+    ((best_b, _),), _ = score([beyond], [whole(key5)], [state_b], last=True)
+    ((best_s, _),), _ = score([sides], [whole(key5)], [state_s], last=True)
+    ((best_o, _),), _ = score([own], [whole(key5)], [state_o], last=True)
+    best_s = best_s[0].reshape(2, 2 * ROWS)
+
+    from_far = give(best_b[0], (2, 0, 0), (2, 0, 0))
+    from_up = give(best_s[0], (1, 0, 0), (-1, 0, 0))
+    from_down = give(best_s[1], (-1, 0, 0), (1, 0, 0))
+    home = functools.reduce(jnp.maximum, [best_o[0], home1, home4, home3, from_far, from_up, from_down])
     return jnp.maximum(home[:ROWS], swap(home[ROWS:]))
 
 

time: 57.2 us -> 57 us (level)
  waiting for transfers between devices: 20.7 us -> 19.7 us
  Pallas kernels: 10.4 us -> 11 us
    ppermute x13, waiting for transfers between devices: 19.5 us -> 18.5 us  [fetch(): return lax.ppermute(value, AXES, pairs)]
    pallas_call x7 -> x9, Pallas kernels: 10.1 us -> 10.6 us  [score(): pl.pallas_call(functools.partial(score_kernel, listed_groups, key_parts,...]
  transfers between devices with their start and end apart: 17 -> 17, of which waited for: 7 -> 7; matrix products, arithmetic and copies ran while one was open for 0% -> 0% of each run, Pallas kernels for 18% -> 19%
where the time goes in v6:
time: 57 us; the launch traced here: 56.8 us
  starting transfers between devices  24.4 us (43%)
  waiting for transfers between devices  19.7 us (35%)
  Pallas kernels  11 us (19%)
  local copies, waits for them, and re-layouts  1.04 us (2%)
  other arithmetic  0.58 us (1%)
    ppermute x13, starting transfers between devices, fetch(): return lax.ppermute(value, AXES, pairs)  20.5 us
    ppermute x13, waiting for transfers between devices, fetch(): return lax.ppermute(value, AXES, pairs)  18.5 us
    pallas_call x9, Pallas kernels, score(): pl.pallas_call(functools.partial(score_kernel, listed_groups, key_parts,...  10.6 us
    ppermute x4, starting transfers between devices, swap(): lax.ppermute(value, AXES, [(i, i ^ 1) for i in range(ny * nz * nx * 2)])  3.93 us
    ppermute x4, waiting for transfers between devices, swap(): lax.ppermute(value, AXES, [(i, i ^ 1) for i in range(ny * nz * nx * 2)])  1.2 us
  transfers between devices with their start and end apart: 17, of which 7 were waited for; matrix products, arithmetic and copies ran while one was open for 0% of the time, Pallas kernels for 19%

profile of v6, /device:TPU:1, one launch (start us, length us, event | category | flops | bytes accessed | tf_op | source)
XLA Modules:
  0.0 56.8 jit_solution(2672690275431659942)
XLA Ops:
  0.0 1.4 %collective-permute-start = (bf16[256,768]{1,0:T(8,128)(2,1)}, bf16[256,768]{1,0:T(8,128)(2,1)S(1)}, u32[]{:S(2)}, u32[]{:S(2)}) collective-permute-start(bf16[256,768]{1,0:T(8,128)(2,1)} %rows_ref.1), channel_id=1, source_target_pairs={{0,1},{1,0},{2,3},{3,2},{4,5},{5,4},{6,7},{7,6},{8,9},{9,8},{10,11... | collective-permute-start | bytes 1179656 | tf_op jit(solution)/shard_map/ppermute | solution.py:174
  1.4 1.0 %copy-done = bf16[256,768]{1,0:T(8,128)(2,1)S(1)} copy-done((bf16[256,768]{1,0:T(8,128)(2,1)S(1)}, bf16[256,768]{1,0:T(8,128)(2,1)}, u32[]{:S(2)}) %copy-start) | copy-done | bytes 393240
  2.6 0.4 collective-permute-done.1
  3.2 1.4 %collective-permute-start.4 = (bf16[528,768]{1,0:T(8,128)(2,1)S(1)}, bf16[528,768]{1,0:T(8,128)(2,1)S(1)}, u32[]{:S(2)}, u32[]{:S(2)}) collective-permute-start(bf16[528,768]{1,0:T(8,128)(2,1)S(1)} %chip.1.refs_0_.refs_2_.refs_1_), channel_id=1, source_target_pairs={{32,0},{97,1},{34,2},{99,3},{36,4},{101,5},{38,6},{103,7},{40,8},{... | collective-permute-start | bytes 2433032 | tf_op jit(solution)/shard_map/ppermute | solution.py:168
  4.6 3.6 %collective-permute-start.2 = (bf16[528,768]{1,0:T(8,128)(2,1)S(1)}, bf16[528,768]{1,0:T(8,128)(2,1)S(1)}, u32[]{:S(2)}, u32[]{:S(2)}) collective-permute-start(bf16[528,768]{1,0:T(8,128)(2,1)S(1)} %chip.1.refs_0_.refs_2_.refs_1_), channel_id=1, source_target_pairs={{4,0},{17,1},{6,2},{19,3},{0,4},{21,5},{2,6},{23,7},{12,8},{25,9},... | collective-permute-start | bytes 2433032 | tf_op jit(solution)/shard_map/ppermute | solution.py:168
  8.2 0.4 collective-permute-start.6
  8.7 7.3 %collective-permute-done.4.refs_0_.refs_1_ = bf16[528,768]{1,0:T(8,128)(2,1)S(1)} collective-permute-done((bf16[528,768]{1,0:T(8,128)(2,1)S(1)}, bf16[528,768]{1,0:T(8,128)(2,1)S(1)}, u32[]{:S(2)}, u32[]{:S(2)}) %collective-permute-start.4) | collective-permute-done | bytes 811040 | tf_op jit(solution)/shard_map/ppermute | solution.py:168
  16.0 0.5 collective-permute-start.5
  16.5 1.7 %collective-permute-done.2.refs_1_.refs_3_.refs_2_ = bf16[528,768]{1,0:T(8,128)(2,1)S(1)} collective-permute-done((bf16[528,768]{1,0:T(8,128)(2,1)S(1)}, bf16[528,768]{1,0:T(8,128)(2,1)S(1)}, u32[]{:S(2)}, u32[]{:S(2)}) %collective-permute-start.2) | collective-permute-done | bytes 811040 | tf_op jit(solution)/shard_map/ppermute | solution.py:168
  18.2 0.9 %collective-permute-start.3 = (bf16[528,768]{1,0:T(8,128)(2,1)S(1)}, bf16[528,768]{1,0:T(8,128)(2,1)S(1)}, u32[]{:S(2)}, u32[]{:S(2)}) collective-permute-start(bf16[528,768]{1,0:T(8,128)(2,1)S(1)} %collective-permute-done.2.refs_1_.refs_3_.refs_2_), channel_id=1, source_target_pairs={{24,0},{7,1},{26,2},{1,3},{28,4},{3,5},{30,6},{5,7},{0,8},{15,9},{... | collective-permute-start | bytes 2433032 | tf_op jit(solution)/shard_map/ppermute | solution.py:168
  19.1 1.3 %collective-permute-start.8 = (bf16[528,768]{1,0:T(8,128)(2,1)S(1)}, bf16[528,768]{1,0:T(8,128)(2,1)S(1)}, u32[]{:S(2)}, u32[]{:S(2)}) collective-permute-start(bf16[528,768]{1,0:T(8,128)(2,1)S(1)} %collective-permute-done.4.refs_0_.refs_1_), channel_id=1, source_target_pairs={{32,0},{97,1},{34,2},{99,3},{36,4},{101,5},{38,6},{103,7},{40,8},{... | collective-permute-start | bytes 2433032 | tf_op jit(solution)/shard_map/ppermute | solution.py:168
  20.4 0.8 %score.9 = (f32[512,128]{1,0:T(8,128)S(1)}, f32[512,128]{1,0:T(8,128)S(1)}) custom-call(bf16[528,768]{1,0:T(8,128)(2,1)S(1)} %chip.1.refs_0_.refs_2_.refs_1_, bf16[528,768]{1,0:T(8,128)(2,1)S(1)} %collective-permute-done.2.refs_1_.refs_3_.refs_2_), custom_call_target="tpu_custom_call" | custom-call | flops 603979776 | bytes 1966080 | tf_op jit(solution)/shard_map/score/pallas_call | solution.py:137
  21.2 6.4 %collective-permute-done.6.refs_3_ = bf16[528,768]{1,0:T(8,128)(2,1)S(1)} collective-permute-done((bf16[528,768]{1,0:T(8,128)(2,1)S(1)}, bf16[528,768]{1,0:T(8,128)(2,1)S(1)}, u32[]{:S(2)}, u32[]{:S(2)}) %collective-permute-start.6) | collective-permute-done | bytes 811040 | tf_op jit(solution)/shard_map/ppermute | solution.py:168
  27.6 2.5 %collective-permute-start.9 = (bf16[528,768]{1,0:T(8,128)(2,1)S(1)}, bf16[528,768]{1,0:T(8,128)(2,1)S(1)}, u32[]{:S(2)}, u32[]{:S(2)}) collective-permute-start(bf16[528,768]{1,0:T(8,128)(2,1)S(1)} %collective-permute-done.6.refs_3_), channel_id=1, source_target_pairs={{24,0},{3,1},{26,2},{5,3},{28,4},{7,5},{30,6},{1,7},{0,8},{11,9},{... | collective-permute-start | bytes 2433032 | tf_op jit(solution)/shard_map/ppermute | solution.py:168
  30.1 1.5 %score.10 = (f32[1024,128]{1,0:T(8,128)S(1)}, f32[1024,128]{1,0:T(8,128)S(1)}) custom-call(bf16[528,768]{1,0:T(8,128)(2,1)S(1)} %collective-permute-done.4.refs_0_.refs_1_, bf16[528,768]{1,0:T(8,128)(2,1)S(1)} %collective-permute-done.5.refs_1_.refs_2_, bf16[528,768]{1,0:T(8,128)(2,1)S(1)} %chip.1.refs_0_.refs_2_.refs_1_, ...), custom_call_target="tpu_custom_call" | custom-call | flops 1207959552 | bytes 2752512 | tf_op jit(solution)/shard_map/score/pallas_call | solution.py:137
  31.6 1.5 %score.11 = (f32[512,128]{1,0:T(8,128)S(1)}, f32[1024,128]{1,0:T(8,128)S(1)}, f32[1,512]{1,0:T(1,128)S(1)}) custom-call(bf16[528,768]{1,0:T(8,128)(2,1)S(1)} %chip.1.refs_0_.refs_2_.refs_1_, bf16[528,768]{1,0:T(8,128)(2,1)S(1)} %collective-permute-done.4.refs_0_.refs_1_, bf16[528,768]{1,0:T(8,128)(2,1)S(1)} %collective-permute-done.5.refs_1_.refs_2_, ...), custom_call_target="tpu_custom_call" | custom-call | flops 1207959552 | bytes 3145728 | tf_op jit(solution)/shard_map/score/pallas_call | solution.py:137
  33.2 1.7 %score.13 = (f32[512,128]{1,0:T(8,128)S(1)}, f32[512,128]{1,0:T(8,128)S(1)}, f32[1,1024]{1,0:T(1,128)S(1)}) custom-call(bf16[528,768]{1,0:T(8,128)(2,1)S(1)} %collective-permute-done.8.refs_0_.refs_3_, bf16[528,768]{1,0:T(8,128)(2,1)S(1)} %chip.1.refs_0_.refs_2_.refs_1_, bf16[528,768]{1,0:T(8,128)(2,1)S(1)} %collective-permute-done.2.refs_1_.refs_3_.refs_2_, ...), custom_call_target="tpu_custom_call" | custom-call | flops 1409286144 | bytes 3538944 | tf_op jit(solution)/shard_map/score/pallas_call | solution.py:137
  34.9 1.5 %score.12 = (f32[512,128]{1,0:T(8,128)S(1)}, f32[1024,128]{1,0:T(8,128)S(1)}, f32[1,512]{1,0:T(1,128)S(1)}) custom-call(bf16[528,768]{1,0:T(8,128)(2,1)S(1)} %chip.1.refs_0_.refs_2_.refs_1_, bf16[528,768]{1,0:T(8,128)(2,1)S(1)} %collective-permute-done.4.refs_0_.refs_1_, bf16[528,768]{1,0:T(8,128)(2,1)S(1)} %collective-permute-done.5.refs_1_.refs_2_, ...), custom_call_target="tpu_custom_call" | custom-call | flops 1207959552 | bytes 3145728 | tf_op jit(solution)/shard_map/score/pallas_call | solution.py:137
  36.4 0.3 collective-permute-start.10
  36.7 5.6 %collective-permute-start.11 = (f32[512]{0:T(512)S(1)}, f32[512]{0:T(512)S(1)}, u32[]{:S(2)}, u32[]{:S(2)}) collective-permute-start(f32[512]{0:T(512)S(1)} %bitcast.14), channel_id=1, source_target_pairs={{12,0},{19,1},{14,2},{21,3},{8,4},{23,5},{10,6},{17,7},{20,8},{27,... | collective-permute-start | bytes 6152 | tf_op jit(solution)/shard_map/ppermute | solution.py:168
  42.3 1.9 %score.14 = (f32[512,128]{1,0:T(8,128)S(1)}, f32[1024,128]{1,0:T(8,128)S(1)}, f32[512,128]{1,0:T(8,128)S(1)}, f32[1,512]{1,0:T(1,128)S(1)}) custom-call(bf16[528,768]{1,0:T(8,128)(2,1)S(1)} %chip.1.refs_0_.refs_2_.refs_1_, bf16[528,768]{1,0:T(8,128)(2,1)S(1)} %collective-permute-done.4.refs_0_.refs_1_, ...), custom_call_target="tpu_custom_call" | custom-call | flops 1610612736 | bytes 3932160 | tf_op jit(solution)/shard_map/score/pallas_call | solution.py:137
  44.4 0.5 score.16
  44.9 2.7 %collective-permute-start.13 = (f32[512]{0:T(512)S(1)}, f32[512]{0:T(512)S(1)}, u32[]{:S(2)}, u32[]{:S(2)}) collective-permute-start(f32[512]{0:T(512)S(1)} %bitcast.10), channel_id=1, source_target_pairs={{64,0},{65,1},{66,2},{67,3},{68,4},{69,5},{70,6},{71,7},{72,8},{73... | collective-permute-start | bytes 6152 | tf_op jit(solution)/shard_map/ppermute | solution.py:168
  47.6 0.7 %score.17 = f32[1,1024]{1,0:T(1,128)S(1)} custom-call(bf16[528,768]{1,0:T(8,128)(2,1)S(1)} %collective-permute-done.4.refs_0_.refs_1_, bf16[528,768]{1,0:T(8,128)(2,1)S(1)} %collective-permute-done.5.refs_1_.refs_2_, bf16[272,768]{1,0:T(8,128)(2,1)S(1)} %collective-permute-done.7.refs_1_.refs_2_, f32[1024,128]{1,0:T(8,128)S(1)} %get-tuple-element.50.refs_3_, ...), custom_call_target="tpu_custom_call" | custom-call | flops 402653184 | bytes 1966080 | tf_op jit(solution)/shard_map/score/pallas_call | solution.py:137
  48.3 1.2 %collective-permute-start.14 = (f32[512]{0:T(512)S(1)}, f32[512]{0:T(512)S(1)}, u32[]{:S(2)}, u32[]{:S(2)}) collective-permute-start(f32[512]{0:T(512)S(1)} %bitcast.17), channel_id=1, source_target_pairs={{96,0},{33,1},{98,2},{35,3},{100,4},{37,5},{102,6},{39,7},{104,8},... | collective-permute-start | bytes 6152 | tf_op jit(solution)/shard_map/ppermute | solution.py:168
  49.5 0.4 collective-permute-start.15
  49.9 0.5 score.15
  50.4 0.4 collective-permute-done.14
  50.8 2.6 %collective-permute-done.15 = f32[512]{0:T(512)S(1)} collective-permute-done((f32[512]{0:T(512)S(1)}, f32[512]{0:T(512)S(1)}, u32[]{:S(2)}, u32[]{:S(2)}) %collective-permute-start.15) | collective-permute-done | bytes 2080 | tf_op jit(solution)/shard_map/ppermute | solution.py:168
  53.4 2.0 %collective-permute-start.16 = (f32[256]{0:T(256)S(1)}, f32[256]{0:T(256)S(1)}, u32[]{:S(2)}, u32[]{:S(2)}) collective-permute-start(f32[256]{0:T(256)S(1)} %slice.31), channel_id=1, source_target_pairs={{0,1},{1,0},{2,3},{3,2},{4,5},{5,4},{6,7},{7,6},{8,9},{9,8},{10,11... | collective-permute-start | bytes 3080 | tf_op jit(solution)/shard_map/ppermute | solution.py:174
  55.5 0.8 %collective-permute-done.16 = f32[256]{0:T(256)S(1)} collective-permute-done((f32[256]{0:T(256)S(1)}, f32[256]{0:T(256)S(1)}, u32[]{:S(2)}, u32[]{:S(2)}) %collective-permute-start.16) | collective-permute-done | bytes 1056 | tf_op jit(solution)/shard_map/ppermute | solution.py:174
  56.3 0.6 slice_maximum_fusion.2
  (23 shorter events, 0.6 us)
Async XLA Ops:
  0.0 1.4 %copy-start.1 = (s32[256]{0:T(256)S(1)}, s32[256]{0:T(256)}, u32[]{:S(2)}) copy-start(s32[256]{0:T(256)} %param.3) | copy-start | bytes 3076
  0.0 3.0 %collective-permute-start = (bf16[256,768]{1,0:T(8,128)(2,1)}, bf16[256,768]{1,0:T(8,128)(2,1)S(1)}, u32[]{:S(2)}, u32[]{:S(2)}) collective-permute-start(bf16[256,768]{1,0:T(8,128)(2,1)} %rows_ref.1), channel_id=1, source_target_pairs={{0,1},{1,0},{2,3},{3,2},{4,5},{5,4},{6,7},{7,6},{8,9},{9,8},{10,11... | collective-permute-start | bytes 1179656 | tf_op jit(solution)/shard_map/ppermute | solution.py:174
  1.4 1.6 %collective-permute-start.1 = (s32[256]{0:T(256)}, s32[256]{0:T(256)S(1)}, u32[]{:S(2)}, u32[]{:S(2)}) collective-permute-start(s32[256]{0:T(256)} %param.3), channel_id=1, source_target_pairs={{0,1},{1,0},{2,3},{3,2},{4,5},{5,4},{6,7},{7,6},{8,9},{9,8},{10,11... | collective-permute-start | bytes 3080 | tf_op jit(solution)/shard_map/ppermute | solution.py:174
  1.4 1.0 %copy-start = (bf16[256,768]{1,0:T(8,128)(2,1)S(1)}, bf16[256,768]{1,0:T(8,128)(2,1)}, u32[]{:S(2)}) copy-start(bf16[256,768]{1,0:T(8,128)(2,1)} %rows_ref.1) | copy-start | bytes 1179652
  3.2 12.8 %collective-permute-start.4 = (bf16[528,768]{1,0:T(8,128)(2,1)S(1)}, bf16[528,768]{1,0:T(8,128)(2,1)S(1)}, u32[]{:S(2)}, u32[]{:S(2)}) collective-permute-start(bf16[528,768]{1,0:T(8,128)(2,1)S(1)} %chip.1.refs_0_.refs_2_.refs_1_), channel_id=1, source_target_pairs={{32,0},{97,1},{34,2},{99,3},{36,4},{101,5},{38,6},{103,7},{40,8},{... | collective-permute-start | bytes 2433032 | tf_op jit(solution)/shard_map/ppermute | solution.py:168
  4.6 13.5 %collective-permute-start.2 = (bf16[528,768]{1,0:T(8,128)(2,1)S(1)}, bf16[528,768]{1,0:T(8,128)(2,1)S(1)}, u32[]{:S(2)}, u32[]{:S(2)}) collective-permute-start(bf16[528,768]{1,0:T(8,128)(2,1)S(1)} %chip.1.refs_0_.refs_2_.refs_1_), channel_id=1, source_target_pairs={{4,0},{17,1},{6,2},{19,3},{0,4},{21,5},{2,6},{23,7},{12,8},{25,9},... | collective-permute-start | bytes 2433032 | tf_op jit(solution)/shard_map/ppermute | solution.py:168
  8.2 19.4 %collective-permute-start.6 = (bf16[528,768]{1,0:T(8,128)(2,1)S(1)}, bf16[528,768]{1,0:T(8,128)(2,1)S(1)}, u32[]{:S(2)}, u32[]{:S(2)}) collective-permute-start(bf16[528,768]{1,0:T(8,128)(2,1)S(1)} %chip.1.refs_0_.refs_2_.refs_1_), channel_id=1, source_target_pairs={{2,0},{9,1},{4,2},{11,3},{6,4},{13,5},{0,6},{15,7},{10,8},{17,9},{... | collective-permute-start | bytes 2433032 | tf_op jit(solution)/shard_map/ppermute | solution.py:168
  16.0 14.1 %collective-permute-start.5 = (bf16[528,768]{1,0:T(8,128)(2,1)S(1)}, bf16[528,768]{1,0:T(8,128)(2,1)S(1)}, u32[]{:S(2)}, u32[]{:S(2)}) collective-permute-start(bf16[528,768]{1,0:T(8,128)(2,1)S(1)} %collective-permute-done.4.refs_0_.refs_1_), channel_id=1, source_target_pairs={{0,1},{1,0},{2,3},{3,2},{4,5},{5,4},{6,7},{7,6},{8,9},{9,8},{10,11... | collective-permute-start | bytes 2433032 | tf_op jit(solution)/shard_map/ppermute | solution.py:174
  18.2 14.9 %collective-permute-start.3 = (bf16[528,768]{1,0:T(8,128)(2,1)S(1)}, bf16[528,768]{1,0:T(8,128)(2,1)S(1)}, u32[]{:S(2)}, u32[]{:S(2)}) collective-permute-start(bf16[528,768]{1,0:T(8,128)(2,1)S(1)} %collective-permute-done.2.refs_1_.refs_3_.refs_2_), channel_id=1, source_target_pairs={{24,0},{7,1},{26,2},{1,3},{28,4},{3,5},{30,6},{5,7},{0,8},{15,9},{... | collective-permute-start | bytes 2433032 | tf_op jit(solution)/shard_map/ppermute | solution.py:168
  19.1 14.1 %collective-permute-start.8 = (bf16[528,768]{1,0:T(8,128)(2,1)S(1)}, bf16[528,768]{1,0:T(8,128)(2,1)S(1)}, u32[]{:S(2)}, u32[]{:S(2)}) collective-permute-start(bf16[528,768]{1,0:T(8,128)(2,1)S(1)} %collective-permute-done.4.refs_0_.refs_1_), channel_id=1, source_target_pairs={{32,0},{97,1},{34,2},{99,3},{36,4},{101,5},{38,6},{103,7},{40,8},{... | collective-permute-start | bytes 2433032 | tf_op jit(solution)/shard_map/ppermute | solution.py:168
  27.6 14.7 %collective-permute-start.9 = (bf16[528,768]{1,0:T(8,128)(2,1)S(1)}, bf16[528,768]{1,0:T(8,128)(2,1)S(1)}, u32[]{:S(2)}, u32[]{:S(2)}) collective-permute-start(bf16[528,768]{1,0:T(8,128)(2,1)S(1)} %collective-permute-done.6.refs_3_), channel_id=1, source_target_pairs={{24,0},{3,1},{26,2},{5,3},{28,4},{7,5},{30,6},{1,7},{0,8},{11,9},{... | collective-permute-start | bytes 2433032 | tf_op jit(solution)/shard_map/ppermute | solution.py:168
  33.1 11.2 %collective-permute-start.7 = (bf16[272,768]{1,0:T(8,128)(2,1)S(1)}, bf16[272,768]{1,0:T(8,128)(2,1)S(1)}, u32[]{:S(2)}, u32[]{:S(2)}) collective-permute-start(bf16[272,768]{1,0:T(8,128)(2,1)S(1)} %slice.25), channel_id=1, source_target_pairs={{24,0},{7,1},{26,2},{1,3},{28,4},{3,5},{30,6},{5,7},{0,8},{15,9},{... | collective-permute-start | bytes 1253384 | tf_op jit(solution)/shard_map/ppermute | solution.py:168
  36.4 13.1 %collective-permute-start.10 = (f32[512]{0:T(512)S(1)}, f32[512]{0:T(512)S(1)}, u32[]{:S(2)}, u32[]{:S(2)}) collective-permute-start(f32[512]{0:T(512)S(1)} %bitcast.15), channel_id=1, source_target_pairs={{6,0},{25,1},{0,2},{27,3},{2,4},{29,5},{4,6},{31,7},{14,8},{1,9},{... | collective-permute-start | bytes 6152 | tf_op jit(solution)/shard_map/ppermute | solution.py:168
  36.7 13.7 %collective-permute-start.11 = (f32[512]{0:T(512)S(1)}, f32[512]{0:T(512)S(1)}, u32[]{:S(2)}, u32[]{:S(2)}) collective-permute-start(f32[512]{0:T(512)S(1)} %bitcast.14), channel_id=1, source_target_pairs={{12,0},{19,1},{14,2},{21,3},{8,4},{23,5},{10,6},{17,7},{20,8},{27,... | collective-permute-start | bytes 6152 | tf_op jit(solution)/shard_map/ppermute | solution.py:168
  44.3 6.1 %collective-permute-start.12 = (f32[512]{0:T(512)S(1)}, f32[512]{0:T(512)S(1)}, u32[]{:S(2)}, u32[]{:S(2)}) collective-permute-start(f32[512]{0:T(512)S(1)} %bitcast.13), channel_id=1, source_target_pairs={{14,0},{31,1},{8,2},{25,3},{10,4},{27,5},{12,6},{29,7},{22,8},{7,9... | collective-permute-start | bytes 6152 | tf_op jit(solution)/shard_map/ppermute | solution.py:168
  44.9 5.5 %collective-permute-start.13 = (f32[512]{0:T(512)S(1)}, f32[512]{0:T(512)S(1)}, u32[]{:S(2)}, u32[]{:S(2)}) collective-permute-start(f32[512]{0:T(512)S(1)} %bitcast.10), channel_id=1, source_target_pairs={{64,0},{65,1},{66,2},{67,3},{68,4},{69,5},{70,6},{71,7},{72,8},{73... | collective-permute-start | bytes 6152 | tf_op jit(solution)/shard_map/ppermute | solution.py:168
  48.3 2.5 %collective-permute-start.14 = (f32[512]{0:T(512)S(1)}, f32[512]{0:T(512)S(1)}, u32[]{:S(2)}, u32[]{:S(2)}) collective-permute-start(f32[512]{0:T(512)S(1)} %bitcast.17), channel_id=1, source_target_pairs={{96,0},{33,1},{98,2},{35,3},{100,4},{37,5},{102,6},{39,7},{104,8},... | collective-permute-start | bytes 6152 | tf_op jit(solution)/shard_map/ppermute | solution.py:168
  49.5 3.9 %collective-permute-start.15 = (f32[512]{0:T(512)S(1)}, f32[512]{0:T(512)S(1)}, u32[]{:S(2)}, u32[]{:S(2)}) collective-permute-start(f32[512]{0:T(512)S(1)} %bitcast.16), channel_id=1, source_target_pairs={{32,0},{97,1},{34,2},{99,3},{36,4},{101,5},{38,6},{103,7},{40,8},{... | collective-permute-start | bytes 6152 | tf_op jit(solution)/shard_map/ppermute | solution.py:168
  53.4 2.8 %collective-permute-start.16 = (f32[256]{0:T(256)S(1)}, f32[256]{0:T(256)S(1)}, u32[]{:S(2)}, u32[]{:S(2)}) collective-permute-start(f32[256]{0:T(256)S(1)} %slice.31), channel_id=1, source_target_pairs={{0,1},{1,0},{2,3},{3,2},{4,5},{5,4},{6,7},{7,6},{8,9},{9,8},{10,11... | collective-permute-start | bytes 3080 | tf_op jit(solution)/shard_map/ppermute | solution.py:174

commit v7 on v6

--- a/solution.py
+++ b/solution.py
@@ -187,7 +187,7 @@
     far = fetch(near, (1, 0, 0), (-1, 0, 0))
 
     own = [(block, (OWN, OTHER))]
-    sides = [whole(near), (swap(near), (OTHER, OWN))]
+    sides = [whole(near), whole(swap(near))]
     beyond = [whole(far)]
     keys = [(block, (OWN,)), whole(key2)]
     (state_o,), _ = score([own], keys, own_key=True)
@@ -209,9 +209,9 @@
     best_s = best_s[0].reshape(2, 2 * ROWS)
 
     from_far = give(best_b[0], (2, 0, 0), (2, 0, 0))
-    from_up = give(best_s[0], (1, 0, 0), (-1, 0, 0))
-    from_down = give(best_s[1], (-1, 0, 0), (1, 0, 0))
-    home = functools.reduce(jnp.maximum, [best_o[0], home1, home4, home3, from_far, from_up, from_down])
+    sides = jnp.maximum(best_s[0], swap(best_s[1]))
+    from_near = give(sides, (1, 0, 0), (-1, 0, 0))
+    home = functools.reduce(jnp.maximum, [best_o[0], home1, home4, home3, from_far, from_near])
     return jnp.maximum(home[:ROWS], swap(home[ROWS:]))
 
 

time: 57 us -> 57 us (level)
  starting transfers between devices: 24.4 us -> 25.2 us
  waiting for transfers between devices: 19.7 us -> 18.9 us
    ppermute x4 -> x5, starting transfers between devices: 3.93 us -> 7.74 us  [swap(): lax.ppermute(value, AXES, [(i, i ^ 1) for i in range(ny * nz * nx * 2)])]
    ppermute x13 -> x12, starting transfers between devices: 20.5 us -> 17.5 us  [fetch(): return lax.ppermute(value, AXES, pairs)]
    ppermute x13 -> x12, waiting for transfers between devices: 18.5 us -> 17.7 us  [fetch(): return lax.ppermute(value, AXES, pairs)]
    ppermute x4 -> x5, waiting for transfers between devices: 1.2 us -> 1.2 us  [swap(): lax.ppermute(value, AXES, [(i, i ^ 1) for i in range(ny * nz * nx * 2)])]
  transfers between devices with their start and end apart: 17 -> 17, of which waited for: 7 -> 6; matrix products, arithmetic and copies ran while one was open for 0% -> 0% of each run, Pallas kernels for 19% -> 19%
where the time goes in v7:
time: 57 us; the launch traced here: 56.8 us
  starting transfers between devices  25.2 us (44%)
  waiting for transfers between devices  18.9 us (33%)
  Pallas kernels  10.9 us (19%)
  local copies, waits for them, and re-layouts  1.04 us (2%)
  other arithmetic  0.58 us (1%)
    ppermute x12, waiting for transfers between devices, fetch(): return lax.ppermute(value, AXES, pairs)  17.7 us
    ppermute x12, starting transfers between devices, fetch(): return lax.ppermute(value, AXES, pairs)  17.5 us
    pallas_call x9, Pallas kernels, score(): pl.pallas_call(functools.partial(score_kernel, listed_groups, key_parts,...  10.6 us
    ppermute x5, starting transfers between devices, swap(): lax.ppermute(value, AXES, [(i, i ^ 1) for i in range(ny * nz * nx * 2)])  7.74 us
    ppermute x5, waiting for transfers between devices, swap(): lax.ppermute(value, AXES, [(i, i ^ 1) for i in range(ny * nz * nx * 2)])  1.2 us
  transfers between devices with their start and end apart: 17, of which 6 were waited for; matrix products, arithmetic and copies ran while one was open for 0% of the time, Pallas kernels for 19%

profile of v7, /device:TPU:1, one launch (start us, length us, event | category | flops | bytes accessed | tf_op | source)
XLA Modules:
  0.0 56.8 jit_solution(5134988076425861337)
XLA Ops:
  0.0 1.4 %collective-permute-start = (bf16[256,768]{1,0:T(8,128)(2,1)}, bf16[256,768]{1,0:T(8,128)(2,1)S(1)}, u32[]{:S(2)}, u32[]{:S(2)}) collective-permute-start(bf16[256,768]{1,0:T(8,128)(2,1)} %rows_ref.1), channel_id=1, source_target_pairs={{0,1},{1,0},{2,3},{3,2},{4,5},{5,4},{6,7},{7,6},{8,9},{9,8},{10,11... | collective-permute-start | bytes 1179656 | tf_op jit(solution)/shard_map/ppermute | solution.py:174
  1.4 1.0 %copy-done = bf16[256,768]{1,0:T(8,128)(2,1)S(1)} copy-done((bf16[256,768]{1,0:T(8,128)(2,1)S(1)}, bf16[256,768]{1,0:T(8,128)(2,1)}, u32[]{:S(2)}) %copy-start) | copy-done | bytes 393240
  2.6 0.4 collective-permute-done.1
  3.0 0.2 chip.1.refs_0_.refs_2_.refs_1_
  3.2 1.4 %collective-permute-start.4 = (bf16[528,768]{1,0:T(8,128)(2,1)S(1)}, bf16[528,768]{1,0:T(8,128)(2,1)S(1)}, u32[]{:S(2)}, u32[]{:S(2)}) collective-permute-start(bf16[528,768]{1,0:T(8,128)(2,1)S(1)} %chip.1.refs_0_.refs_2_.refs_1_), channel_id=1, source_target_pairs={{32,0},{97,1},{34,2},{99,3},{36,4},{101,5},{38,6},{103,7},{40,8},{... | collective-permute-start | bytes 2433032 | tf_op jit(solution)/shard_map/ppermute | solution.py:168
  4.6 3.6 %collective-permute-start.2 = (bf16[528,768]{1,0:T(8,128)(2,1)S(1)}, bf16[528,768]{1,0:T(8,128)(2,1)S(1)}, u32[]{:S(2)}, u32[]{:S(2)}) collective-permute-start(bf16[528,768]{1,0:T(8,128)(2,1)S(1)} %chip.1.refs_0_.refs_2_.refs_1_), channel_id=1, source_target_pairs={{4,0},{17,1},{6,2},{19,3},{0,4},{21,5},{2,6},{23,7},{12,8},{25,9},... | collective-permute-start | bytes 2433032 | tf_op jit(solution)/shard_map/ppermute | solution.py:168
  8.2 0.4 collective-permute-start.6
  8.7 7.3 %collective-permute-done.4.refs_0_.refs_1_ = bf16[528,768]{1,0:T(8,128)(2,1)S(1)} collective-permute-done((bf16[528,768]{1,0:T(8,128)(2,1)S(1)}, bf16[528,768]{1,0:T(8,128)(2,1)S(1)}, u32[]{:S(2)}, u32[]{:S(2)}) %collective-permute-start.4) | collective-permute-done | bytes 811040 | tf_op jit(solution)/shard_map/ppermute | solution.py:168
  16.0 0.5 collective-permute-start.5
  16.5 1.7 %collective-permute-done.2.refs_1_.refs_3_.refs_2_ = bf16[528,768]{1,0:T(8,128)(2,1)S(1)} collective-permute-done((bf16[528,768]{1,0:T(8,128)(2,1)S(1)}, bf16[528,768]{1,0:T(8,128)(2,1)S(1)}, u32[]{:S(2)}, u32[]{:S(2)}) %collective-permute-start.2) | collective-permute-done | bytes 811040 | tf_op jit(solution)/shard_map/ppermute | solution.py:168
  18.2 0.9 %collective-permute-start.3 = (bf16[528,768]{1,0:T(8,128)(2,1)S(1)}, bf16[528,768]{1,0:T(8,128)(2,1)S(1)}, u32[]{:S(2)}, u32[]{:S(2)}) collective-permute-start(bf16[528,768]{1,0:T(8,128)(2,1)S(1)} %collective-permute-done.2.refs_1_.refs_3_.refs_2_), channel_id=1, source_target_pairs={{24,0},{7,1},{26,2},{1,3},{28,4},{3,5},{30,6},{5,7},{0,8},{15,9},{... | collective-permute-start | bytes 2433032 | tf_op jit(solution)/shard_map/ppermute | solution.py:168
  19.1 1.3 %collective-permute-start.8 = (bf16[528,768]{1,0:T(8,128)(2,1)S(1)}, bf16[528,768]{1,0:T(8,128)(2,1)S(1)}, u32[]{:S(2)}, u32[]{:S(2)}) collective-permute-start(bf16[528,768]{1,0:T(8,128)(2,1)S(1)} %collective-permute-done.4.refs_0_.refs_1_), channel_id=1, source_target_pairs={{32,0},{97,1},{34,2},{99,3},{36,4},{101,5},{38,6},{103,7},{40,8},{... | collective-permute-start | bytes 2433032 | tf_op jit(solution)/shard_map/ppermute | solution.py:168
  20.4 0.8 %score.9 = (f32[512,128]{1,0:T(8,128)S(1)}, f32[512,128]{1,0:T(8,128)S(1)}) custom-call(bf16[528,768]{1,0:T(8,128)(2,1)S(1)} %chip.1.refs_0_.refs_2_.refs_1_, bf16[528,768]{1,0:T(8,128)(2,1)S(1)} %collective-permute-done.2.refs_1_.refs_3_.refs_2_), custom_call_target="tpu_custom_call" | custom-call | flops 603979776 | bytes 1966080 | tf_op jit(solution)/shard_map/score/pallas_call | solution.py:137
  21.2 6.4 %collective-permute-done.6.refs_3_ = bf16[528,768]{1,0:T(8,128)(2,1)S(1)} collective-permute-done((bf16[528,768]{1,0:T(8,128)(2,1)S(1)}, bf16[528,768]{1,0:T(8,128)(2,1)S(1)}, u32[]{:S(2)}, u32[]{:S(2)}) %collective-permute-start.6) | collective-permute-done | bytes 811040 | tf_op jit(solution)/shard_map/ppermute | solution.py:168
  27.6 2.5 %collective-permute-start.9 = (bf16[528,768]{1,0:T(8,128)(2,1)S(1)}, bf16[528,768]{1,0:T(8,128)(2,1)S(1)}, u32[]{:S(2)}, u32[]{:S(2)}) collective-permute-start(bf16[528,768]{1,0:T(8,128)(2,1)S(1)} %collective-permute-done.6.refs_3_), channel_id=1, source_target_pairs={{24,0},{3,1},{26,2},{5,3},{28,4},{7,5},{30,6},{1,7},{0,8},{11,9},{... | collective-permute-start | bytes 2433032 | tf_op jit(solution)/shard_map/ppermute | solution.py:168
  30.1 1.5 %score.10 = (f32[1024,128]{1,0:T(8,128)S(1)}, f32[1024,128]{1,0:T(8,128)S(1)}) custom-call(bf16[528,768]{1,0:T(8,128)(2,1)S(1)} %collective-permute-done.4.refs_0_.refs_1_, bf16[528,768]{1,0:T(8,128)(2,1)S(1)} %collective-permute-done.5.refs_1_.refs_2_, bf16[528,768]{1,0:T(8,128)(2,1)S(1)} %chip.1.refs_0_.refs_2_.refs_1_, ...), custom_call_target="tpu_custom_call" | custom-call | flops 1207959552 | bytes 2752512 | tf_op jit(solution)/shard_map/score/pallas_call | solution.py:137
  31.6 1.4 %score.11 = (f32[512,128]{1,0:T(8,128)S(1)}, f32[1024,128]{1,0:T(8,128)S(1)}, f32[1,512]{1,0:T(1,128)S(1)}) custom-call(bf16[528,768]{1,0:T(8,128)(2,1)S(1)} %chip.1.refs_0_.refs_2_.refs_1_, bf16[528,768]{1,0:T(8,128)(2,1)S(1)} %collective-permute-done.4.refs_0_.refs_1_, bf16[528,768]{1,0:T(8,128)(2,1)S(1)} %collective-permute-done.5.refs_1_.refs_2_, ...), custom_call_target="tpu_custom_call" | custom-call | flops 1207959552 | bytes 3145728 | tf_op jit(solution)/shard_map/score/pallas_call | solution.py:137
  33.2 1.7 %score.13 = (f32[512,128]{1,0:T(8,128)S(1)}, f32[512,128]{1,0:T(8,128)S(1)}, f32[1,1024]{1,0:T(1,128)S(1)}) custom-call(bf16[528,768]{1,0:T(8,128)(2,1)S(1)} %collective-permute-done.8.refs_0_.refs_3_, bf16[528,768]{1,0:T(8,128)(2,1)S(1)} %chip.1.refs_0_.refs_2_.refs_1_, bf16[528,768]{1,0:T(8,128)(2,1)S(1)} %collective-permute-done.2.refs_1_.refs_3_.refs_2_, ...), custom_call_target="tpu_custom_call" | custom-call | flops 1409286144 | bytes 3538944 | tf_op jit(solution)/shard_map/score/pallas_call | solution.py:137
  34.9 1.5 %score.12 = (f32[512,128]{1,0:T(8,128)S(1)}, f32[1024,128]{1,0:T(8,128)S(1)}, f32[1,512]{1,0:T(1,128)S(1)}) custom-call(bf16[528,768]{1,0:T(8,128)(2,1)S(1)} %chip.1.refs_0_.refs_2_.refs_1_, bf16[528,768]{1,0:T(8,128)(2,1)S(1)} %collective-permute-done.4.refs_0_.refs_1_, bf16[528,768]{1,0:T(8,128)(2,1)S(1)} %collective-permute-done.5.refs_1_.refs_2_, ...), custom_call_target="tpu_custom_call" | custom-call | flops 1207959552 | bytes 3145728 | tf_op jit(solution)/shard_map/score/pallas_call | solution.py:137
  36.4 0.3 collective-permute-start.10
  36.7 5.7 %collective-permute-start.11 = (f32[512]{0:T(512)S(1)}, f32[512]{0:T(512)S(1)}, u32[]{:S(2)}, u32[]{:S(2)}) collective-permute-start(f32[512]{0:T(512)S(1)} %bitcast.15), channel_id=1, source_target_pairs={{12,0},{19,1},{14,2},{21,3},{8,4},{23,5},{10,6},{17,7},{20,8},{27,... | collective-permute-start | bytes 6152 | tf_op jit(solution)/shard_map/ppermute | solution.py:168
  42.3 1.9 %score.14 = (f32[512,128]{1,0:T(8,128)S(1)}, f32[1024,128]{1,0:T(8,128)S(1)}, f32[512,128]{1,0:T(8,128)S(1)}, f32[1,512]{1,0:T(1,128)S(1)}) custom-call(bf16[528,768]{1,0:T(8,128)(2,1)S(1)} %chip.1.refs_0_.refs_2_.refs_1_, bf16[528,768]{1,0:T(8,128)(2,1)S(1)} %collective-permute-done.4.refs_0_.refs_1_, ...), custom_call_target="tpu_custom_call" | custom-call | flops 1610612736 | bytes 3932160 | tf_op jit(solution)/shard_map/score/pallas_call | solution.py:137
  44.3 0.7 %score.17 = f32[1,1024]{1,0:T(1,128)S(1)} custom-call(bf16[528,768]{1,0:T(8,128)(2,1)S(1)} %collective-permute-done.4.refs_0_.refs_1_, bf16[528,768]{1,0:T(8,128)(2,1)S(1)} %collective-permute-done.5.refs_1_.refs_2_, bf16[272,768]{1,0:T(8,128)(2,1)S(1)} %collective-permute-done.7.refs_1_.refs_2_, f32[1024,128]{1,0:T(8,128)S(1)} %get-tuple-element.50.refs_3_, ...), custom_call_target="tpu_custom_call" | custom-call | flops 402653184 | bytes 1966080 | tf_op jit(solution)/shard_map/score/pallas_call | solution.py:137
  45.1 4.3 %collective-permute-start.14 = (f32[512]{0:T(512)S(1)}, f32[512]{0:T(512)S(1)}, u32[]{:S(2)}, u32[]{:S(2)}) collective-permute-start(f32[512]{0:T(512)S(1)} %bitcast.17), channel_id=1, source_target_pairs={{0,1},{1,0},{2,3},{3,2},{4,5},{5,4},{6,7},{7,6},{8,9},{9,8},{10,11... | collective-permute-start | bytes 6152 | tf_op jit(solution)/shard_map/ppermute | solution.py:174
  49.3 0.5 score.16
  49.9 0.4 collective-permute-start.13
  50.3 0.8 %collective-permute-start.15 = (f32[512]{0:T(512)S(1)}, f32[512]{0:T(512)S(1)}, u32[]{:S(2)}, u32[]{:S(2)}) collective-permute-start(f32[512]{0:T(512)S(1)} %max.41), channel_id=1, source_target_pairs={{96,0},{33,1},{98,2},{35,3},{100,4},{37,5},{102,6},{39,7},{104,8},... | collective-permute-start | bytes 6152 | tf_op jit(solution)/shard_map/ppermute | solution.py:168
  51.1 0.5 score.15
  51.6 2.3 %collective-permute-done.13 = f32[512]{0:T(512)S(1)} collective-permute-done((f32[512]{0:T(512)S(1)}, f32[512]{0:T(512)S(1)}, u32[]{:S(2)}, u32[]{:S(2)}) %collective-permute-start.13) | collective-permute-done | bytes 2080 | tf_op jit(solution)/shard_map/ppermute | solution.py:168
  53.9 1.6 %collective-permute-start.16 = (f32[256]{0:T(256)S(1)}, f32[256]{0:T(256)S(1)}, u32[]{:S(2)}, u32[]{:S(2)}) collective-permute-start(f32[256]{0:T(256)S(1)} %slice.31), channel_id=1, source_target_pairs={{0,1},{1,0},{2,3},{3,2},{4,5},{5,4},{6,7},{7,6},{8,9},{9,8},{10,11... | collective-permute-start | bytes 3080 | tf_op jit(solution)/shard_map/ppermute | solution.py:174
  55.5 0.8 %collective-permute-done.16 = f32[256]{0:T(256)S(1)} collective-permute-done((f32[256]{0:T(256)S(1)}, f32[256]{0:T(256)S(1)}, u32[]{:S(2)}, u32[]{:S(2)}) %collective-permute-start.16) | collective-permute-done | bytes 1056 | tf_op jit(solution)/shard_map/ppermute | solution.py:174
  56.3 0.6 slice_maximum_fusion.2
  (24 shorter events, 0.4 us)
Async XLA Ops:
  0.0 1.4 %copy-start.1 = (s32[256]{0:T(256)S(1)}, s32[256]{0:T(256)}, u32[]{:S(2)}) copy-start(s32[256]{0:T(256)} %param.3) | copy-start | bytes 3076
  0.0 3.0 %collective-permute-start = (bf16[256,768]{1,0:T(8,128)(2,1)}, bf16[256,768]{1,0:T(8,128)(2,1)S(1)}, u32[]{:S(2)}, u32[]{:S(2)}) collective-permute-start(bf16[256,768]{1,0:T(8,128)(2,1)} %rows_ref.1), channel_id=1, source_target_pairs={{0,1},{1,0},{2,3},{3,2},{4,5},{5,4},{6,7},{7,6},{8,9},{9,8},{10,11... | collective-permute-start | bytes 1179656 | tf_op jit(solution)/shard_map/ppermute | solution.py:174
  1.4 1.6 %collective-permute-start.1 = (s32[256]{0:T(256)}, s32[256]{0:T(256)S(1)}, u32[]{:S(2)}, u32[]{:S(2)}) collective-permute-start(s32[256]{0:T(256)} %param.3), channel_id=1, source_target_pairs={{0,1},{1,0},{2,3},{3,2},{4,5},{5,4},{6,7},{7,6},{8,9},{9,8},{10,11... | collective-permute-start | bytes 3080 | tf_op jit(solution)/shard_map/ppermute | solution.py:174
  1.4 1.0 %copy-start = (bf16[256,768]{1,0:T(8,128)(2,1)S(1)}, bf16[256,768]{1,0:T(8,128)(2,1)}, u32[]{:S(2)}) copy-start(bf16[256,768]{1,0:T(8,128)(2,1)} %rows_ref.1) | copy-start | bytes 1179652
  3.2 12.8 %collective-permute-start.4 = (bf16[528,768]{1,0:T(8,128)(2,1)S(1)}, bf16[528,768]{1,0:T(8,128)(2,1)S(1)}, u32[]{:S(2)}, u32[]{:S(2)}) collective-permute-start(bf16[528,768]{1,0:T(8,128)(2,1)S(1)} %chip.1.refs_0_.refs_2_.refs_1_), channel_id=1, source_target_pairs={{32,0},{97,1},{34,2},{99,3},{36,4},{101,5},{38,6},{103,7},{40,8},{... | collective-permute-start | bytes 2433032 | tf_op jit(solution)/shard_map/ppermute | solution.py:168
  4.6 13.5 %collective-permute-start.2 = (bf16[528,768]{1,0:T(8,128)(2,1)S(1)}, bf16[528,768]{1,0:T(8,128)(2,1)S(1)}, u32[]{:S(2)}, u32[]{:S(2)}) collective-permute-start(bf16[528,768]{1,0:T(8,128)(2,1)S(1)} %chip.1.refs_0_.refs_2_.refs_1_), channel_id=1, source_target_pairs={{4,0},{17,1},{6,2},{19,3},{0,4},{21,5},{2,6},{23,7},{12,8},{25,9},... | collective-permute-start | bytes 2433032 | tf_op jit(solution)/shard_map/ppermute | solution.py:168
  8.2 19.4 %collective-permute-start.6 = (bf16[528,768]{1,0:T(8,128)(2,1)S(1)}, bf16[528,768]{1,0:T(8,128)(2,1)S(1)}, u32[]{:S(2)}, u32[]{:S(2)}) collective-permute-start(bf16[528,768]{1,0:T(8,128)(2,1)S(1)} %chip.1.refs_0_.refs_2_.refs_1_), channel_id=1, source_target_pairs={{2,0},{9,1},{4,2},{11,3},{6,4},{13,5},{0,6},{15,7},{10,8},{17,9},{... | collective-permute-start | bytes 2433032 | tf_op jit(solution)/shard_map/ppermute | solution.py:168
  16.0 14.1 %collective-permute-start.5 = (bf16[528,768]{1,0:T(8,128)(2,1)S(1)}, bf16[528,768]{1,0:T(8,128)(2,1)S(1)}, u32[]{:S(2)}, u32[]{:S(2)}) collective-permute-start(bf16[528,768]{1,0:T(8,128)(2,1)S(1)} %collective-permute-done.4.refs_0_.refs_1_), channel_id=1, source_target_pairs={{0,1},{1,0},{2,3},{3,2},{4,5},{5,4},{6,7},{7,6},{8,9},{9,8},{10,11... | collective-permute-start | bytes 2433032 | tf_op jit(solution)/shard_map/ppermute | solution.py:174
  18.2 14.9 %collective-permute-start.3 = (bf16[528,768]{1,0:T(8,128)(2,1)S(1)}, bf16[528,768]{1,0:T(8,128)(2,1)S(1)}, u32[]{:S(2)}, u32[]{:S(2)}) collective-permute-start(bf16[528,768]{1,0:T(8,128)(2,1)S(1)} %collective-permute-done.2.refs_1_.refs_3_.refs_2_), channel_id=1, source_target_pairs={{24,0},{7,1},{26,2},{1,3},{28,4},{3,5},{30,6},{5,7},{0,8},{15,9},{... | collective-permute-start | bytes 2433032 | tf_op jit(solution)/shard_map/ppermute | solution.py:168
  19.1 14.1 %collective-permute-start.8 = (bf16[528,768]{1,0:T(8,128)(2,1)S(1)}, bf16[528,768]{1,0:T(8,128)(2,1)S(1)}, u32[]{:S(2)}, u32[]{:S(2)}) collective-permute-start(bf16[528,768]{1,0:T(8,128)(2,1)S(1)} %collective-permute-done.4.refs_0_.refs_1_), channel_id=1, source_target_pairs={{32,0},{97,1},{34,2},{99,3},{36,4},{101,5},{38,6},{103,7},{40,8},{... | collective-permute-start | bytes 2433032 | tf_op jit(solution)/shard_map/ppermute | solution.py:168
  27.6 14.7 %collective-permute-start.9 = (bf16[528,768]{1,0:T(8,128)(2,1)S(1)}, bf16[528,768]{1,0:T(8,128)(2,1)S(1)}, u32[]{:S(2)}, u32[]{:S(2)}) collective-permute-start(bf16[528,768]{1,0:T(8,128)(2,1)S(1)} %collective-permute-done.6.refs_3_), channel_id=1, source_target_pairs={{24,0},{3,1},{26,2},{5,3},{28,4},{7,5},{30,6},{1,7},{0,8},{11,9},{... | collective-permute-start | bytes 2433032 | tf_op jit(solution)/shard_map/ppermute | solution.py:168
  33.1 11.2 %collective-permute-start.7 = (bf16[272,768]{1,0:T(8,128)(2,1)S(1)}, bf16[272,768]{1,0:T(8,128)(2,1)S(1)}, u32[]{:S(2)}, u32[]{:S(2)}) collective-permute-start(bf16[272,768]{1,0:T(8,128)(2,1)S(1)} %slice.25), channel_id=1, source_target_pairs={{24,0},{7,1},{26,2},{1,3},{28,4},{3,5},{30,6},{5,7},{0,8},{15,9},{... | collective-permute-start | bytes 1253384 | tf_op jit(solution)/shard_map/ppermute | solution.py:168
  36.4 15.2 %collective-permute-start.10 = (f32[512]{0:T(512)S(1)}, f32[512]{0:T(512)S(1)}, u32[]{:S(2)}, u32[]{:S(2)}) collective-permute-start(f32[512]{0:T(512)S(1)} %bitcast.16), channel_id=1, source_target_pairs={{6,0},{25,1},{0,2},{27,3},{2,4},{29,5},{4,6},{31,7},{14,8},{1,9},{... | collective-permute-start | bytes 6152 | tf_op jit(solution)/shard_map/ppermute | solution.py:168
  36.7 14.9 %collective-permute-start.11 = (f32[512]{0:T(512)S(1)}, f32[512]{0:T(512)S(1)}, u32[]{:S(2)}, u32[]{:S(2)}) collective-permute-start(f32[512]{0:T(512)S(1)} %bitcast.15), channel_id=1, source_target_pairs={{12,0},{19,1},{14,2},{21,3},{8,4},{23,5},{10,6},{17,7},{20,8},{27,... | collective-permute-start | bytes 6152 | tf_op jit(solution)/shard_map/ppermute | solution.py:168
  44.2 7.4 %collective-permute-start.12 = (f32[512]{0:T(512)S(1)}, f32[512]{0:T(512)S(1)}, u32[]{:S(2)}, u32[]{:S(2)}) collective-permute-start(f32[512]{0:T(512)S(1)} %bitcast.13), channel_id=1, source_target_pairs={{14,0},{31,1},{8,2},{25,3},{10,4},{27,5},{12,6},{29,7},{22,8},{7,9... | collective-permute-start | bytes 6152 | tf_op jit(solution)/shard_map/ppermute | solution.py:168
  45.1 5.2 %collective-permute-start.14 = (f32[512]{0:T(512)S(1)}, f32[512]{0:T(512)S(1)}, u32[]{:S(2)}, u32[]{:S(2)}) collective-permute-start(f32[512]{0:T(512)S(1)} %bitcast.17), channel_id=1, source_target_pairs={{0,1},{1,0},{2,3},{3,2},{4,5},{5,4},{6,7},{7,6},{8,9},{9,8},{10,11... | collective-permute-start | bytes 6152 | tf_op jit(solution)/shard_map/ppermute | solution.py:174
  49.9 4.0 %collective-permute-start.13 = (f32[512]{0:T(512)S(1)}, f32[512]{0:T(512)S(1)}, u32[]{:S(2)}, u32[]{:S(2)}) collective-permute-start(f32[512]{0:T(512)S(1)} %bitcast.10), channel_id=1, source_target_pairs={{64,0},{65,1},{66,2},{67,3},{68,4},{69,5},{70,6},{71,7},{72,8},{73... | collective-permute-start | bytes 6152 | tf_op jit(solution)/shard_map/ppermute | solution.py:168
  50.3 3.6 %collective-permute-start.15 = (f32[512]{0:T(512)S(1)}, f32[512]{0:T(512)S(1)}, u32[]{:S(2)}, u32[]{:S(2)}) collective-permute-start(f32[512]{0:T(512)S(1)} %max.41), channel_id=1, source_target_pairs={{96,0},{33,1},{98,2},{35,3},{100,4},{37,5},{102,6},{39,7},{104,8},... | collective-permute-start | bytes 6152 | tf_op jit(solution)/shard_map/ppermute | solution.py:168
  53.9 2.4 %collective-permute-start.16 = (f32[256]{0:T(256)S(1)}, f32[256]{0:T(256)S(1)}, u32[]{:S(2)}, u32[]{:S(2)}) collective-permute-start(f32[256]{0:T(256)S(1)} %slice.31), channel_id=1, source_target_pairs={{0,1},{1,0},{2,3},{3,2},{4,5},{5,4},{6,7},{7,6},{8,9},{9,8},{10,11... | collective-permute-start | bytes 3080 | tf_op jit(solution)/shard_map/ppermute | solution.py:174

commit v8 on v6

--- a/solution.py
+++ b/solution.py
@@ -108,7 +108,7 @@
         refs[0][0:1, at : at + LANES] = jnp.max(top, axis=0, keepdims=True)
 
 
-def score(groups, keys, states=None, last=False, collect=None, own_key=False):
+def score(groups, keys, states=None, last=False, collect=None, own_key=False, weight=1):
     blocks = []
 
     def listed(pieces):
@@ -139,7 +139,7 @@
         out_shape=tuple(shapes),
         compiler_params=pltpu.CompilerParams(vmem_limit_bytes=32 * 1024 * 1024),
         cost_estimate=pl.CostEstimate(
-            flops=2 * count * key_rows * width,
+            flops=2 * weight * count * key_rows * width,
             bytes_accessed=2 * width * (count + key_rows),
             transcendentals=0,
         ),
@@ -193,7 +193,7 @@
     (state_o,), _ = score([own], keys, own_key=True)
     key1, state_o = after((key1, state_o))
     key3 = fetch(key1, (0, -1, 0), (0, 0, 1))
-    (state_s,), _ = score([sides], keys)
+    (state_s,), _ = score([sides], keys, weight=4)
     (state_o, state_s), top1 = score([own, sides], [whole(key1)], [state_o, state_s], collect=0)
     key4, state_s = after((key4, state_s))
     key5 = fetch(key4[:HALF], (0, -1, 0), (0, 0, -1))

time: 57 us -> 57 us (level)
  no operation moved by 1% of the time
where the time goes in v8:
time: 57 us; the launch traced here: 56.8 us
  starting transfers between devices  24.4 us (43%)
  waiting for transfers between devices  19.7 us (35%)
  Pallas kernels  11 us (19%)
  local copies, waits for them, and re-layouts  1.04 us (2%)
  other arithmetic  0.58 us (1%)
    ppermute x13, starting transfers between devices, fetch(): return lax.ppermute(value, AXES, pairs)  20.5 us
    ppermute x13, waiting for transfers between devices, fetch(): return lax.ppermute(value, AXES, pairs)  18.5 us
    pallas_call x9, Pallas kernels, score(): pl.pallas_call(functools.partial(score_kernel, listed_groups, key_parts,...  10.6 us
    ppermute x4, starting transfers between devices, swap(): lax.ppermute(value, AXES, [(i, i ^ 1) for i in range(ny * nz * nx * 2)])  3.93 us
    ppermute x4, waiting for transfers between devices, swap(): lax.ppermute(value, AXES, [(i, i ^ 1) for i in range(ny * nz * nx * 2)])  1.2 us
  transfers between devices with their start and end apart: 17, of which 7 were waited for; matrix products, arithmetic and copies ran while one was open for 0% of the time, Pallas kernels for 19%

profile of v8, /device:TPU:1, one launch (start us, length us, event | category | flops | bytes accessed | tf_op | source)
XLA Modules:
  0.0 56.8 jit_solution(2672690275431659942)
XLA Ops:
  0.0 1.4 %collective-permute-start = (bf16[256,768]{1,0:T(8,128)(2,1)}, bf16[256,768]{1,0:T(8,128)(2,1)S(1)}, u32[]{:S(2)}, u32[]{:S(2)}) collective-permute-start(bf16[256,768]{1,0:T(8,128)(2,1)} %rows_ref.1), channel_id=1, source_target_pairs={{0,1},{1,0},{2,3},{3,2},{4,5},{5,4},{6,7},{7,6},{8,9},{9,8},{10,11... | collective-permute-start | bytes 1179656 | tf_op jit(solution)/shard_map/ppermute | solution.py:174
  1.4 1.0 %copy-done = bf16[256,768]{1,0:T(8,128)(2,1)S(1)} copy-done((bf16[256,768]{1,0:T(8,128)(2,1)S(1)}, bf16[256,768]{1,0:T(8,128)(2,1)}, u32[]{:S(2)}) %copy-start) | copy-done | bytes 393240
  2.6 0.4 collective-permute-done.1
  3.2 1.4 %collective-permute-start.4 = (bf16[528,768]{1,0:T(8,128)(2,1)S(1)}, bf16[528,768]{1,0:T(8,128)(2,1)S(1)}, u32[]{:S(2)}, u32[]{:S(2)}) collective-permute-start(bf16[528,768]{1,0:T(8,128)(2,1)S(1)} %chip.1.refs_0_.refs_2_.refs_1_), channel_id=1, source_target_pairs={{32,0},{97,1},{34,2},{99,3},{36,4},{101,5},{38,6},{103,7},{40,8},{... | collective-permute-start | bytes 2433032 | tf_op jit(solution)/shard_map/ppermute | solution.py:168
  4.6 3.6 %collective-permute-start.2 = (bf16[528,768]{1,0:T(8,128)(2,1)S(1)}, bf16[528,768]{1,0:T(8,128)(2,1)S(1)}, u32[]{:S(2)}, u32[]{:S(2)}) collective-permute-start(bf16[528,768]{1,0:T(8,128)(2,1)S(1)} %chip.1.refs_0_.refs_2_.refs_1_), channel_id=1, source_target_pairs={{4,0},{17,1},{6,2},{19,3},{0,4},{21,5},{2,6},{23,7},{12,8},{25,9},... | collective-permute-start | bytes 2433032 | tf_op jit(solution)/shard_map/ppermute | solution.py:168
  8.2 0.4 collective-permute-start.6
  8.7 7.3 %collective-permute-done.4.refs_0_.refs_1_ = bf16[528,768]{1,0:T(8,128)(2,1)S(1)} collective-permute-done((bf16[528,768]{1,0:T(8,128)(2,1)S(1)}, bf16[528,768]{1,0:T(8,128)(2,1)S(1)}, u32[]{:S(2)}, u32[]{:S(2)}) %collective-permute-start.4) | collective-permute-done | bytes 811040 | tf_op jit(solution)/shard_map/ppermute | solution.py:168
  16.0 0.5 collective-permute-start.5
  16.5 1.7 %collective-permute-done.2.refs_1_.refs_3_.refs_2_ = bf16[528,768]{1,0:T(8,128)(2,1)S(1)} collective-permute-done((bf16[528,768]{1,0:T(8,128)(2,1)S(1)}, bf16[528,768]{1,0:T(8,128)(2,1)S(1)}, u32[]{:S(2)}, u32[]{:S(2)}) %collective-permute-start.2) | collective-permute-done | bytes 811040 | tf_op jit(solution)/shard_map/ppermute | solution.py:168
  18.2 0.9 %collective-permute-start.3 = (bf16[528,768]{1,0:T(8,128)(2,1)S(1)}, bf16[528,768]{1,0:T(8,128)(2,1)S(1)}, u32[]{:S(2)}, u32[]{:S(2)}) collective-permute-start(bf16[528,768]{1,0:T(8,128)(2,1)S(1)} %collective-permute-done.2.refs_1_.refs_3_.refs_2_), channel_id=1, source_target_pairs={{24,0},{7,1},{26,2},{1,3},{28,4},{3,5},{30,6},{5,7},{0,8},{15,9},{... | collective-permute-start | bytes 2433032 | tf_op jit(solution)/shard_map/ppermute | solution.py:168
  19.1 1.3 %collective-permute-start.8 = (bf16[528,768]{1,0:T(8,128)(2,1)S(1)}, bf16[528,768]{1,0:T(8,128)(2,1)S(1)}, u32[]{:S(2)}, u32[]{:S(2)}) collective-permute-start(bf16[528,768]{1,0:T(8,128)(2,1)S(1)} %collective-permute-done.4.refs_0_.refs_1_), channel_id=1, source_target_pairs={{32,0},{97,1},{34,2},{99,3},{36,4},{101,5},{38,6},{103,7},{40,8},{... | collective-permute-start | bytes 2433032 | tf_op jit(solution)/shard_map/ppermute | solution.py:168
  20.4 0.8 %score.9 = (f32[512,128]{1,0:T(8,128)S(1)}, f32[512,128]{1,0:T(8,128)S(1)}) custom-call(bf16[528,768]{1,0:T(8,128)(2,1)S(1)} %chip.1.refs_0_.refs_2_.refs_1_, bf16[528,768]{1,0:T(8,128)(2,1)S(1)} %collective-permute-done.2.refs_1_.refs_3_.refs_2_), custom_call_target="tpu_custom_call" | custom-call | flops 603979776 | bytes 1966080 | tf_op jit(solution)/shard_map/score/pallas_call | solution.py:137
  21.2 6.4 %collective-permute-done.6.refs_3_ = bf16[528,768]{1,0:T(8,128)(2,1)S(1)} collective-permute-done((bf16[528,768]{1,0:T(8,128)(2,1)S(1)}, bf16[528,768]{1,0:T(8,128)(2,1)S(1)}, u32[]{:S(2)}, u32[]{:S(2)}) %collective-permute-start.6) | collective-permute-done | bytes 811040 | tf_op jit(solution)/shard_map/ppermute | solution.py:168
  27.6 2.5 %collective-permute-start.9 = (bf16[528,768]{1,0:T(8,128)(2,1)S(1)}, bf16[528,768]{1,0:T(8,128)(2,1)S(1)}, u32[]{:S(2)}, u32[]{:S(2)}) collective-permute-start(bf16[528,768]{1,0:T(8,128)(2,1)S(1)} %collective-permute-done.6.refs_3_), channel_id=1, source_target_pairs={{24,0},{3,1},{26,2},{5,3},{28,4},{7,5},{30,6},{1,7},{0,8},{11,9},{... | collective-permute-start | bytes 2433032 | tf_op jit(solution)/shard_map/ppermute | solution.py:168
  30.1 1.5 %score.10 = (f32[1024,128]{1,0:T(8,128)S(1)}, f32[1024,128]{1,0:T(8,128)S(1)}) custom-call(bf16[528,768]{1,0:T(8,128)(2,1)S(1)} %collective-permute-done.4.refs_0_.refs_1_, bf16[528,768]{1,0:T(8,128)(2,1)S(1)} %collective-permute-done.5.refs_1_.refs_2_, bf16[528,768]{1,0:T(8,128)(2,1)S(1)} %chip.1.refs_0_.refs_2_.refs_1_, ...), custom_call_target="tpu_custom_call" | custom-call | flops 4831838208 | bytes 2752512 | tf_op jit(solution)/shard_map/score/pallas_call | solution.py:137
  31.6 1.5 %score.11 = (f32[512,128]{1,0:T(8,128)S(1)}, f32[1024,128]{1,0:T(8,128)S(1)}, f32[1,512]{1,0:T(1,128)S(1)}) custom-call(bf16[528,768]{1,0:T(8,128)(2,1)S(1)} %chip.1.refs_0_.refs_2_.refs_1_, bf16[528,768]{1,0:T(8,128)(2,1)S(1)} %collective-permute-done.4.refs_0_.refs_1_, bf16[528,768]{1,0:T(8,128)(2,1)S(1)} %collective-permute-done.5.refs_1_.refs_2_, ...), custom_call_target="tpu_custom_call" | custom-call | flops 1207959552 | bytes 3145728 | tf_op jit(solution)/shard_map/score/pallas_call | solution.py:137
  33.2 1.7 %score.13 = (f32[512,128]{1,0:T(8,128)S(1)}, f32[512,128]{1,0:T(8,128)S(1)}, f32[1,1024]{1,0:T(1,128)S(1)}) custom-call(bf16[528,768]{1,0:T(8,128)(2,1)S(1)} %collective-permute-done.8.refs_0_.refs_3_, bf16[528,768]{1,0:T(8,128)(2,1)S(1)} %chip.1.refs_0_.refs_2_.refs_1_, bf16[528,768]{1,0:T(8,128)(2,1)S(1)} %collective-permute-done.2.refs_1_.refs_3_.refs_2_, ...), custom_call_target="tpu_custom_call" | custom-call | flops 1409286144 | bytes 3538944 | tf_op jit(solution)/shard_map/score/pallas_call | solution.py:137
  34.9 1.5 %score.12 = (f32[512,128]{1,0:T(8,128)S(1)}, f32[1024,128]{1,0:T(8,128)S(1)}, f32[1,512]{1,0:T(1,128)S(1)}) custom-call(bf16[528,768]{1,0:T(8,128)(2,1)S(1)} %chip.1.refs_0_.refs_2_.refs_1_, bf16[528,768]{1,0:T(8,128)(2,1)S(1)} %collective-permute-done.4.refs_0_.refs_1_, bf16[528,768]{1,0:T(8,128)(2,1)S(1)} %collective-permute-done.5.refs_1_.refs_2_, ...), custom_call_target="tpu_custom_call" | custom-call | flops 1207959552 | bytes 3145728 | tf_op jit(solution)/shard_map/score/pallas_call | solution.py:137
  36.4 0.3 collective-permute-start.10
  36.7 5.6 %collective-permute-start.11 = (f32[512]{0:T(512)S(1)}, f32[512]{0:T(512)S(1)}, u32[]{:S(2)}, u32[]{:S(2)}) collective-permute-start(f32[512]{0:T(512)S(1)} %bitcast.14), channel_id=1, source_target_pairs={{12,0},{19,1},{14,2},{21,3},{8,4},{23,5},{10,6},{17,7},{20,8},{27,... | collective-permute-start | bytes 6152 | tf_op jit(solution)/shard_map/ppermute | solution.py:168
  42.3 1.9 %score.14 = (f32[512,128]{1,0:T(8,128)S(1)}, f32[1024,128]{1,0:T(8,128)S(1)}, f32[512,128]{1,0:T(8,128)S(1)}, f32[1,512]{1,0:T(1,128)S(1)}) custom-call(bf16[528,768]{1,0:T(8,128)(2,1)S(1)} %chip.1.refs_0_.refs_2_.refs_1_, bf16[528,768]{1,0:T(8,128)(2,1)S(1)} %collective-permute-done.4.refs_0_.refs_1_, ...), custom_call_target="tpu_custom_call" | custom-call | flops 1610612736 | bytes 3932160 | tf_op jit(solution)/shard_map/score/pallas_call | solution.py:137
  44.4 0.5 score.16
  44.9 2.7 %collective-permute-start.13 = (f32[512]{0:T(512)S(1)}, f32[512]{0:T(512)S(1)}, u32[]{:S(2)}, u32[]{:S(2)}) collective-permute-start(f32[512]{0:T(512)S(1)} %bitcast.10), channel_id=1, source_target_pairs={{64,0},{65,1},{66,2},{67,3},{68,4},{69,5},{70,6},{71,7},{72,8},{73... | collective-permute-start | bytes 6152 | tf_op jit(solution)/shard_map/ppermute | solution.py:168
  47.6 0.7 %score.17 = f32[1,1024]{1,0:T(1,128)S(1)} custom-call(bf16[528,768]{1,0:T(8,128)(2,1)S(1)} %collective-permute-done.4.refs_0_.refs_1_, bf16[528,768]{1,0:T(8,128)(2,1)S(1)} %collective-permute-done.5.refs_1_.refs_2_, bf16[272,768]{1,0:T(8,128)(2,1)S(1)} %collective-permute-done.7.refs_1_.refs_2_, f32[1024,128]{1,0:T(8,128)S(1)} %get-tuple-element.50.refs_3_, ...), custom_call_target="tpu_custom_call" | custom-call | flops 402653184 | bytes 1966080 | tf_op jit(solution)/shard_map/score/pallas_call | solution.py:137
  48.3 1.2 %collective-permute-start.14 = (f32[512]{0:T(512)S(1)}, f32[512]{0:T(512)S(1)}, u32[]{:S(2)}, u32[]{:S(2)}) collective-permute-start(f32[512]{0:T(512)S(1)} %bitcast.17), channel_id=1, source_target_pairs={{96,0},{33,1},{98,2},{35,3},{100,4},{37,5},{102,6},{39,7},{104,8},... | collective-permute-start | bytes 6152 | tf_op jit(solution)/shard_map/ppermute | solution.py:168
  49.5 0.4 collective-permute-start.15
  49.9 0.5 score.15
  50.4 0.4 collective-permute-done.14
  50.8 2.6 %collective-permute-done.15 = f32[512]{0:T(512)S(1)} collective-permute-done((f32[512]{0:T(512)S(1)}, f32[512]{0:T(512)S(1)}, u32[]{:S(2)}, u32[]{:S(2)}) %collective-permute-start.15) | collective-permute-done | bytes 2080 | tf_op jit(solution)/shard_map/ppermute | solution.py:168
  53.4 2.0 %collective-permute-start.16 = (f32[256]{0:T(256)S(1)}, f32[256]{0:T(256)S(1)}, u32[]{:S(2)}, u32[]{:S(2)}) collective-permute-start(f32[256]{0:T(256)S(1)} %slice.31), channel_id=1, source_target_pairs={{0,1},{1,0},{2,3},{3,2},{4,5},{5,4},{6,7},{7,6},{8,9},{9,8},{10,11... | collective-permute-start | bytes 3080 | tf_op jit(solution)/shard_map/ppermute | solution.py:174
  55.5 0.8 %collective-permute-done.16 = f32[256]{0:T(256)S(1)} collective-permute-done((f32[256]{0:T(256)S(1)}, f32[256]{0:T(256)S(1)}, u32[]{:S(2)}, u32[]{:S(2)}) %collective-permute-start.16) | collective-permute-done | bytes 1056 | tf_op jit(solution)/shard_map/ppermute | solution.py:174
  56.3 0.6 slice_maximum_fusion.2
  (23 shorter events, 0.6 us)
Async XLA Ops:
  0.0 1.4 %copy-start.1 = (s32[256]{0:T(256)S(1)}, s32[256]{0:T(256)}, u32[]{:S(2)}) copy-start(s32[256]{0:T(256)} %param.3) | copy-start | bytes 3076
  0.0 3.0 %collective-permute-start = (bf16[256,768]{1,0:T(8,128)(2,1)}, bf16[256,768]{1,0:T(8,128)(2,1)S(1)}, u32[]{:S(2)}, u32[]{:S(2)}) collective-permute-start(bf16[256,768]{1,0:T(8,128)(2,1)} %rows_ref.1), channel_id=1, source_target_pairs={{0,1},{1,0},{2,3},{3,2},{4,5},{5,4},{6,7},{7,6},{8,9},{9,8},{10,11... | collective-permute-start | bytes 1179656 | tf_op jit(solution)/shard_map/ppermute | solution.py:174
  1.4 1.6 %collective-permute-start.1 = (s32[256]{0:T(256)}, s32[256]{0:T(256)S(1)}, u32[]{:S(2)}, u32[]{:S(2)}) collective-permute-start(s32[256]{0:T(256)} %param.3), channel_id=1, source_target_pairs={{0,1},{1,0},{2,3},{3,2},{4,5},{5,4},{6,7},{7,6},{8,9},{9,8},{10,11... | collective-permute-start | bytes 3080 | tf_op jit(solution)/shard_map/ppermute | solution.py:174
  1.4 1.0 %copy-start = (bf16[256,768]{1,0:T(8,128)(2,1)S(1)}, bf16[256,768]{1,0:T(8,128)(2,1)}, u32[]{:S(2)}) copy-start(bf16[256,768]{1,0:T(8,128)(2,1)} %rows_ref.1) | copy-start | bytes 1179652
  3.2 12.8 %collective-permute-start.4 = (bf16[528,768]{1,0:T(8,128)(2,1)S(1)}, bf16[528,768]{1,0:T(8,128)(2,1)S(1)}, u32[]{:S(2)}, u32[]{:S(2)}) collective-permute-start(bf16[528,768]{1,0:T(8,128)(2,1)S(1)} %chip.1.refs_0_.refs_2_.refs_1_), channel_id=1, source_target_pairs={{32,0},{97,1},{34,2},{99,3},{36,4},{101,5},{38,6},{103,7},{40,8},{... | collective-permute-start | bytes 2433032 | tf_op jit(solution)/shard_map/ppermute | solution.py:168
  4.6 13.5 %collective-permute-start.2 = (bf16[528,768]{1,0:T(8,128)(2,1)S(1)}, bf16[528,768]{1,0:T(8,128)(2,1)S(1)}, u32[]{:S(2)}, u32[]{:S(2)}) collective-permute-start(bf16[528,768]{1,0:T(8,128)(2,1)S(1)} %chip.1.refs_0_.refs_2_.refs_1_), channel_id=1, source_target_pairs={{4,0},{17,1},{6,2},{19,3},{0,4},{21,5},{2,6},{23,7},{12,8},{25,9},... | collective-permute-start | bytes 2433032 | tf_op jit(solution)/shard_map/ppermute | solution.py:168
  8.2 19.4 %collective-permute-start.6 = (bf16[528,768]{1,0:T(8,128)(2,1)S(1)}, bf16[528,768]{1,0:T(8,128)(2,1)S(1)}, u32[]{:S(2)}, u32[]{:S(2)}) collective-permute-start(bf16[528,768]{1,0:T(8,128)(2,1)S(1)} %chip.1.refs_0_.refs_2_.refs_1_), channel_id=1, source_target_pairs={{2,0},{9,1},{4,2},{11,3},{6,4},{13,5},{0,6},{15,7},{10,8},{17,9},{... | collective-permute-start | bytes 2433032 | tf_op jit(solution)/shard_map/ppermute | solution.py:168
  16.0 14.1 %collective-permute-start.5 = (bf16[528,768]{1,0:T(8,128)(2,1)S(1)}, bf16[528,768]{1,0:T(8,128)(2,1)S(1)}, u32[]{:S(2)}, u32[]{:S(2)}) collective-permute-start(bf16[528,768]{1,0:T(8,128)(2,1)S(1)} %collective-permute-done.4.refs_0_.refs_1_), channel_id=1, source_target_pairs={{0,1},{1,0},{2,3},{3,2},{4,5},{5,4},{6,7},{7,6},{8,9},{9,8},{10,11... | collective-permute-start | bytes 2433032 | tf_op jit(solution)/shard_map/ppermute | solution.py:174
  18.2 14.9 %collective-permute-start.3 = (bf16[528,768]{1,0:T(8,128)(2,1)S(1)}, bf16[528,768]{1,0:T(8,128)(2,1)S(1)}, u32[]{:S(2)}, u32[]{:S(2)}) collective-permute-start(bf16[528,768]{1,0:T(8,128)(2,1)S(1)} %collective-permute-done.2.refs_1_.refs_3_.refs_2_), channel_id=1, source_target_pairs={{24,0},{7,1},{26,2},{1,3},{28,4},{3,5},{30,6},{5,7},{0,8},{15,9},{... | collective-permute-start | bytes 2433032 | tf_op jit(solution)/shard_map/ppermute | solution.py:168
  19.1 14.1 %collective-permute-start.8 = (bf16[528,768]{1,0:T(8,128)(2,1)S(1)}, bf16[528,768]{1,0:T(8,128)(2,1)S(1)}, u32[]{:S(2)}, u32[]{:S(2)}) collective-permute-start(bf16[528,768]{1,0:T(8,128)(2,1)S(1)} %collective-permute-done.4.refs_0_.refs_1_), channel_id=1, source_target_pairs={{32,0},{97,1},{34,2},{99,3},{36,4},{101,5},{38,6},{103,7},{40,8},{... | collective-permute-start | bytes 2433032 | tf_op jit(solution)/shard_map/ppermute | solution.py:168
  27.6 14.7 %collective-permute-start.9 = (bf16[528,768]{1,0:T(8,128)(2,1)S(1)}, bf16[528,768]{1,0:T(8,128)(2,1)S(1)}, u32[]{:S(2)}, u32[]{:S(2)}) collective-permute-start(bf16[528,768]{1,0:T(8,128)(2,1)S(1)} %collective-permute-done.6.refs_3_), channel_id=1, source_target_pairs={{24,0},{3,1},{26,2},{5,3},{28,4},{7,5},{30,6},{1,7},{0,8},{11,9},{... | collective-permute-start | bytes 2433032 | tf_op jit(solution)/shard_map/ppermute | solution.py:168
  33.1 11.2 %collective-permute-start.7 = (bf16[272,768]{1,0:T(8,128)(2,1)S(1)}, bf16[272,768]{1,0:T(8,128)(2,1)S(1)}, u32[]{:S(2)}, u32[]{:S(2)}) collective-permute-start(bf16[272,768]{1,0:T(8,128)(2,1)S(1)} %slice.25), channel_id=1, source_target_pairs={{24,0},{7,1},{26,2},{1,3},{28,4},{3,5},{30,6},{5,7},{0,8},{15,9},{... | collective-permute-start | bytes 1253384 | tf_op jit(solution)/shard_map/ppermute | solution.py:168
  36.4 13.1 %collective-permute-start.10 = (f32[512]{0:T(512)S(1)}, f32[512]{0:T(512)S(1)}, u32[]{:S(2)}, u32[]{:S(2)}) collective-permute-start(f32[512]{0:T(512)S(1)} %bitcast.15), channel_id=1, source_target_pairs={{6,0},{25,1},{0,2},{27,3},{2,4},{29,5},{4,6},{31,7},{14,8},{1,9},{... | collective-permute-start | bytes 6152 | tf_op jit(solution)/shard_map/ppermute | solution.py:168
  36.7 13.7 %collective-permute-start.11 = (f32[512]{0:T(512)S(1)}, f32[512]{0:T(512)S(1)}, u32[]{:S(2)}, u32[]{:S(2)}) collective-permute-start(f32[512]{0:T(512)S(1)} %bitcast.14), channel_id=1, source_target_pairs={{12,0},{19,1},{14,2},{21,3},{8,4},{23,5},{10,6},{17,7},{20,8},{27,... | collective-permute-start | bytes 6152 | tf_op jit(solution)/shard_map/ppermute | solution.py:168
  44.3 6.1 %collective-permute-start.12 = (f32[512]{0:T(512)S(1)}, f32[512]{0:T(512)S(1)}, u32[]{:S(2)}, u32[]{:S(2)}) collective-permute-start(f32[512]{0:T(512)S(1)} %bitcast.13), channel_id=1, source_target_pairs={{14,0},{31,1},{8,2},{25,3},{10,4},{27,5},{12,6},{29,7},{22,8},{7,9... | collective-permute-start | bytes 6152 | tf_op jit(solution)/shard_map/ppermute | solution.py:168
  44.9 5.5 %collective-permute-start.13 = (f32[512]{0:T(512)S(1)}, f32[512]{0:T(512)S(1)}, u32[]{:S(2)}, u32[]{:S(2)}) collective-permute-start(f32[512]{0:T(512)S(1)} %bitcast.10), channel_id=1, source_target_pairs={{64,0},{65,1},{66,2},{67,3},{68,4},{69,5},{70,6},{71,7},{72,8},{73... | collective-permute-start | bytes 6152 | tf_op jit(solution)/shard_map/ppermute | solution.py:168
  48.3 2.5 %collective-permute-start.14 = (f32[512]{0:T(512)S(1)}, f32[512]{0:T(512)S(1)}, u32[]{:S(2)}, u32[]{:S(2)}) collective-permute-start(f32[512]{0:T(512)S(1)} %bitcast.17), channel_id=1, source_target_pairs={{96,0},{33,1},{98,2},{35,3},{100,4},{37,5},{102,6},{39,7},{104,8},... | collective-permute-start | bytes 6152 | tf_op jit(solution)/shard_map/ppermute | solution.py:168
  49.5 3.9 %collective-permute-start.15 = (f32[512]{0:T(512)S(1)}, f32[512]{0:T(512)S(1)}, u32[]{:S(2)}, u32[]{:S(2)}) collective-permute-start(f32[512]{0:T(512)S(1)} %bitcast.16), channel_id=1, source_target_pairs={{32,0},{97,1},{34,2},{99,3},{36,4},{101,5},{38,6},{103,7},{40,8},{... | collective-permute-start | bytes 6152 | tf_op jit(solution)/shard_map/ppermute | solution.py:168
  53.4 2.8 %collective-permute-start.16 = (f32[256]{0:T(256)S(1)}, f32[256]{0:T(256)S(1)}, u32[]{:S(2)}, u32[]{:S(2)}) collective-permute-start(f32[256]{0:T(256)S(1)} %slice.31), channel_id=1, source_target_pairs={{0,1},{1,0},{2,3},{3,2},{4,5},{5,4},{6,7},{7,6},{8,9},{9,8},{10,11... | collective-permute-start | bytes 3080 | tf_op jit(solution)/shard_map/ppermute | solution.py:174

commit v9 on v6

--- a/solution.py
+++ b/solution.py
@@ -184,11 +184,11 @@
     key2 = fetch(block, (0, 0, 2), (0, 2, 0))
     near = fetch(block, (1, 0, 0), (-1, 0, 0))
     key4 = fetch(key2, (0, -1, 0), (0, 0, -1))
-    far = fetch(near, (1, 0, 0), (-1, 0, 0))
+    far = fetch(near[:HALF], (1, 0, 0), (-1, 0, 0))
 
     own = [(block, (OWN, OTHER))]
     sides = [whole(near), (swap(near), (OTHER, OWN))]
-    beyond = [whole(far)]
+    beyond = [whole(far), whole(swap(far))]
     keys = [(block, (OWN,)), whole(key2)]
     (state_o,), _ = score([own], keys, own_key=True)
     key1, state_o = after((key1, state_o))

time: 57 us -> 57.3 us (level)
    ppermute x4 -> x5, starting transfers between devices: 3.93 us -> 5.35 us  [swap(): lax.ppermute(value, AXES, [(i, i ^ 1) for i in range(ny * nz * nx * 2)])]
    ppermute x13, starting transfers between devices: 20.5 us -> 19.5 us  [fetch(): return lax.ppermute(value, AXES, pairs)]
    ppermute x4 -> x5, waiting for transfers between devices: 1.2 us -> 1.2 us  [swap(): lax.ppermute(value, AXES, [(i, i ^ 1) for i in range(ny * nz * nx * 2)])]
  transfers between devices with their start and end apart: 17 -> 18, of which waited for: 7 -> 7; matrix products, arithmetic and copies ran while one was open for 0% -> 0% of each run, Pallas kernels for 19% -> 19%
where the time goes in v9:
time: 57.3 us; the launch traced here: 57.1 us
  starting transfers between devices  24.8 us (43%)
  waiting for transfers between devices  19.6 us (34%)
  Pallas kernels  10.9 us (19%)
  local copies, waits for them, and re-layouts  1.07 us (2%)
  other arithmetic  0.58 us (1%)
    ppermute x13, starting transfers between devices, fetch(): return lax.ppermute(value, AXES, pairs)  19.5 us
    ppermute x13, waiting for transfers between devices, fetch(): return lax.ppermute(value, AXES, pairs)  18.4 us
    pallas_call x9, Pallas kernels, score(): pl.pallas_call(functools.partial(score_kernel, listed_groups, key_parts,...  10.5 us
    ppermute x5, starting transfers between devices, swap(): lax.ppermute(value, AXES, [(i, i ^ 1) for i in range(ny * nz * nx * 2)])  5.35 us
    ppermute x5, waiting for transfers between devices, swap(): lax.ppermute(value, AXES, [(i, i ^ 1) for i in range(ny * nz * nx * 2)])  1.2 us
  transfers between devices with their start and end apart: 18, of which 7 were waited for; matrix products, arithmetic and copies ran while one was open for 0% of the time, Pallas kernels for 19%

profile of v9, /device:TPU:1, one launch (start us, length us, event | category | flops | bytes accessed | tf_op | source)
XLA Modules:
  0.0 57.1 jit_solution(12321985783966413154)
XLA Ops:
  0.0 1.4 %collective-permute-start = (bf16[256,768]{1,0:T(8,128)(2,1)}, bf16[256,768]{1,0:T(8,128)(2,1)S(1)}, u32[]{:S(2)}, u32[]{:S(2)}) collective-permute-start(bf16[256,768]{1,0:T(8,128)(2,1)} %rows_ref.1), channel_id=1, source_target_pairs={{0,1},{1,0},{2,3},{3,2},{4,5},{5,4},{6,7},{7,6},{8,9},{9,8},{10,11... | collective-permute-start | bytes 1179656 | tf_op jit(solution)/shard_map/ppermute | solution.py:174
  1.4 1.0 %copy-done = bf16[256,768]{1,0:T(8,128)(2,1)S(1)} copy-done((bf16[256,768]{1,0:T(8,128)(2,1)S(1)}, bf16[256,768]{1,0:T(8,128)(2,1)}, u32[]{:S(2)}) %copy-start) | copy-done | bytes 393240
  3.2 1.4 %collective-permute-start.4 = (bf16[528,768]{1,0:T(8,128)(2,1)S(1)}, bf16[528,768]{1,0:T(8,128)(2,1)S(1)}, u32[]{:S(2)}, u32[]{:S(2)}) collective-permute-start(bf16[528,768]{1,0:T(8,128)(2,1)S(1)} %chip.1.refs_0_.refs_2_), channel_id=1, source_target_pairs={{32,0},{97,1},{34,2},{99,3},{36,4},{101,5},{38,6},{103,7},{40,8},{... | collective-permute-start | bytes 2433032 | tf_op jit(solution)/shard_map/ppermute | solution.py:168
  4.6 3.6 %collective-permute-start.2 = (bf16[528,768]{1,0:T(8,128)(2,1)S(1)}, bf16[528,768]{1,0:T(8,128)(2,1)S(1)}, u32[]{:S(2)}, u32[]{:S(2)}) collective-permute-start(bf16[528,768]{1,0:T(8,128)(2,1)S(1)} %chip.1.refs_0_.refs_2_), channel_id=1, source_target_pairs={{4,0},{17,1},{6,2},{19,3},{0,4},{21,5},{2,6},{23,7},{12,8},{25,9},... | collective-permute-start | bytes 2433032 | tf_op jit(solution)/shard_map/ppermute | solution.py:168
  8.2 0.4 collective-permute-start.6
  8.7 7.3 %collective-permute-done.4.refs_0_.refs_1_ = bf16[528,768]{1,0:T(8,128)(2,1)S(1)} collective-permute-done((bf16[528,768]{1,0:T(8,128)(2,1)S(1)}, bf16[528,768]{1,0:T(8,128)(2,1)S(1)}, u32[]{:S(2)}, u32[]{:S(2)}) %collective-permute-start.4) | collective-permute-done | bytes 811040 | tf_op jit(solution)/shard_map/ppermute | solution.py:168
  16.0 0.5 collective-permute-start.5
  16.5 1.7 %collective-permute-done.2.refs_1_.refs_3_ = bf16[528,768]{1,0:T(8,128)(2,1)S(1)} collective-permute-done((bf16[528,768]{1,0:T(8,128)(2,1)S(1)}, bf16[528,768]{1,0:T(8,128)(2,1)S(1)}, u32[]{:S(2)}, u32[]{:S(2)}) %collective-permute-start.2) | collective-permute-done | bytes 811040 | tf_op jit(solution)/shard_map/ppermute | solution.py:168
  18.2 0.9 %collective-permute-start.3 = (bf16[528,768]{1,0:T(8,128)(2,1)S(1)}, bf16[528,768]{1,0:T(8,128)(2,1)S(1)}, u32[]{:S(2)}, u32[]{:S(2)}) collective-permute-start(bf16[528,768]{1,0:T(8,128)(2,1)S(1)} %collective-permute-done.2.refs_1_.refs_3_), channel_id=1, source_target_pairs={{24,0},{7,1},{26,2},{1,3},{28,4},{3,5},{30,6},{5,7},{0,8},{15,9},{... | collective-permute-start | bytes 2433032 | tf_op jit(solution)/shard_map/ppermute | solution.py:168
  19.1 1.4 %collective-permute-start.8 = (bf16[272,768]{1,0:T(8,128)(2,1)S(1)}, bf16[272,768]{1,0:T(8,128)(2,1)S(1)}, u32[]{:S(2)}, u32[]{:S(2)}) collective-permute-start(bf16[272,768]{1,0:T(8,128)(2,1)S(1)} %slice.36), channel_id=1, source_target_pairs={{32,0},{97,1},{34,2},{99,3},{36,4},{101,5},{38,6},{103,7},{40,8},{... | collective-permute-start | bytes 1253384 | tf_op jit(solution)/shard_map/ppermute | solution.py:168
  20.5 0.8 %score.9 = (f32[512,128]{1,0:T(8,128)S(1)}, f32[512,128]{1,0:T(8,128)S(1)}) custom-call(bf16[528,768]{1,0:T(8,128)(2,1)S(1)} %chip.1.refs_0_.refs_2_, bf16[528,768]{1,0:T(8,128)(2,1)S(1)} %collective-permute-done.2.refs_1_.refs_3_), custom_call_target="tpu_custom_call" | custom-call | flops 603979776 | bytes 1966080 | tf_op jit(solution)/shard_map/score/pallas_call | solution.py:137
  21.3 6.3 %collective-permute-done.6.refs_3_.refs_4_ = bf16[528,768]{1,0:T(8,128)(2,1)S(1)} collective-permute-done((bf16[528,768]{1,0:T(8,128)(2,1)S(1)}, bf16[528,768]{1,0:T(8,128)(2,1)S(1)}, u32[]{:S(2)}, u32[]{:S(2)}) %collective-permute-start.6) | collective-permute-done | bytes 811040 | tf_op jit(solution)/shard_map/ppermute | solution.py:168
  27.6 2.5 %collective-permute-start.10 = (bf16[528,768]{1,0:T(8,128)(2,1)S(1)}, bf16[528,768]{1,0:T(8,128)(2,1)S(1)}, u32[]{:S(2)}, u32[]{:S(2)}) collective-permute-start(bf16[528,768]{1,0:T(8,128)(2,1)S(1)} %collective-permute-done.6.refs_3_.refs_4_), channel_id=1, source_target_pairs={{24,0},{3,1},{26,2},{5,3},{28,4},{7,5},{30,6},{1,7},{0,8},{11,9},{... | collective-permute-start | bytes 2433032 | tf_op jit(solution)/shard_map/ppermute | solution.py:168
  30.1 1.1 %collective-permute-start.9 = (bf16[272,768]{1,0:T(8,128)(2,1)S(1)}, bf16[272,768]{1,0:T(8,128)(2,1)S(1)}, u32[]{:S(2)}, u32[]{:S(2)}) collective-permute-start(bf16[272,768]{1,0:T(8,128)(2,1)S(1)} %collective-permute-done.8.refs_0_.refs_3_), channel_id=1, source_target_pairs={{0,1},{1,0},{2,3},{3,2},{4,5},{5,4},{6,7},{7,6},{8,9},{9,8},{10,11... | collective-permute-start | bytes 1253384 | tf_op jit(solution)/shard_map/ppermute | solution.py:174
  31.2 1.5 %score.10 = (f32[1024,128]{1,0:T(8,128)S(1)}, f32[1024,128]{1,0:T(8,128)S(1)}) custom-call(bf16[528,768]{1,0:T(8,128)(2,1)S(1)} %collective-permute-done.4.refs_0_.refs_1_, bf16[528,768]{1,0:T(8,128)(2,1)S(1)} %collective-permute-done.5.refs_1_.refs_2_, bf16[528,768]{1,0:T(8,128)(2,1)S(1)} %chip.1.refs_0_.refs_2_, ...), custom_call_target="tpu_custom_call" | custom-call | flops 1207959552 | bytes 2752512 | tf_op jit(solution)/shard_map/score/pallas_call | solution.py:137
  32.7 1.5 %score.11 = (f32[512,128]{1,0:T(8,128)S(1)}, f32[1024,128]{1,0:T(8,128)S(1)}, f32[1,512]{1,0:T(1,128)S(1)}) custom-call(bf16[528,768]{1,0:T(8,128)(2,1)S(1)} %chip.1.refs_0_.refs_2_, bf16[528,768]{1,0:T(8,128)(2,1)S(1)} %collective-permute-done.4.refs_0_.refs_1_, bf16[528,768]{1,0:T(8,128)(2,1)S(1)} %collective-permute-done.5.refs_1_.refs_2_, ...), custom_call_target="tpu_custom_call" | custom-call | flops 1207959552 | bytes 3145728 | tf_op jit(solution)/shard_map/score/pallas_call | solution.py:137
  34.2 1.2 %collective-permute-start.7 = (bf16[272,768]{1,0:T(8,128)(2,1)S(1)}, bf16[272,768]{1,0:T(8,128)(2,1)S(1)}, u32[]{:S(2)}, u32[]{:S(2)}) collective-permute-start(bf16[272,768]{1,0:T(8,128)(2,1)S(1)} %slice.28), channel_id=1, source_target_pairs={{24,0},{7,1},{26,2},{1,3},{28,4},{3,5},{30,6},{5,7},{0,8},{15,9},{... | collective-permute-start | bytes 1253384 | tf_op jit(solution)/shard_map/ppermute | solution.py:168
  35.4 1.5 %score.12 = (f32[512,128]{1,0:T(8,128)S(1)}, f32[1024,128]{1,0:T(8,128)S(1)}, f32[1,512]{1,0:T(1,128)S(1)}) custom-call(bf16[528,768]{1,0:T(8,128)(2,1)S(1)} %chip.1.refs_0_.refs_2_, bf16[528,768]{1,0:T(8,128)(2,1)S(1)} %collective-permute-done.4.refs_0_.refs_1_, bf16[528,768]{1,0:T(8,128)(2,1)S(1)} %collective-permute-done.5.refs_1_.refs_2_, ...), custom_call_target="tpu_custom_call" | custom-call | flops 1207959552 | bytes 3145728 | tf_op jit(solution)/shard_map/score/pallas_call | solution.py:137
  36.8 1.7 %score.13 = (f32[512,128]{1,0:T(8,128)S(1)}, f32[512,128]{1,0:T(8,128)S(1)}, f32[1,1024]{1,0:T(1,128)S(1)}) custom-call(bf16[272,768]{1,0:T(8,128)(2,1)S(1)} %collective-permute-done.8.refs_0_.refs_3_, bf16[272,768]{1,0:T(8,128)(2,1)S(1)} %collective-permute-done.9.refs_1_.refs_4_, bf16[528,768]{1,0:T(8,128)(2,1)S(1)} %chip.1.refs_0_.refs_2_, ...), custom_call_target="tpu_custom_call" | custom-call | flops 1409286144 | bytes 3538944 | tf_op jit(solution)/shard_map/score/pallas_call | solution.py:137
  38.5 2.8 %collective-permute-start.11 = (f32[512]{0:T(512)S(1)}, f32[512]{0:T(512)S(1)}, u32[]{:S(2)}, u32[]{:S(2)}) collective-permute-start(f32[512]{0:T(512)S(1)} %bitcast.15), channel_id=1, source_target_pairs={{6,0},{25,1},{0,2},{27,3},{2,4},{29,5},{4,6},{31,7},{14,8},{1,9},{... | collective-permute-start | bytes 6152 | tf_op jit(solution)/shard_map/ppermute | solution.py:168
  41.3 2.2 %collective-permute-start.12 = (f32[512]{0:T(512)S(1)}, f32[512]{0:T(512)S(1)}, u32[]{:S(2)}, u32[]{:S(2)}) collective-permute-start(f32[512]{0:T(512)S(1)} %bitcast.14), channel_id=1, source_target_pairs={{12,0},{19,1},{14,2},{21,3},{8,4},{23,5},{10,6},{17,7},{20,8},{27,... | collective-permute-start | bytes 6152 | tf_op jit(solution)/shard_map/ppermute | solution.py:168
  43.5 1.9 %score.14 = (f32[512,128]{1,0:T(8,128)S(1)}, f32[1024,128]{1,0:T(8,128)S(1)}, f32[512,128]{1,0:T(8,128)S(1)}, f32[1,512]{1,0:T(1,128)S(1)}) custom-call(bf16[528,768]{1,0:T(8,128)(2,1)S(1)} %chip.1.refs_0_.refs_2_, bf16[528,768]{1,0:T(8,128)(2,1)S(1)} %collective-permute-done.4.refs_0_.refs_1_, bf16[528,768]{1,0:T(8,128)(2,1)S(1)} %collective-permute-done.5.refs_1_.refs_2_, ...), custom_call_target="tpu_custom_call" | custom-call | flops 1610612736 | bytes 3932160 | tf_op jit(solution)/shard_map/score/pallas_call | solution.py:137
  45.5 0.5 score.16
  46.0 1.5 %collective-permute-start.14 = (f32[512]{0:T(512)S(1)}, f32[512]{0:T(512)S(1)}, u32[]{:S(2)}, u32[]{:S(2)}) collective-permute-start(f32[512]{0:T(512)S(1)} %bitcast.10), channel_id=1, source_target_pairs={{64,0},{65,1},{66,2},{67,3},{68,4},{69,5},{70,6},{71,7},{72,8},{73... | collective-permute-start | bytes 6152 | tf_op jit(solution)/shard_map/ppermute | solution.py:168
  47.5 0.7 %score.17 = f32[1,1024]{1,0:T(1,128)S(1)} custom-call(bf16[528,768]{1,0:T(8,128)(2,1)S(1)} %collective-permute-done.4.refs_0_.refs_1_, bf16[528,768]{1,0:T(8,128)(2,1)S(1)} %collective-permute-done.5.refs_1_.refs_2_, bf16[272,768]{1,0:T(8,128)(2,1)S(1)} %collective-permute-done.7.refs_1_.refs_2_, f32[1024,128]{1,0:T(8,128)S(1)} %get-tuple-element.50.refs_3_, ...), custom_call_target="tpu_custom_call" | custom-call | flops 402653184 | bytes 1966080 | tf_op jit(solution)/shard_map/score/pallas_call | solution.py:137
  48.3 1.1 %collective-permute-start.15 = (f32[512]{0:T(512)S(1)}, f32[512]{0:T(512)S(1)}, u32[]{:S(2)}, u32[]{:S(2)}) collective-permute-start(f32[512]{0:T(512)S(1)} %bitcast.17), channel_id=1, source_target_pairs={{96,0},{33,1},{98,2},{35,3},{100,4},{37,5},{102,6},{39,7},{104,8},... | collective-permute-start | bytes 6152 | tf_op jit(solution)/shard_map/ppermute | solution.py:168
  49.8 0.5 score.15
  50.4 0.9 %collective-permute-done.13 = f32[512]{0:T(512)S(1)} collective-permute-done((f32[512]{0:T(512)S(1)}, f32[512]{0:T(512)S(1)}, u32[]{:S(2)}, u32[]{:S(2)}) %collective-permute-start.13) | collective-permute-done | bytes 2080 | tf_op jit(solution)/shard_map/ppermute | solution.py:168
  51.2 2.1 %collective-permute-done.16 = f32[512]{0:T(512)S(1)} collective-permute-done((f32[512]{0:T(512)S(1)}, f32[512]{0:T(512)S(1)}, u32[]{:S(2)}, u32[]{:S(2)}) %collective-permute-start.16) | collective-permute-done | bytes 2080 | tf_op jit(solution)/shard_map/ppermute | solution.py:168
  53.4 2.3 %collective-permute-start.17 = (f32[256]{0:T(256)S(1)}, f32[256]{0:T(256)S(1)}, u32[]{:S(2)}, u32[]{:S(2)}) collective-permute-start(f32[256]{0:T(256)S(1)} %slice.35), channel_id=1, source_target_pairs={{0,1},{1,0},{2,3},{3,2},{4,5},{5,4},{6,7},{7,6},{8,9},{9,8},{10,11... | collective-permute-start | bytes 3080 | tf_op jit(solution)/shard_map/ppermute | solution.py:174
  55.7 0.8 %collective-permute-done.17 = f32[256]{0:T(256)S(1)} collective-permute-done((f32[256]{0:T(256)S(1)}, f32[256]{0:T(256)S(1)}, u32[]{:S(2)}, u32[]{:S(2)}) %collective-permute-start.17) | collective-permute-done | bytes 1056 | tf_op jit(solution)/shard_map/ppermute | solution.py:174
  56.5 0.6 slice_maximum_fusion.2
  (26 shorter events, 1.3 us)
Async XLA Ops:
  0.0 1.4 %copy-start.1 = (s32[256]{0:T(256)S(1)}, s32[256]{0:T(256)}, u32[]{:S(2)}) copy-start(s32[256]{0:T(256)} %param.3) | copy-start | bytes 3076
  0.0 3.0 %collective-permute-start = (bf16[256,768]{1,0:T(8,128)(2,1)}, bf16[256,768]{1,0:T(8,128)(2,1)S(1)}, u32[]{:S(2)}, u32[]{:S(2)}) collective-permute-start(bf16[256,768]{1,0:T(8,128)(2,1)} %rows_ref.1), channel_id=1, source_target_pairs={{0,1},{1,0},{2,3},{3,2},{4,5},{5,4},{6,7},{7,6},{8,9},{9,8},{10,11... | collective-permute-start | bytes 1179656 | tf_op jit(solution)/shard_map/ppermute | solution.py:174
  1.4 1.6 %collective-permute-start.1 = (s32[256]{0:T(256)}, s32[256]{0:T(256)S(1)}, u32[]{:S(2)}, u32[]{:S(2)}) collective-permute-start(s32[256]{0:T(256)} %param.3), channel_id=1, source_target_pairs={{0,1},{1,0},{2,3},{3,2},{4,5},{5,4},{6,7},{7,6},{8,9},{9,8},{10,11... | collective-permute-start | bytes 3080 | tf_op jit(solution)/shard_map/ppermute | solution.py:174
  1.4 1.0 %copy-start = (bf16[256,768]{1,0:T(8,128)(2,1)S(1)}, bf16[256,768]{1,0:T(8,128)(2,1)}, u32[]{:S(2)}) copy-start(bf16[256,768]{1,0:T(8,128)(2,1)} %rows_ref.1) | copy-start | bytes 1179652
  3.2 12.8 %collective-permute-start.4 = (bf16[528,768]{1,0:T(8,128)(2,1)S(1)}, bf16[528,768]{1,0:T(8,128)(2,1)S(1)}, u32[]{:S(2)}, u32[]{:S(2)}) collective-permute-start(bf16[528,768]{1,0:T(8,128)(2,1)S(1)} %chip.1.refs_0_.refs_2_), channel_id=1, source_target_pairs={{32,0},{97,1},{34,2},{99,3},{36,4},{101,5},{38,6},{103,7},{40,8},{... | collective-permute-start | bytes 2433032 | tf_op jit(solution)/shard_map/ppermute | solution.py:168
  4.6 13.5 %collective-permute-start.2 = (bf16[528,768]{1,0:T(8,128)(2,1)S(1)}, bf16[528,768]{1,0:T(8,128)(2,1)S(1)}, u32[]{:S(2)}, u32[]{:S(2)}) collective-permute-start(bf16[528,768]{1,0:T(8,128)(2,1)S(1)} %chip.1.refs_0_.refs_2_), channel_id=1, source_target_pairs={{4,0},{17,1},{6,2},{19,3},{0,4},{21,5},{2,6},{23,7},{12,8},{25,9},... | collective-permute-start | bytes 2433032 | tf_op jit(solution)/shard_map/ppermute | solution.py:168
  8.2 19.4 %collective-permute-start.6 = (bf16[528,768]{1,0:T(8,128)(2,1)S(1)}, bf16[528,768]{1,0:T(8,128)(2,1)S(1)}, u32[]{:S(2)}, u32[]{:S(2)}) collective-permute-start(bf16[528,768]{1,0:T(8,128)(2,1)S(1)} %chip.1.refs_0_.refs_2_), channel_id=1, source_target_pairs={{2,0},{9,1},{4,2},{11,3},{6,4},{13,5},{0,6},{15,7},{10,8},{17,9},{... | collective-permute-start | bytes 2433032 | tf_op jit(solution)/shard_map/ppermute | solution.py:168
  16.0 15.2 %collective-permute-start.5 = (bf16[528,768]{1,0:T(8,128)(2,1)S(1)}, bf16[528,768]{1,0:T(8,128)(2,1)S(1)}, u32[]{:S(2)}, u32[]{:S(2)}) collective-permute-start(bf16[528,768]{1,0:T(8,128)(2,1)S(1)} %collective-permute-done.4.refs_0_.refs_1_), channel_id=1, source_target_pairs={{0,1},{1,0},{2,3},{3,2},{4,5},{5,4},{6,7},{7,6},{8,9},{9,8},{10,11... | collective-permute-start | bytes 2433032 | tf_op jit(solution)/shard_map/ppermute | solution.py:174
  18.2 16.0 %collective-permute-start.3 = (bf16[528,768]{1,0:T(8,128)(2,1)S(1)}, bf16[528,768]{1,0:T(8,128)(2,1)S(1)}, u32[]{:S(2)}, u32[]{:S(2)}) collective-permute-start(bf16[528,768]{1,0:T(8,128)(2,1)S(1)} %collective-permute-done.2.refs_1_.refs_3_), channel_id=1, source_target_pairs={{24,0},{7,1},{26,2},{1,3},{28,4},{3,5},{30,6},{5,7},{0,8},{15,9},{... | collective-permute-start | bytes 2433032 | tf_op jit(solution)/shard_map/ppermute | solution.py:168
  19.1 11.0 %collective-permute-start.8 = (bf16[272,768]{1,0:T(8,128)(2,1)S(1)}, bf16[272,768]{1,0:T(8,128)(2,1)S(1)}, u32[]{:S(2)}, u32[]{:S(2)}) collective-permute-start(bf16[272,768]{1,0:T(8,128)(2,1)S(1)} %slice.36), channel_id=1, source_target_pairs={{32,0},{97,1},{34,2},{99,3},{36,4},{101,5},{38,6},{103,7},{40,8},{... | collective-permute-start | bytes 1253384 | tf_op jit(solution)/shard_map/ppermute | solution.py:168
  27.6 15.9 %collective-permute-start.10 = (bf16[528,768]{1,0:T(8,128)(2,1)S(1)}, bf16[528,768]{1,0:T(8,128)(2,1)S(1)}, u32[]{:S(2)}, u32[]{:S(2)}) collective-permute-start(bf16[528,768]{1,0:T(8,128)(2,1)S(1)} %collective-permute-done.6.refs_3_.refs_4_), channel_id=1, source_target_pairs={{24,0},{3,1},{26,2},{5,3},{28,4},{7,5},{30,6},{1,7},{0,8},{11,9},{... | collective-permute-start | bytes 2433032 | tf_op jit(solution)/shard_map/ppermute | solution.py:168
  30.1 6.7 %collective-permute-start.9 = (bf16[272,768]{1,0:T(8,128)(2,1)S(1)}, bf16[272,768]{1,0:T(8,128)(2,1)S(1)}, u32[]{:S(2)}, u32[]{:S(2)}) collective-permute-start(bf16[272,768]{1,0:T(8,128)(2,1)S(1)} %collective-permute-done.8.refs_0_.refs_3_), channel_id=1, source_target_pairs={{0,1},{1,0},{2,3},{3,2},{4,5},{5,4},{6,7},{7,6},{8,9},{9,8},{10,11... | collective-permute-start | bytes 1253384 | tf_op jit(solution)/shard_map/ppermute | solution.py:174
  34.2 11.3 %collective-permute-start.7 = (bf16[272,768]{1,0:T(8,128)(2,1)S(1)}, bf16[272,768]{1,0:T(8,128)(2,1)S(1)}, u32[]{:S(2)}, u32[]{:S(2)}) collective-permute-start(bf16[272,768]{1,0:T(8,128)(2,1)S(1)} %slice.28), channel_id=1, source_target_pairs={{24,0},{7,1},{26,2},{1,3},{28,4},{3,5},{30,6},{5,7},{0,8},{15,9},{... | collective-permute-start | bytes 1253384 | tf_op jit(solution)/shard_map/ppermute | solution.py:168
  38.5 10.9 %collective-permute-start.11 = (f32[512]{0:T(512)S(1)}, f32[512]{0:T(512)S(1)}, u32[]{:S(2)}, u32[]{:S(2)}) collective-permute-start(f32[512]{0:T(512)S(1)} %bitcast.15), channel_id=1, source_target_pairs={{6,0},{25,1},{0,2},{27,3},{2,4},{29,5},{4,6},{31,7},{14,8},{1,9},{... | collective-permute-start | bytes 6152 | tf_op jit(solution)/shard_map/ppermute | solution.py:168
  41.3 9.0 %collective-permute-start.12 = (f32[512]{0:T(512)S(1)}, f32[512]{0:T(512)S(1)}, u32[]{:S(2)}, u32[]{:S(2)}) collective-permute-start(f32[512]{0:T(512)S(1)} %bitcast.14), channel_id=1, source_target_pairs={{12,0},{19,1},{14,2},{21,3},{8,4},{23,5},{10,6},{17,7},{20,8},{27,... | collective-permute-start | bytes 6152 | tf_op jit(solution)/shard_map/ppermute | solution.py:168
  45.4 5.8 %collective-permute-start.13 = (f32[512]{0:T(512)S(1)}, f32[512]{0:T(512)S(1)}, u32[]{:S(2)}, u32[]{:S(2)}) collective-permute-start(f32[512]{0:T(512)S(1)} %bitcast.13), channel_id=1, source_target_pairs={{14,0},{31,1},{8,2},{25,3},{10,4},{27,5},{12,6},{29,7},{22,8},{7,9... | collective-permute-start | bytes 6152 | tf_op jit(solution)/shard_map/ppermute | solution.py:168
  46.0 5.2 %collective-permute-start.14 = (f32[512]{0:T(512)S(1)}, f32[512]{0:T(512)S(1)}, u32[]{:S(2)}, u32[]{:S(2)}) collective-permute-start(f32[512]{0:T(512)S(1)} %bitcast.10), channel_id=1, source_target_pairs={{64,0},{65,1},{66,2},{67,3},{68,4},{69,5},{70,6},{71,7},{72,8},{73... | collective-permute-start | bytes 6152 | tf_op jit(solution)/shard_map/ppermute | solution.py:168
  48.3 3.0 %collective-permute-start.15 = (f32[512]{0:T(512)S(1)}, f32[512]{0:T(512)S(1)}, u32[]{:S(2)}, u32[]{:S(2)}) collective-permute-start(f32[512]{0:T(512)S(1)} %bitcast.17), channel_id=1, source_target_pairs={{96,0},{33,1},{98,2},{35,3},{100,4},{37,5},{102,6},{39,7},{104,8},... | collective-permute-start | bytes 6152 | tf_op jit(solution)/shard_map/ppermute | solution.py:168
  49.4 3.9 %collective-permute-start.16 = (f32[512]{0:T(512)S(1)}, f32[512]{0:T(512)S(1)}, u32[]{:S(2)}, u32[]{:S(2)}) collective-permute-start(f32[512]{0:T(512)S(1)} %bitcast.16), channel_id=1, source_target_pairs={{32,0},{97,1},{34,2},{99,3},{36,4},{101,5},{38,6},{103,7},{40,8},{... | collective-permute-start | bytes 6152 | tf_op jit(solution)/shard_map/ppermute | solution.py:168
  53.4 3.2 %collective-permute-start.17 = (f32[256]{0:T(256)S(1)}, f32[256]{0:T(256)S(1)}, u32[]{:S(2)}, u32[]{:S(2)}) collective-permute-start(f32[256]{0:T(256)S(1)} %slice.35), channel_id=1, source_target_pairs={{0,1},{1,0},{2,3},{3,2},{4,5},{5,4},{6,7},{7,6},{8,9},{9,8},{10,11... | collective-permute-start | bytes 3080 | tf_op jit(solution)/shard_map/ppermute | solution.py:174
